TPU v7x, 32 devices: a whole 2x2x4 slice. The times are simulated.
32 devices in a mesh: seqa: 8 (over y, x, core), seqb: 4 (over z).
Axes of the slice: x: 2, y: 2, z: 4, core: 2. Of those that a mesh axis runs over, the one named last changes fastest.
Arguments:
- hidden_in: bfloat16 [4096, 2880], P(('seqa', 'seqb')), may hold values from -6 to 6
- queries: bfloat16 [4096, 4096], P(('seqa', 'seqb')), may hold values from -200 to 200
- grad_out: bfloat16 [4096, 4096], P(('seqa', 'seqb')), may hold values from -5 to 5
- key_weight: bfloat16 [2880, 512], P(None, ('seqa', 'seqb')), may hold values from -0.109375 to 0.109375
- value_weight: bfloat16 [2880, 512], P(None, ('seqa', 'seqb')), may hold values from -0.109375 to 0.109375
Outputs:
- grad_queries: bfloat16 [4096, 4096], P(('seqa', 'seqb'))
- grad_keys: bfloat16 [4096, 512], P(('seqa', 'seqb'))
- grad_values: bfloat16 [4096, 512], P(('seqa', 'seqb'))
- grad_inputs: bfloat16 [4096, 2880], P(('seqa', 'seqb'))
- grad_key_weight: float32 [2880, 512], P(None, ('seqa', 'seqb'))
- grad_value_weight: float32 [2880, 512], P(None, ('seqa', 'seqb'))
All inputs are finite; a program needn't handle non-finite values.
Results may differ from a plain program's by a relative error of at most 0.011.
Values may be sent and summed in bfloat16 or wider, within the bound.
No kernel may reach another device: no remote copies, remote signals or barrier semaphores. Data moves between devices by JAX's collectives and lax.ppermute only.
A program may use at most 128 MiB of HBM per device.

v0:
```python
import jax
import jax.numpy as jnp
from jax import lax
from jax.sharding import PartitionSpec as P

KV_HEADS = 8
HEAD = 64
WIN = 128


def passed_along(array, axis, by):
    size = lax.axis_size(axis)
    pairs = [(i, i + by) for i in range(size) if 0 <= i + by < size]
    return lax.ppermute(array, axis, pairs)


def head_group(query_rows, grad_rows, key_rows, value_rows, allowed):
    count = query_rows.shape[0]
    width = key_rows.shape[1]
    group = query_rows.shape[1] // width
    factor = width ** (-0.5)
    query_heads = query_rows.reshape(count, group, width)
    grad_heads = grad_rows.reshape(count, group, width)
    scores = (
        jnp.einsum("tgh,lh->gtl", query_heads, key_rows, preferred_element_type=jnp.float32)
        * factor
    )
    masked = jnp.where(allowed[None], scores, -1e30)
    peak = jnp.max(masked, axis=2, keepdims=True)
    weights = jnp.where(allowed[None], jnp.exp(masked - peak), 0.0)
    weights = weights / jnp.sum(weights, axis=2, keepdims=True)
    weights_low = weights.astype(jnp.bfloat16)
    attended = jnp.einsum(
        "gtl,lh->tgh", weights_low, value_rows, preferred_element_type=jnp.float32
    ).astype(jnp.bfloat16)
    delta = jnp.sum(grad_heads.astype(jnp.float32) * attended.astype(jnp.float32), axis=2)
    grad_weights = jnp.einsum(
        "tgh,lh->gtl", grad_heads, value_rows, preferred_element_type=jnp.float32
    )
    grad_scores = (weights * (grad_weights - jnp.transpose(delta)[:, :, None])).astype(jnp.bfloat16)
    grad_query = (
        jnp.einsum("gtl,lh->tgh", grad_scores, key_rows, preferred_element_type=jnp.float32)
        * factor
    )
    grad_key = (
        jnp.einsum("gtl,tgh->lh", grad_scores, query_heads, preferred_element_type=jnp.float32)
        * factor
    )
    grad_value = jnp.einsum(
        "gtl,tgh->lh", weights_low, grad_heads, preferred_element_type=jnp.float32
    )
    return (grad_query.reshape(count, group * width).astype(jnp.bfloat16), grad_key, grad_value)


def shards(hidden_in, queries, grad_out, key_weight, value_weight):
    inner_cols = (
        lax.all_gather(key_weight, "seqb", axis=1, tiled=True),
        lax.all_gather(value_weight, "seqb", axis=1, tiled=True),
    )
    key_full, value_full = (
        lax.all_gather(inner_cols[0], "seqa", axis=1, tiled=True),
        lax.all_gather(inner_cols[1], "seqa", axis=1, tiled=True),
    )
    row_count = hidden_in.shape[0]
    span = row_count + WIN
    keys_own = jnp.dot(hidden_in, key_full, preferred_element_type=jnp.float32).astype(jnp.bfloat16)
    values_own = jnp.dot(hidden_in, value_full, preferred_element_type=jnp.float32).astype(
        jnp.bfloat16
    )
    prior_keys, prior_values = passed_along((keys_own, values_own), ("seqa", "seqb"), 1)
    key_rows = jnp.concatenate([prior_keys, keys_own], axis=0)
    value_rows = jnp.concatenate([prior_values, values_own], axis=0)
    device_index = lax.axis_index(("seqa", "seqb"))
    first_row = device_index * row_count
    query_pos = first_row + jnp.arange(row_count, dtype=jnp.int32)
    key_pos = first_row - WIN + jnp.arange(span, dtype=jnp.int32)
    gap_grid = query_pos[:, None] - key_pos[None, :]
    allowed = (gap_grid >= 0) & (gap_grid <= WIN) & (key_pos[None, :] >= 0)
    query_groups = jnp.moveaxis(queries.reshape(row_count, KV_HEADS, -1), 1, 0)
    grad_groups = jnp.moveaxis(grad_out.reshape(row_count, KV_HEADS, -1), 1, 0)
    key_groups = jnp.moveaxis(key_rows.reshape(span, KV_HEADS, HEAD), 1, 0)
    value_groups = jnp.moveaxis(value_rows.reshape(span, KV_HEADS, HEAD), 1, 0)
    grad_query, grad_key, grad_value = lax.map(
        lambda items: head_group(items[0], items[1], items[2], items[3], allowed),
        (query_groups, grad_groups, key_groups, value_groups),
    )
    grad_queries = jnp.moveaxis(grad_query, 0, 1).reshape(row_count, -1)
    key_sums = jnp.moveaxis(grad_key, 0, 1).reshape(span, -1)
    value_sums = jnp.moveaxis(grad_value, 0, 1).reshape(span, -1)
    later_keys, later_values = passed_along(
        (key_sums[:WIN], value_sums[:WIN]), ("seqa", "seqb"), -1
    )
    key_local = key_sums[WIN:]
    value_local = value_sums[WIN:]
    grad_keys = jnp.concatenate(
        [key_local[: row_count - WIN], key_local + later_keys], axis=0
    ).astype(jnp.bfloat16)
    grad_values = jnp.concatenate(
        [value_local[: row_count - WIN], value_local + later_values], axis=0
    ).astype(jnp.bfloat16)
    contract_cols = (((1,), (1,)), ((), ()))
    grad_inputs = (
        lax.dot_general(grad_keys, key_full, contract_cols, preferred_element_type=jnp.float32)
        + lax.dot_general(
            grad_values, value_full, contract_cols, preferred_element_type=jnp.float32
        )
    ).astype(jnp.bfloat16)
    contract_rows = (((0,), (0,)), ((), ()))
    key_term = lax.dot_general(
        hidden_in, grad_keys, contract_rows, preferred_element_type=jnp.float32
    )
    value_term = lax.dot_general(
        hidden_in, grad_values, contract_rows, preferred_element_type=jnp.float32
    )
    outer_sums = (
        lax.psum_scatter(key_term, "seqa", scatter_dimension=1, tiled=True),
        lax.psum_scatter(value_term, "seqa", scatter_dimension=1, tiled=True),
    )
    key_total, value_total = (
        lax.psum_scatter(outer_sums[0], "seqb", scatter_dimension=1, tiled=True),
        lax.psum_scatter(outer_sums[1], "seqb", scatter_dimension=1, tiled=True),
    )
    grad_scale = (row_count * lax.axis_size(("seqa", "seqb"))) ** (-0.5)
    return (
        grad_queries,
        grad_keys,
        grad_values,
        grad_inputs,
        key_total * grad_scale,
        value_total * grad_scale,
    )


def solution(mesh):
    in_specs = (
        P(("seqa", "seqb"), None),
        P(("seqa", "seqb"), None),
        P(("seqa", "seqb"), None),
        P(None, ("seqa", "seqb")),
        P(None, ("seqa", "seqb")),
    )
    out_specs = (
        P(("seqa", "seqb"), None),
        P(("seqa", "seqb"), None),
        P(("seqa", "seqb"), None),
        P(("seqa", "seqb"), None),
        P(None, ("seqa", "seqb")),
        P(None, ("seqa", "seqb")),
    )
    return jax.shard_map(shards, mesh=mesh, in_specs=in_specs, out_specs=out_specs, check_vma=False)
```

profile of v0, /device:TPU:0, one launch (start us, length us, event | category | flops | bytes accessed | tf_op | source)
XLA Modules:
  0.0 377.8 jit_solution(13307501852548184914)
XLA Ops:
  7.2 18.2 %all_gather.12 = bf16[2880,64]{0,1:T(8,128)(2,1)} all-gather(bf16[2880,16]{0,1:T(8,128)(2,1)} %param.10), channel_id=1, replica_groups=mesh['seqa'=8,'seqb'=4] {'seqb'}, dimensions={1}, use_global_device_ids=true | all-gather | bytes 460800 | tf_op jit(solution)/shard_map/all_gather | solution.py:57
  25.5 15.7 %all_gather.14 = bf16[2880,64]{0,1:T(8,128)(2,1)} all-gather(bf16[2880,16]{0,1:T(8,128)(2,1)} %param.11), channel_id=1, replica_groups=mesh['seqa'=8,'seqb'=4] {'seqb'}, dimensions={1}, use_global_device_ids=true | all-gather | bytes 460800 | tf_op jit(solution)/shard_map/all_gather | solution.py:58
  41.3 16.0 %all-gather.3.cloned.1.call-done = bf16[2880,512]{0,1:T(8,128)(2,1)} async-done(((bf16[2880,64]{0,1:T(8,128)(2,1)}), bf16[2880,512]{0,1:T(8,128)(2,1)}) %all-gather.3.cloned.1.call-update) | async-done | bytes 2949136 | tf_op jit(solution)/shard_map/all_gather | solution.py:61
  57.3 3.0 convolution_convert_fusion.2
  60.3 3.4 collective-permute-start
  63.7 27.3 %all-gather.5.cloned.1.call-done = bf16[2880,512]{0,1:T(8,128)(2,1)} async-done(((bf16[2880,64]{0,1:T(8,128)(2,1)}), bf16[2880,512]{0,1:T(8,128)(2,1)}) %all-gather.5.cloned.1.call-update) | async-done | bytes 2949136 | tf_op jit(solution)/shard_map/all_gather | solution.py:62
  91.0 3.6 convolution_convert_fusion.1
  94.6 4.0 %collective-permute-start.1 = (bf16[128,512]{1,0:T(8,128)(2,1)}, bf16[128,512]{1,0:T(8,128)(2,1)}, u32[]{:S(2)}, u32[]{:S(2)}) collective-permute-start(bf16[128,512]{1,0:T(8,128)(2,1)} %convolution_convert_fusion.1), channel_id=1, source_target_pairs={{0,1},{1,2},{2,3},{3,4},{4,5},{5,6},{6,7},{7,8},{8,9},{9,10},{10,1... | collective-permute-start | bytes 393224 | tf_op jit(solution)/shard_map/ppermute | solution.py:14
  99.3 1.6 copy.46
  103.3 64.0 %while.15 = (s32[]{:T(128)}, bf16[8,128,512]{1,2,0:T(8,128)(2,1)}, f32[8,256,64]{1,2,0:T(8,128)}, f32[8,256,64]{1,2,0:T(8,128)}, bf16[8,256,64]{1,2,0:T(8,128)(2...) while((s32[]{:T(128)}, bf16[8,128,512]{1,2,0:T(8,128)(2,1)}, ...), condition=%wide.region_4.5_spmd.clone, body=%wide.region_0.4_spmd.clone.sunk | while | flops 274581248 | bytes 6090645 | solution.py:83
  169.7 8.8 %collective-permute-done.2 = f32[128,512]{0,1:T(8,128)S(1)} collective-permute-done((f32[128,512]{0,1:T(8,128)S(1)}, f32[128,512]{0,1:T(8,128)S(1)}, u32[]{:S(2)}, u32[]{:S(2)}) %collective-permute-start.2) | collective-permute-done | bytes 262176 | tf_op jit(solution)/shard_map/ppermute | solution.py:14
  178.5 3.5 convolution_bitcast_fusion.4
  182.0 6.4 %copy.57 = f32[2880,512]{0,1:T(8,128)} copy(f32[2880,512]{1,0:T(8,128)} %convolution_bitcast_fusion.4) | data formatting | bytes 11796480
  190.8 9.5 %collective-permute-done.3 = f32[128,512]{0,1:T(8,128)S(1)} collective-permute-done((f32[128,512]{0,1:T(8,128)S(1)}, f32[128,512]{0,1:T(8,128)S(1)}, u32[]{:S(2)}, u32[]{:S(2)}) %collective-permute-start.3) | collective-permute-done | bytes 262176 | tf_op jit(solution)/shard_map/ppermute | solution.py:14
  200.4 3.8 %convolution_bitcast_fusion.3 = f32[2880,512]{1,0:T(8,128)} fusion(bf16[128,512]{0,1:T(8,128)(2,1)S(1)} %fusion.57, bf16[128,2880]{0,1:T(8,128)(2,1)S(1)} %copy-done), kind=kOutput, calls=%fused_computation.52 | convolution fusion | flops 377487360 | bytes 6766592 | tf_op jit(solution)/shard_map/dot_general | solution.py:112
  204.2 6.6 %copy.61 = f32[2880,512]{0,1:T(8,128)} copy(f32[2880,512]{1,0:T(8,128)} %convolution_bitcast_fusion.3) | data formatting | bytes 11796480
  210.9 41.4 %reduce-scatter.13.cloned.1.call-done = f32[64,2880]{1,0:T(8,128)} async-done(((f32[512,2880]{1,0:T(8,128)}), f32[64,2880]{1,0:T(8,128)}) %reduce-scatter.13.cloned.1.call-update) | async-done | bytes 737296
  252.6 63.8 %reduce-scatter.17.cloned.1.call-done = f32[64,2880]{1,0:T(8,128)} async-done(((f32[512,2880]{1,0:T(8,128)}), f32[64,2880]{1,0:T(8,128)}) %reduce-scatter.17.cloned.1.call-update) | async-done | bytes 737296
  319.3 3.3 fusion.64
  322.6 2.2 fusion.56
  324.8 16.7 %reduce-scatter.15.cloned.1.call-done = f32[16,2880]{1,0:T(8,128)} async-done(((f32[64,2880]{1,0:T(8,128)}), f32[16,2880]{1,0:T(8,128)}) %reduce-scatter.15.cloned.1.call-update) | async-done | bytes 184336
  344.1 2.5 copy.50
  346.6 19.2 %reduce-scatter.19.cloned.1.call-done = f32[16,2880]{1,0:T(8,128)} async-done(((f32[64,2880]{1,0:T(8,128)}), f32[16,2880]{1,0:T(8,128)}) %reduce-scatter.19.cloned.1.call-update) | async-done | bytes 184336
  368.4 2.5 copy.51
  (120 shorter events, 80.0 us)
Async XLA Ops:
  7.2 50.1 %copy-start = (bf16[128,2880]{0,1:T(8,128)(2,1)S(1)}, bf16[128,2880]{0,1:T(8,128)(2,1)}, u32[]{:S(2)}) copy-start(bf16[128,2880]{0,1:T(8,128)(2,1)} %param.7) | copy-start | bytes 2211844
  7.2 50.1 %all-gather.3.cloned.1.call-start = ((), (), s32[]{:S(2)}) async-start(), calls=%async_computation.4 | async-start | bytes 3391488 | tf_op jit(solution)/shard_map/all_gather | solution.py:61
  25.4 65.6 %all-gather.5.cloned.1.call-start = ((), (), s32[]{:S(2)}) async-start(), calls=%async_computation.5 | async-start | bytes 3391488 | tf_op jit(solution)/shard_map/all_gather | solution.py:62
  41.2 211.1 %reduce-scatter.13.cloned.1.call-start = ((), (), s32[]{:S(2)}) async-start(), calls=%async_computation.6 | async-start | bytes 6782976
  41.3 57.4 %copy-start.2 = (bf16[128,4096]{1,0:T(8,128)(2,1)S(1)}, bf16[128,4096]{1,0:T(8,128)(2,1)}, u32[]{:S(2)}) copy-start(bf16[128,4096]{1,0:T(8,128)(2,1)} %param.8) | copy-start | bytes 3145732
  60.3 40.7 %collective-permute-start = (bf16[128,512]{1,0:T(8,128)(2,1)S(1)}, bf16[128,512]{1,0:T(8,128)(2,1)S(1)}, u32[]{:S(2)}, u32[]{:S(2)}) collective-permute-start(bf16[128,512]{1,0:T(8,128)(2,1)S(1)} %convolution_convert_fusion.2), channel_id=1, source_target_pairs={{0,1},{1,2},{2,3},{3,4},{4,5},{5,6},{6,7},{7,8},{8,9},{9,10},{10,1... | collective-permute-start | bytes 393224 | tf_op jit(solution)/shard_map/ppermute | solution.py:14
  94.6 6.9 %collective-permute-start.1 = (bf16[128,512]{1,0:T(8,128)(2,1)}, bf16[128,512]{1,0:T(8,128)(2,1)}, u32[]{:S(2)}, u32[]{:S(2)}) collective-permute-start(bf16[128,512]{1,0:T(8,128)(2,1)} %convolution_convert_fusion.1), channel_id=1, source_target_pairs={{0,1},{1,2},{2,3},{3,4},{4,5},{5,6},{6,7},{7,8},{8,9},{9,10},{10,1... | collective-permute-start | bytes 393224 | tf_op jit(solution)/shard_map/ppermute | solution.py:14
  168.4 10.1 %collective-permute-start.2 = (f32[128,512]{0,1:T(8,128)S(1)}, f32[128,512]{0,1:T(8,128)S(1)}, u32[]{:S(2)}, u32[]{:S(2)}) collective-permute-start(f32[128,512]{0,1:T(8,128)S(1)} %bitcast.212), channel_id=1, source_target_pairs={{1,0},{2,1},{3,2},{4,3},{5,4},{6,5},{7,6},{8,7},{9,8},{10,9},{11,1... | collective-permute-start | bytes 786440 | tf_op jit(solution)/shard_map/ppermute | solution.py:14
  188.4 1.0 copy-start.4
  188.5 127.9 %reduce-scatter.17.cloned.1.call-start = ((), (), s32[]{:S(2)}) async-start(), calls=%async_computation.8 | async-start | bytes 6782976
  189.5 10.8 %collective-permute-start.3 = (f32[128,512]{0,1:T(8,128)S(1)}, f32[128,512]{0,1:T(8,128)S(1)}, u32[]{:S(2)}, u32[]{:S(2)}) collective-permute-start(f32[128,512]{0,1:T(8,128)S(1)} %bitcast.213), channel_id=1, source_target_pairs={{1,0},{2,1},{3,2},{4,3},{5,4},{6,5},{7,6},{8,7},{9,8},{10,9},{11,1... | collective-permute-start | bytes 786440 | tf_op jit(solution)/shard_map/ppermute | solution.py:14
  210.9 105.6 %copy-start.3 = (bf16[8,128,512]{1,2,0:T(8,128)(2,1)S(1)}, bf16[8,128,512]{1,2,0:T(8,128)(2,1)}, u32[]{:S(2)}) copy-start(bf16[8,128,512]{1,2,0:T(8,128)(2,1)} %get-tuple-element.55) | copy-start | bytes 3145732
  210.9 130.6 %reduce-scatter.15.cloned.1.call-start = ((), (), s32[]{:S(2)}) async-start(), calls=%async_computation.7 | async-start | bytes 942080
  252.3 113.5 %reduce-scatter.19.cloned.1.call-start = ((), (), s32[]{:S(2)}) async-start(), calls=%async_computation.9 | async-start | bytes 942080
  319.3 3.3 copy-start.1
Sparse Core Ops, SparseCore 0:
  25.6 31.7 all-gather.2
  59.2 31.7 all-gather.4
  188.6 63.6 reduce-scatter.12
  256.1 60.2 reduce-scatter.16
  318.5 22.9 reduce-scatter.14
  343.7 22.0 reduce-scatter.18
where the time goes:
time: 379 us; the launch traced here: 378 us
  waiting for transfers between devices  203 us (54%)
  matrix products  76.5 us (20%)
  local copies, waits for them, and re-layouts  34.5 us (9%)
  blocking collectives  33.9 us (9%)
  between operations  14.3 us (4%)
  starting transfers between devices  10.4 us (3%)
  other arithmetic  4.59 us (1%)
    unnamed x10, waiting for transfers between devices  141 us
    all_gather x1, waiting for transfers between devices, shards(): lax.all_gather(inner_cols[1], 'seqa', axis=1, tiled=True)  27.3 us
    unnamed x20, local copies, waits for them, and re-layouts  25.6 us
    ppermute x4, waiting for transfers between devices, passed_along(): return lax.ppermute(array, axis, pairs)  18.7 us
    all_gather x1, blocking collectives, shards(): lax.all_gather(key_weight, 'seqb', axis=1, tiled=True)  18.2 us
    all_gather x1, waiting for transfers between devices, shards(): lax.all_gather(inner_cols[0], 'seqa', axis=1, tiled=True)  16 us
    all_gather x1, blocking collectives, shards(): lax.all_gather(value_weight, 'seqb', axis=1, tiled=True)  15.7 us
    dot_general x8, matrix products, head_group(): jnp.einsum('tgh,lh->gtl', grad_heads, value_rows, preferred_element_type=...  12.7 us
  transfers between devices with their start and end apart: 10, of which 9 were waited for; matrix products, arithmetic and copies ran while one was open for 9% of the time, Pallas kernels for 0%

commit v1 on v0

v1 whole, which is shorter than its diff:
```python
import functools
import math

import jax
import jax.numpy as jnp
from jax import lax
from jax.experimental import pallas as pl
from jax.experimental.pallas import tpu as pltpu
from jax.sharding import Mesh, PartitionSpec as P

KV_HEADS = 8
HEAD = 64
WIN = 128
LANES = 128
QUARTERS = 4
SUBLANES = 16

F32 = jnp.float32
BF16 = jnp.bfloat16
NT = (((1,), (1,)), ((), ()))
AXES = ("hi", "x", "c", "z")


def params(megabytes=48):
    return pltpu.CompilerParams(vmem_limit_bytes=megabytes * 1024 * 1024)


def cost(flops, *arrays):
    size = sum(math.prod(a.shape) * a.dtype.itemsize for a in arrays)
    return pl.CostEstimate(flops=int(flops), bytes_accessed=int(size), transcendentals=0)


def struct(shape, dtype):
    return jax.ShapeDtypeStruct(shape, dtype)


VMEM = pl.BlockSpec(memory_space=pltpu.VMEM)
SMEM = pl.BlockSpec(memory_space=pltpu.SMEM)


def padded_pair(block, half):
    lane = lax.broadcasted_iota(jnp.int32, block.shape, 1)
    here = jnp.where(lane // HEAD == half, block.astype(F32), 0.0)
    there = pltpu.roll(here, HEAD, 1)
    even, odd = jnp.where(half == 0, here, there), jnp.where(half == 0, there, here)
    return even.astype(BF16), odd.astype(BF16)


def stacked(own, halo, half):
    own_even, own_odd = padded_pair(own, half)
    halo_even, halo_odd = padded_pair(halo, half)
    return jnp.concatenate([own_even, halo_even, own_odd, halo_odd], axis=0)


def folded(total):
    rows = total.shape[0] // 4
    lane = lax.broadcasted_iota(jnp.int32, (rows, LANES), 1)
    out = []
    for part in range(2):
        even = total[part * rows : (part + 1) * rows]
        odd = total[(2 + part) * rows : (3 + part) * rows]
        both = jnp.where(lane < HEAD, even, odd)
        out.append(both + pltpu.roll(both, HEAD, 1))
    return out


def store_half(ref, value, half):
    lane = lax.broadcasted_iota(jnp.int32, value.shape, 1)
    ref[0] = jnp.where(lane // HEAD == half, value, ref[0].astype(F32)).astype(ref.dtype)


def softmax_kernel(first_ref, q_ref, go_ref, key_ref, halo_ref, probs_ref, diag_ref, own_ref, back_ref):
    rows = key_ref.shape[1]
    u = lax.broadcasted_iota(jnp.int32, (rows, rows), 0)
    t = lax.broadcasted_iota(jnp.int32, (rows, rows), 1)
    later, same = u > t, u == t
    rate = HEAD ** (-0.5) * math.log2(math.e)
    shift = jnp.where(first_ref[0] == 1, -1e30, 0.0).astype(F32)
    half = pl.program_id(1)
    keys = stacked(key_ref[0], halo_ref[0], half)
    total = jnp.zeros((4 * rows, LANES), F32)
    for pair in range(q_ref.shape[1] // LANES):
        cols = slice(pair * LANES, (pair + 1) * LANES)
        scores = lax.dot_general(keys, q_ref[:, cols], NT, preferred_element_type=F32)
        weights = []
        for head in range(2):
            own = scores[2 * head * rows : (2 * head + 1) * rows]
            halo = scores[(2 * head + 1) * rows : (2 * head + 2) * rows] + shift
            mixed = jnp.where(later, halo, own)
            diag = jnp.sum(jnp.where(same, halo, 0.0), axis=0, keepdims=True)
            peak = jnp.maximum(jnp.max(mixed, axis=0, keepdims=True), diag)
            mixed = jnp.exp2((mixed - peak) * rate)
            diag = jnp.exp2((diag - peak) * rate)
            inverse = 1.0 / (jnp.sum(mixed, axis=0, keepdims=True) + diag)
            mixed = mixed * inverse
            diag = diag * inverse
            index = 2 * pair + head
            probs_ref[0, index] = mixed.astype(BF16)
            diag_ref[0, index : index + 1] = diag
            weights.append(jnp.where(later, 0.0, mixed).astype(BF16))
            weights.append(jnp.where(later, mixed, jnp.where(same, diag, 0.0)).astype(BF16))
        total += jnp.dot(
            jnp.concatenate(weights, axis=0), go_ref[:, cols], preferred_element_type=F32
        )
    own, back = folded(total)
    store_half(own_ref, own, half)
    store_half(back_ref, back, half)


def scores_kernel(
    q_ref, go_ref, key_ref, key_halo_ref, value_ref, value_halo_ref, probs_ref, diag_ref,
    gq_ref, own_ref, back_ref,
):
    rows = key_ref.shape[1]
    u = lax.broadcasted_iota(jnp.int32, (rows, rows), 0)
    t = lax.broadcasted_iota(jnp.int32, (rows, rows), 1)
    later, same = u > t, u == t
    factor = HEAD ** (-0.5)
    half = pl.program_id(1)
    keys = stacked(key_ref[0], key_halo_ref[0], half)
    keys_across = keys.astype(F32).T.astype(BF16)
    values = stacked(value_ref[0], value_halo_ref[0], half)
    total = jnp.zeros((4 * rows, LANES), F32)
    for pair in range(q_ref.shape[1] // LANES):
        cols = slice(pair * LANES, (pair + 1) * LANES)
        grads = lax.dot_general(values, go_ref[:, cols], NT, preferred_element_type=F32)
        terms = []
        for head in range(2):
            own = grads[2 * head * rows : (2 * head + 1) * rows]
            halo = grads[(2 * head + 1) * rows : (2 * head + 2) * rows]
            index = 2 * pair + head
            probs = probs_ref[0, index].astype(F32)
            diag = diag_ref[0, index : index + 1]
            mixed = jnp.where(later, halo, own)
            edge = jnp.sum(jnp.where(same, halo, 0.0), axis=0, keepdims=True)
            delta = jnp.sum(probs * mixed, axis=0, keepdims=True) + diag * edge
            mixed = probs * (mixed - delta)
            edge = diag * (edge - delta)
            terms.append(jnp.where(later, 0.0, mixed).astype(BF16))
            terms.append(jnp.where(later, mixed, jnp.where(same, edge, 0.0)).astype(BF16))
        stack = jnp.concatenate(terms, axis=0)
        total += jnp.dot(stack, q_ref[:, cols], preferred_element_type=F32)
        across = jnp.dot(keys_across, stack, preferred_element_type=F32)
        gq_ref[:, cols] = (across.T * factor).astype(BF16)
    own, back = folded(total)
    store_half(own_ref, own * factor, half)
    store_half(back_ref, back * factor, half)


def by_head(array):
    rows, width = array.shape
    return pl.BlockSpec((rows, width // KV_HEADS), lambda q, h: (0, h * QUARTERS + q))


def by_step(array):
    block = (1,) + array.shape[1:]
    return pl.BlockSpec(block, lambda q, h: (2 * q + h,) + (0,) * (len(block) - 1))


def by_quarter(array):
    block = (1,) + array.shape[1:]
    return pl.BlockSpec(block, lambda q, h: (q,) + (0,) * (len(block) - 1))


def softmax_part(first, queries, grad_out, keys, halo):
    rows, width = queries.shape
    group = width // (KV_HEADS * HEAD)
    probs = struct((KV_HEADS, group, rows, rows), BF16)
    diag = struct((KV_HEADS, group, rows), F32)
    sums = struct(keys.shape, F32)
    back = struct(keys.shape, BF16)
    return pl.pallas_call(
        softmax_kernel,
        grid=(QUARTERS, 2),
        in_specs=[SMEM] + [by_head(queries)] * 2 + [by_quarter(keys)] * 2,
        out_specs=[by_step(probs), by_step(diag), by_quarter(sums), by_quarter(back)],
        out_shape=[probs, diag, sums, back],
        compiler_params=params(),
        cost_estimate=cost(8 * rows * rows * width, queries, grad_out, probs),
        name="softmax_part",
    )(first, queries, grad_out, keys, halo)


def scores_part(queries, grad_out, keys, halo, values, value_halo, probs, diag):
    rows, width = queries.shape
    sums = struct(keys.shape, F32)
    back = struct(keys.shape, BF16)
    return pl.pallas_call(
        scores_kernel,
        grid=(QUARTERS, 2),
        in_specs=[by_head(queries)] * 2
        + [by_quarter(keys)] * 4
        + [by_step(probs), by_step(diag)],
        out_specs=[by_head(queries), by_quarter(sums), by_quarter(back)],
        out_shape=[struct(queries.shape, BF16), sums, back],
        compiler_params=params(),
        cost_estimate=cost(12 * rows * rows * width, queries, grad_out, queries, probs),
        name="scores_part",
    )(queries, grad_out, keys, halo, values, value_halo, probs, diag)


def project_kernel(place_ref, *refs):
    pieces, hidden = refs[:8], refs[8:12]
    weight_ref, outs = refs[12], refs[13:]
    hi, z = place_ref[0], place_ref[1]
    step = pieces[0].shape[0]
    depth = len(pieces) // 2
    for r in range(2):
        for k in range(depth):
            row = ((hi ^ r) * depth + (z ^ k)) * step
            weight_ref[pl.ds(pl.multiple_of(row, step), step), :] = pieces[r * depth + k][...]
    weight = weight_ref[...]
    for h_ref, out_ref in zip(hidden, outs):
        across = jnp.dot(weight, h_ref[...], preferred_element_type=F32)
        out_ref[...] = across.T.astype(BF16)


def project(place, pieces, hidden):
    depth, tokens = hidden[0].shape
    cols = sum(p.shape[0] for p in pieces)
    weight = struct((cols, depth), BF16)
    out = struct((tokens, cols), BF16)
    return pl.pallas_call(
        project_kernel,
        in_specs=[SMEM] + [VMEM] * (len(pieces) + len(hidden)),
        out_specs=[VMEM] * (1 + len(hidden)),
        out_shape=[weight] + [out] * len(hidden),
        compiler_params=params(),
        cost_estimate=cost(2 * 4 * tokens * cols * depth, *hidden, weight, weight),
        name="project",
    )(place, *pieces, *hidden)


def arrange_kernel(place_ref, *refs):
    out_ref = refs[-1]
    for r, ref in enumerate(refs[:-1]):
        out_ref[place_ref[2] ^ r] = ref[...]


def arrange(place, parts):
    return pl.pallas_call(
        arrange_kernel,
        in_specs=[SMEM] + [VMEM] * len(parts),
        out_specs=VMEM,
        out_shape=struct((len(parts),) + parts[0].shape, BF16),
        compiler_params=params(),
        name="arrange",
    )(place, *parts)


def natural(quarters):
    lane = lax.broadcasted_iota(jnp.int32, quarters[0].shape, 1)
    blocks = []
    for half in range(2):
        for first in range(0, QUARTERS, 2):
            left, right = quarters[first], quarters[first + 1]
            if half == 0:
                right = pltpu.roll(right, HEAD, 1)
            else:
                left = pltpu.roll(left, HEAD, 1)
            blocks.append(jnp.where(lane < HEAD, left, right))
    return blocks


def finish_kernel(place_ref, own_ref, back_ref, natural_ref, all_ref, *outs):
    quarters = []
    for q in range(QUARTERS):
        total = (own_ref[q] + back_ref[q].astype(F32)).astype(BF16)
        all_ref[q] = total
        quarters.append(total.astype(F32))
    for m, block in enumerate(natural(quarters)):
        natural_ref[:, m * LANES : (m + 1) * LANES] = block.astype(BF16)
    for r, ref in enumerate(outs):
        ref[...] = all_ref[place_ref[2] ^ r]


def finish(place, own, back):
    rows = own.shape[1]
    part = struct(own.shape[1:], BF16)
    return pl.pallas_call(
        finish_kernel,
        in_specs=[SMEM, VMEM, VMEM],
        out_specs=[VMEM] * (2 + QUARTERS),
        out_shape=[struct((rows, QUARTERS * LANES), BF16), struct(own.shape, BF16)]
        + [part] * QUARTERS,
        compiler_params=params(),
        name="finish",
    )(place, own, back)


def spans(size, step):
    return [(at, min(step, size - at)) for at in range(0, size, step)]


def weight_grad_kernel(place_ref, *refs):
    grads, hidden = refs[:4], refs[4:8]
    keep_ref, send_ref, wide_ref = refs[8:]
    hi, z = place_ref[0], place_ref[1]
    for at, size in spans(hidden[0].shape[0], 256):
        total = jnp.zeros((size, grads[0].shape[1]), F32)
        for g_ref, h_ref in zip(grads, hidden):
            total += jnp.dot(h_ref[at : at + size, :], g_ref[...], preferred_element_type=F32)
        wide_ref[:, at : at + size] = total.T
    depth, step = keep_ref.shape[:2]
    for k in range(depth):
        for r, ref in enumerate((keep_ref, send_ref)):
            row = ((hi ^ r) * depth + (z ^ k)) * step
            ref[k] = wide_ref[pl.ds(pl.multiple_of(row, step), step), :].astype(BF16)


def weight_grad(place, grads, hidden, depth):
    size, tokens = hidden[0].shape
    cols = grads[0].shape[1]
    part = struct((depth, cols // (2 * depth), size), BF16)
    return pl.pallas_call(
        weight_grad_kernel,
        in_specs=[SMEM] + [VMEM] * 8,
        out_specs=[VMEM] * 2,
        out_shape=[part] * 2,
        scratch_shapes=[pltpu.VMEM((cols, size), F32)],
        compiler_params=params(),
        cost_estimate=cost(2 * 4 * tokens * cols * size, *hidden, part, part),
        name="weight_grad",
    )(place, *grads, *hidden)


def input_grad_kernel(place_ref, key_ref, value_ref, *refs):
    out_ref = refs[-1]
    weights = (refs[:QUARTERS], refs[QUARTERS:-1])
    for at, size in spans(out_ref.shape[0], 256):
        total = jnp.zeros((key_ref.shape[1], size), F32)
        for grad_ref, group in zip((key_ref, value_ref), weights):
            for r, w_ref in enumerate(group):
                total += jnp.dot(
                    grad_ref[place_ref[2] ^ r],
                    w_ref[:, at : at + size],
                    preferred_element_type=F32,
                )
        out_ref[at : at + size, :] = total.T.astype(BF16)


def input_grad(place, key_all, value_all, key_weights, value_weights):
    cols, size = key_weights[0].shape
    rows = key_all.shape[1]
    out = struct((size, rows), BF16)
    return pl.pallas_call(
        input_grad_kernel,
        in_specs=[SMEM] + [VMEM] * 10,
        out_specs=VMEM,
        out_shape=out,
        compiler_params=params(),
        cost_estimate=cost(16 * rows * cols * size, *key_weights, *value_weights, out),
        name="input_grad",
    )(place, key_all, value_all, *key_weights, *value_weights)


def flip(array, axis, by):
    return lax.ppermute(array, axis, [(i, i ^ by) for i in range(lax.axis_size(axis))])


def flip_group(array, by):
    return lax.ppermute(array, ("x", "c"), [(i, i ^ by) for i in range(QUARTERS)])


def shifted(array, by):
    size = lax.axis_size(AXES)
    pairs = [(i, i + by) for i in range(size) if 0 <= i + by < size]
    return lax.ppermute(array, AXES, pairs)


def gathered(weight):
    depth = lax.axis_size("z")
    mine = [weight] + [flip(weight, "z", k) for k in range(1, depth)]
    return mine + [flip(piece, "hi", 1) for piece in mine]


def scattered(keep, send):
    got = flip(send, "hi", 1)
    total = keep.astype(F32) + got.astype(F32)
    depth = total.shape[0]
    result = total[0]
    for k in range(1, depth):
        result = result + flip(total[k].astype(BF16), "z", k).astype(F32)
    return result


def fast_shards(hidden_in, queries, grad_out, key_weight, value_weight):
    here = lax.axis_index(AXES)
    group = lax.axis_index(("x", "c"))
    place = jnp.stack([lax.axis_index("hi"), lax.axis_index("z"), group]).astype(jnp.int32)
    first = (here == 0).astype(jnp.int32).reshape(1)
    own = hidden_in.T
    across = flip(own, "x", 1)
    hidden = [own, flip(own, "c", 1), across, flip(across, "c", 1)]
    depth = lax.axis_size("z")
    key_pieces = gathered(key_weight.T)
    value_pieces = gathered(value_weight.T)

    def projected(pieces):
        weight, *parts = project(place, pieces, hidden)
        parts = [parts[0]] + [flip_group(parts[r], r) for r in range(1, QUARTERS)]
        rows = arrange(place, parts)
        return weight, rows, shifted(rows, 1)

    key_mine, keys, key_halo = projected(key_pieces)
    value_mine, values, value_halo = projected(value_pieces)

    def filled(mine):
        x_side = flip(mine, "x", 1)
        return [mine, flip(mine, "c", 1), x_side, flip(x_side, "c", 1)]

    key_weights, value_weights = filled(key_mine), filled(value_mine)
    probs, diag, value_own, value_back = softmax_part(first, queries, grad_out, keys, key_halo)

    def finished(sums, back):
        rows, every, *parts = finish(place, sums, shifted(back, -1))
        parts = [parts[0]] + [flip_group(parts[r], r) for r in range(1, QUARTERS)]
        return rows, every, scattered(*weight_grad(place, parts, hidden, depth))

    grad_values, value_every, value_total = finished(value_own, value_back)
    grad_queries, key_own, key_back = scores_part(
        queries, grad_out, keys, key_halo, values, value_halo, probs, diag
    )
    grad_keys, key_every, key_total = finished(key_own, key_back)
    grad_inputs = input_grad(place, key_every, value_every, key_weights, value_weights).T
    scale = (hidden_in.shape[0] * lax.axis_size(AXES)) ** (-0.5)
    return (
        grad_queries,
        grad_keys,
        grad_values,
        grad_inputs,
        (key_total * scale).T,
        (value_total * scale).T,
    )


def to_quarters(rows):
    count = rows.shape[0]
    split = rows.reshape(count, 2, QUARTERS, HEAD)
    return jnp.transpose(split, (2, 0, 1, 3)).reshape(QUARTERS, count, 2 * HEAD)


def from_quarters(quarters):
    count = quarters.shape[1]
    split = quarters.reshape(QUARTERS, count, 2, HEAD)
    return jnp.transpose(split, (1, 2, 0, 3)).reshape(count, 2 * QUARTERS * HEAD)


def plain_shards(hidden_in, queries, grad_out, key_weight, value_weight):
    key_full = lax.all_gather(key_weight.T, AXES, axis=0, tiled=True)
    value_full = lax.all_gather(value_weight.T, AXES, axis=0, tiled=True)
    first = (lax.axis_index(AXES) == 0).astype(jnp.int32).reshape(1)

    def rows_of(weight):
        rows = lax.dot_general(hidden_in, weight, NT, preferred_element_type=F32)
        return to_quarters(rows.astype(BF16))

    keys, values = rows_of(key_full), rows_of(value_full)
    key_halo, value_halo = shifted(keys, 1), shifted(values, 1)
    probs, diag, value_own, value_back = softmax_part(first, queries, grad_out, keys, key_halo)
    grad_queries, key_own, key_back = scores_part(
        queries, grad_out, keys, key_halo, values, value_halo, probs, diag
    )
    grad_keys = from_quarters(key_own + shifted(key_back, -1)).astype(BF16)
    grad_values = from_quarters(value_own + shifted(value_back, -1)).astype(BF16)
    grad_inputs = (
        jnp.dot(grad_keys, key_full, preferred_element_type=F32)
        + jnp.dot(grad_values, value_full, preferred_element_type=F32)
    ).astype(BF16)
    scale = (hidden_in.shape[0] * lax.axis_size(AXES)) ** (-0.5)

    def summed(grad):
        rows = (((0,), (0,)), ((), ()))
        part = lax.dot_general(grad, hidden_in, rows, preferred_element_type=F32)
        return (lax.psum_scatter(part, AXES, scatter_dimension=0, tiled=True) * scale).T

    return (
        grad_queries,
        grad_keys,
        grad_values,
        grad_inputs,
        summed(grad_keys),
        summed(grad_values),
    )


def solution(mesh):
    outer, inner = mesh.shape["seqa"], mesh.shape["seqb"]
    split = Mesh(mesh.devices.reshape(outer // QUARTERS, 2, 2, inner), AXES)
    cols = KV_HEADS * HEAD // (outer * inner)
    fast = outer == 2 * QUARTERS and inner & (inner - 1) == 0 and cols % SUBLANES == 0
    rows, columns = P(AXES, None), P(None, AXES)
    return jax.shard_map(
        fast_shards if fast else plain_shards,
        mesh=split,
        in_specs=(rows, rows, rows, columns, columns),
        out_specs=(rows, rows, rows, rows, columns, columns),
        check_vma=False,
    )
```

time: 379 us -> 195 us (0.51)
  waiting for transfers between devices: 203 us -> 61.8 us
  matrix products: 76.5 us -> 0 us
  starting transfers between devices: 10.4 us -> 61.1 us
  Pallas kernels: 0 us -> 34.5 us
  blocking collectives: 33.9 us -> 0 us
  between operations: 14.3 us -> 0.89 us
  local copies, waits for them, and re-layouts: 34.5 us -> 28.8 us
    unnamed x10 -> x0, waiting for transfers between devices: 141 us -> none
    dot_general x46 -> x0, matrix products: 64.5 us -> none  [the longest x8 12.7 us: head_group(): jnp.einsum('tgh,lh->gtl', grad_heads, value_rows, preferred_element_type=...]
    ppermute x4 -> x47, starting transfers between devices: 10 us -> 61.1 us  [the longest x31 39.2 us: flip(): lax.ppermute(array, axis, [(i, i ^ by) for i in range(lax.axis_size(axis))])]
    all_gather x2 -> x0, waiting for transfers between devices: 43.3 us -> none  [the longest x1 27.3 us: shards(): lax.all_gather(inner_cols[1], 'seqa', axis=1, tiled=True)]
    ppermute x4 -> x47, waiting for transfers between devices: 18.7 us -> 61.8 us  [the longest x31 53.1 us: flip(): lax.ppermute(array, axis, [(i, i ^ by) for i in range(lax.axis_size(axis))])]
    pallas_call x0 -> x11, Pallas kernels: none -> 34.5 us  [the longest x1 11.9 us: scores_part(): pl.pallas_call(scores_kernel, grid=(QUARTERS, 2), in_specs=[by_head(queri...]
    all_gather x2 -> x0, blocking collectives: 33.9 us -> none  [the longest x1 18.2 us: shards(): lax.all_gather(key_weight, 'seqb', axis=1, tiled=True)]
    unnamed x20 -> x38, local copies, waits for them, and re-layouts: 25.6 us -> 11.4 us
  transfers between devices with their start and end apart: 10 -> 47, of which waited for: 9 -> 16; matrix products, arithmetic and copies ran while one was open for 9% -> 11% of each run, Pallas kernels for 0% -> 15%
where the time goes in v1:
time: 195 us; the launch traced here: 194 us
  waiting for transfers between devices  61.8 us (32%)
  starting transfers between devices  61.1 us (31%)
  Pallas kernels  34.5 us (18%)
  local copies, waits for them, and re-layouts  28.8 us (15%)
  other arithmetic  6.43 us (3%)
    ppermute x31, waiting for transfers between devices, flip(): lax.ppermute(array, axis, [(i, i ^ by) for i in range(lax.axis_size(axis))])  53.1 us
    ppermute x31, starting transfers between devices, flip(): lax.ppermute(array, axis, [(i, i ^ by) for i in range(lax.axis_size(axis))])  39.2 us
    ppermute x12, starting transfers between devices, flip_group(): lax.ppermute(array, ('x', 'c'), [(i, i ^ by) for i in range(QUARTERS)])  13.7 us
    ppermute x6, local copies, waits for them, and re-layouts, flip(): lax.ppermute(array, axis, [(i, i ^ by) for i in range(lax.axis_size(axis))])  12.8 us
    pallas_call x1, Pallas kernels, scores_part(): pl.pallas_call(scores_kernel, grid=(QUARTERS, 2), in_specs=[by_head(queri...  11.9 us
    unnamed x38, local copies, waits for them, and re-layouts  11.4 us
    ppermute x4, starting transfers between devices, shifted(): return lax.ppermute(array, AXES, pairs)  8.28 us
    pallas_call x1, Pallas kernels, softmax_part(): pl.pallas_call(softmax_kernel, grid=(QUARTERS, 2), in_specs=[SMEM] + [by_...  7.1 us
  transfers between devices with their start and end apart: 47, of which 16 were waited for; matrix products, arithmetic and copies ran while one was open for 11% of the time, Pallas kernels for 15%

profile of v1, /device:TPU:0, one launch (start us, length us, event | category | flops | bytes accessed | tf_op | source)
XLA Modules:
  0.0 193.6 jit_solution(4758732780012140332)
XLA Ops:
  0.6 3.0 %collective-permute-start.8 = (bf16[2880,128]{1,0:T(8,128)(2,1)}, bf16[2880,128]{1,0:T(8,128)(2,1)S(1)}, u32[]{:S(2)}, u32[]{:S(2)}) collective-permute-start(bf16[2880,128]{1,0:T(8,128)(2,1)} %bitcast.48), channel_id=1, source_target_pairs={{0,8},{8,0},{1,9},{9,1},{2,10},{10,2},{3,11},{11,3},{4,12},{12,4},... | collective-permute-start | bytes 2211848 | tf_op jit(solution)/shard_map/ppermute | solution.py:358
  3.6 16.7 %collective-permute-done.8.refs_10_.refs_6_ = bf16[2880,128]{1,0:T(8,128)(2,1)S(1)} collective-permute-done((bf16[2880,128]{1,0:T(8,128)(2,1)}, bf16[2880,128]{1,0:T(8,128)(2,1)S(1)}, u32[]{:S(2)}, u32[]{:S(2)}) %collective-permute-start.8) | collective-permute-done | bytes 737312 | tf_op jit(solution)/shard_map/ppermute | solution.py:358
  22.2 2.6 %collective-permute-start.1 = (bf16[16,2880]{1,0:T(8,128)(2,1)}, bf16[16,2880]{1,0:T(8,128)(2,1)S(1)}, u32[]{:S(2)}, u32[]{:S(2)}) collective-permute-start(bf16[16,2880]{1,0:T(8,128)(2,1)} %bitcast.55), channel_id=1, source_target_pairs={{0,2},{1,3},{2,0},{3,1},{4,6},{5,7},{6,4},{7,5},{8,10},{9,11},{10,... | collective-permute-start | bytes 276488 | tf_op jit(solution)/shard_map/ppermute | solution.py:358
  27.4 5.4 %collective-permute-done.1.refs_2_ = bf16[16,2880]{1,0:T(8,128)(2,1)S(1)} collective-permute-done((bf16[16,2880]{1,0:T(8,128)(2,1)}, bf16[16,2880]{1,0:T(8,128)(2,1)S(1)}, u32[]{:S(2)}, u32[]{:S(2)}) %collective-permute-start.1) | collective-permute-done | bytes 92192 | tf_op jit(solution)/shard_map/ppermute | solution.py:358
  49.9 3.2 %collective-permute-start.13 = (bf16[4,128,128]{2,1,0:T(8,128)(2,1)S(1)}, bf16[4,128,128]{2,1,0:T(8,128)(2,1)S(1)}, u32[]{:S(2)}, u32[]{:S(2)}) collective-permute-start(bf16[4,128,128]{2,1,0:T(8,128)(2,1)S(1)} %arrange.2.key_ref), channel_id=1, source_target_pairs={{0,1},{1,2},{2,3},{3,4},{4,5},{5,6},{6,7},{7,8},{8,9},{9,10},{10,1... | collective-permute-start | bytes 393224 | tf_op jit(solution)/shard_map/ppermute | solution.py:368
  59.2 3.5 %collective-permute-done.14.refs_1_ = bf16[16,2880]{1,0:T(8,128)(2,1)S(1)} collective-permute-done((bf16[16,2880]{1,0:T(8,128)(2,1)S(1)}, bf16[16,2880]{1,0:T(8,128)(2,1)S(1)}, u32[]{:S(2)}, u32[]{:S(2)}) %collective-permute-start.14) | collective-permute-done | bytes 92192 | tf_op jit(solution)/shard_map/ppermute | solution.py:358
  69.6 7.1 %softmax_part.1 = (bf16[8,8,128,128]{3,2,1,0:T(8,128)(2,1)S(1)}, f32[8,8,128]{2,1,0:T(8,128)S(1)}, f32[4,128,128]{2,1,0:T(8,128)S(1)}, bf16[4,128,128]{2,1,0:T(8,128)(2,1)S(1)}) custom-call(s32[1]{0:T(128)} %bitcast.6.first_ref, bf16[128,4096]{1,0:T(8,128)(2,1)S(1)} %copy-done.2, bf16[128,4096]{1,0:T(8,128)(2,1)S(1)} %copy-done.4, ...), custom_call_target="tpu_custom_call" | custom-call | flops 536870912 | bytes 4194304 | tf_op jit(solution)/shard_map/softmax_part/pallas_call | solution.py:172
  81.0 3.2 %collective-permute-start.21 = (bf16[128,128]{1,0:T(8,128)(2,1)S(1)}, bf16[128,128]{1,0:T(8,128)(2,1)S(1)}, u32[]{:S(2)}, u32[]{:S(2)}) collective-permute-start(bf16[128,128]{1,0:T(8,128)(2,1)S(1)} %get-tuple-element.44), channel_id=1, source_target_pairs={{0,4},{4,0},{8,12},{12,8},{1,5},{5,1},{9,13},{13,9},{2,6},{6,2},{1... | collective-permute-start | bytes 98312 | tf_op jit(solution)/shard_map/ppermute | solution.py:362
  89.5 2.3 %collective-permute-start.24 = (bf16[4,128,128]{2,1,0:T(8,128)(2,1)S(1)}, bf16[4,128,128]{2,1,0:T(8,128)(2,1)S(1)}, u32[]{:S(2)}, u32[]{:S(2)}) collective-permute-start(bf16[4,128,128]{2,1,0:T(8,128)(2,1)S(1)} %arrange.3.value_ref), channel_id=1, source_target_pairs={{0,1},{1,2},{2,3},{3,4},{4,5},{5,6},{6,7},{7,8},{8,9},{9,10},{10,1... | collective-permute-start | bytes 393224 | tf_op jit(solution)/shard_map/ppermute | solution.py:368
  92.2 2.4 %weight_grad.3 = (bf16[4,16,2880]{2,1,0:T(8,128)(2,1)S(1)}, bf16[4,16,2880]{2,1,0:T(8,128)(2,1)}) custom-call(s32[3]{0:T(128)S(1)} %pad_add_fusion.place_ref, bf16[128,128]{1,0:T(8,128)(2,1)S(1)} %get-tuple-element.66.refs_0_, bf16[128,128]{1,0:T(8,128)(2,1)S(1)} %collective-permute-done.40.refs_1_, bf16[128,128]{1,0:T(8,128)(2,1)S(1)} %collective-permute-done.41.refs_2_, ...), custom_call_target="tpu_custom_call" | custom-call | flops 377487360 | bytes 3686400 | tf_op jit(solution)/shard_map/weight_grad/pallas_call | solution.py:315
  95.8 11.9 %scores_part.1 = (bf16[128,4096]{1,0:T(8,128)(2,1)}, f32[4,128,128]{2,1,0:T(8,128)S(1)}, bf16[4,128,128]{2,1,0:T(8,128)(2,1)S(1)}) custom-call(bf16[128,4096]{1,0:T(8,128)(2,1)S(1)} %copy-done.3, bf16[128,4096]{1,0:T(8,128)(2,1)S(1)} %copy-done.4, bf16[4,128,128]{2,1,0:T(8,128)(2,1)S(1)} %arrange.2.key_ref, ...), custom_call_target="tpu_custom_call" | custom-call | flops 805306368 | bytes 5242880 | tf_op jit(solution)/shard_map/scores_part/pallas_call | solution.py:188
  109.2 5.5 %collective-permute-done.25.back_ref = bf16[4,128,128]{2,1,0:T(8,128)(2,1)S(1)} collective-permute-done((bf16[4,128,128]{2,1,0:T(8,128)(2,1)S(1)}, bf16[4,128,128]{2,1,0:T(8,128)(2,1)S(1)}, u32[]{:S(2)}, u32[]{:S(2)}) %collective-permute-start.25) | collective-permute-done | bytes 131104 | tf_op jit(solution)/shard_map/ppermute | solution.py:368
  118.8 2.9 %collective-permute-start.34 = (bf16[128,128]{1,0:T(8,128)(2,1)}, bf16[128,128]{1,0:T(8,128)(2,1)}, u32[]{:S(2)}, u32[]{:S(2)}) collective-permute-start(bf16[128,128]{1,0:T(8,128)(2,1)} %get-tuple-element.62), channel_id=1, source_target_pairs={{0,8},{4,12},{8,0},{12,4},{1,9},{5,13},{9,1},{13,5},{2,10},{6,14},... | collective-permute-start | bytes 98312 | tf_op jit(solution)/shard_map/ppermute | solution.py:362
  125.7 2.3 %copy.11 = bf16[128,2880]{0,1:T(8,128)(2,1)} copy(bf16[128,2880]{1,0:T(8,128)(2,1)} %copy-done.5) | data formatting | bytes 1474560 | tf_op jit(solution)/shard_map/project/pallas_call | solution.py:223
  130.5 2.7 %collective-permute-start.36 = (bf16[4,16,2880]{2,1,0:T(8,128)(2,1)S(1)}, bf16[4,16,2880]{2,1,0:T(8,128)(2,1)S(1)}, u32[]{:S(2)}, u32[]{:S(2)}) collective-permute-start(bf16[4,16,2880]{2,1,0:T(8,128)(2,1)S(1)} %get-tuple-element.65), channel_id=1, source_target_pairs={{0,16},{16,0},{1,17},{17,1},{2,18},{18,2},{3,19},{19,3},{4,20},{20... | collective-permute-start | bytes 1105928 | tf_op jit(solution)/shard_map/ppermute | solution.py:358
  135.2 7.3 %collective-permute-done.36 = bf16[4,16,2880]{2,1,0:T(8,128)(2,1)S(1)} collective-permute-done((bf16[4,16,2880]{2,1,0:T(8,128)(2,1)S(1)}, bf16[4,16,2880]{2,1,0:T(8,128)(2,1)S(1)}, u32[]{:S(2)}, u32[]{:S(2)}) %collective-permute-start.36) | collective-permute-done | bytes 368672 | tf_op jit(solution)/shard_map/ppermute | solution.py:358
  143.7 2.9 %collective-permute-start.45 = (bf16[16,2880]{1,0:T(8,128)(2,1)S(1)}, bf16[16,2880]{1,0:T(8,128)(2,1)S(1)}, u32[]{:S(2)}, u32[]{:S(2)}) collective-permute-start(bf16[16,2880]{1,0:T(8,128)(2,1)S(1)} %get-tuple-element.78), channel_id=1, source_target_pairs={{0,2},{1,3},{2,0},{3,1},{4,6},{5,7},{6,4},{7,5},{8,10},{9,11},{10,... | collective-permute-start | bytes 276488 | tf_op jit(solution)/shard_map/ppermute | solution.py:358
  146.5 12.2 %collective-permute-done.28 = bf16[128,2880]{0,1:T(8,128)(2,1)} collective-permute-done((bf16[128,2880]{0,1:T(8,128)(2,1)}, bf16[128,2880]{0,1:T(8,128)(2,1)}, u32[]{:S(2)}, u32[]{:S(2)}) %collective-permute-start.28) | collective-permute-done | bytes 737312 | tf_op jit(solution)/shard_map/ppermute | solution.py:358
  158.8 3.5 %collective-permute-start.46 = (bf16[16,2880]{1,0:T(8,128)(2,1)S(1)}, bf16[16,2880]{1,0:T(8,128)(2,1)S(1)}, u32[]{:S(2)}, u32[]{:S(2)}) collective-permute-start(bf16[16,2880]{1,0:T(8,128)(2,1)S(1)} %get-tuple-element.77), channel_id=1, source_target_pairs={{0,3},{1,2},{2,1},{3,0},{4,7},{5,6},{6,5},{7,4},{8,11},{9,10},{10,... | collective-permute-start | bytes 276488 | tf_op jit(solution)/shard_map/ppermute | solution.py:358
  164.5 2.3 %copy.16.refs_2_ = bf16[128,2880]{1,0:T(8,128)(2,1)} copy(bf16[128,2880]{0,1:T(8,128)(2,1)} %collective-permute-done.28) | data formatting | bytes 1474560 | tf_op jit(solution)/shard_map/ppermute | solution.py:358
  171.5 3.5 %collective-permute-start.39 = (bf16[16,2880]{1,0:T(8,128)(2,1)S(1)}, bf16[16,2880]{1,0:T(8,128)(2,1)S(1)}, u32[]{:S(2)}, u32[]{:S(2)}) collective-permute-start(bf16[16,2880]{1,0:T(8,128)(2,1)S(1)} %get-tuple-element.80), channel_id=1, source_target_pairs={{0,3},{1,2},{2,1},{3,0},{4,7},{5,6},{6,5},{7,4},{8,11},{9,10},{10,... | collective-permute-start | bytes 276488 | tf_op jit(solution)/shard_map/ppermute | solution.py:358
  180.8 2.3 %copy.20.refs_7_ = bf16[128,2880]{1,0:T(8,128)(2,1)} copy(bf16[128,2880]{0,1:T(8,128)(2,1)} %collective-permute-done.32) | data formatting | bytes 1474560 | tf_op jit(solution)/shard_map/ppermute | solution.py:358
  183.0 2.3 %copy.17.refs_3_ = bf16[128,2880]{1,0:T(8,128)(2,1)} copy(bf16[128,2880]{0,1:T(8,128)(2,1)} %collective-permute-done.29) | data formatting | bytes 1474560 | tf_op jit(solution)/shard_map/ppermute | solution.py:358
  189.8 3.8 %input_grad.1 = bf16[2880,128]{1,0:T(8,128)(2,1)} custom-call(s32[3]{0:T(128)S(1)} %pad_add_fusion.place_ref, bf16[4,128,128]{2,1,0:T(8,128)(2,1)S(1)} %copy-done.16, bf16[4,128,128]{2,1,0:T(8,128)(2,1)S(1)} %get-tuple-element.57.value_ref, bf16[128,2880]{1,0:T(8,128)(2,1)S(1)} %copy-done.6, bf16[128,2880]{1,0:T(8,128)(2,1)S(1)} %copy.15.refs_1_, ...), custom_call_target="tpu_custom_call" | custom-call | flops 754974720 | bytes 6635520 | tf_op jit(solution)/shard_map/input_grad/pallas_call | solution.py:346
  (134 shorter events, 78.1 us)
Async XLA Ops:
  0.6 19.7 %collective-permute-start.8 = (bf16[2880,128]{1,0:T(8,128)(2,1)}, bf16[2880,128]{1,0:T(8,128)(2,1)S(1)}, u32[]{:S(2)}, u32[]{:S(2)}) collective-permute-start(bf16[2880,128]{1,0:T(8,128)(2,1)} %bitcast.48), channel_id=1, source_target_pairs={{0,8},{8,0},{1,9},{9,1},{2,10},{10,2},{3,11},{11,3},{4,12},{12,4},... | collective-permute-start | bytes 2211848 | tf_op jit(solution)/shard_map/ppermute | solution.py:358
  3.6 36.3 %collective-permute-start.7 = (bf16[2880,128]{1,0:T(8,128)(2,1)}, bf16[2880,128]{1,0:T(8,128)(2,1)S(1)}, u32[]{:S(2)}, u32[]{:S(2)}) collective-permute-start(bf16[2880,128]{1,0:T(8,128)(2,1)} %bitcast.49), channel_id=1, source_target_pairs={{0,4},{4,0},{1,5},{5,1},{2,6},{6,2},{3,7},{7,3},{8,12},{12,8},{9,1... | collective-permute-start | bytes 2211848 | tf_op jit(solution)/shard_map/ppermute | solution.py:358
  20.3 19.6 %collective-permute-start.9 = (bf16[2880,128]{1,0:T(8,128)(2,1)S(1)}, bf16[2880,128]{1,0:T(8,128)(2,1)S(1)}, u32[]{:S(2)}, u32[]{:S(2)}) collective-permute-start(bf16[2880,128]{1,0:T(8,128)(2,1)S(1)} %collective-permute-done.8.refs_10_.refs_6_), channel_id=1, source_target_pairs={{0,4},{4,0},{1,5},{5,1},{2,6},{6,2},{3,7},{7,3},{8,12},{12,8},{9,1... | collective-permute-start | bytes 2211848 | tf_op jit(solution)/shard_map/ppermute | solution.py:358
  22.2 10.7 %collective-permute-start.1 = (bf16[16,2880]{1,0:T(8,128)(2,1)}, bf16[16,2880]{1,0:T(8,128)(2,1)S(1)}, u32[]{:S(2)}, u32[]{:S(2)}) collective-permute-start(bf16[16,2880]{1,0:T(8,128)(2,1)} %bitcast.55), channel_id=1, source_target_pairs={{0,2},{1,3},{2,0},{3,1},{4,6},{5,7},{6,4},{7,5},{8,10},{9,11},{10,... | collective-permute-start | bytes 276488 | tf_op jit(solution)/shard_map/ppermute | solution.py:358
  24.8 9.6 %collective-permute-start.2 = (bf16[16,2880]{1,0:T(8,128)(2,1)}, bf16[16,2880]{1,0:T(8,128)(2,1)S(1)}, u32[]{:S(2)}, u32[]{:S(2)}) collective-permute-start(bf16[16,2880]{1,0:T(8,128)(2,1)} %bitcast.56), channel_id=1, source_target_pairs={{0,3},{1,2},{2,1},{3,0},{4,7},{5,6},{6,5},{7,4},{8,11},{9,10},{10,... | collective-permute-start | bytes 276488 | tf_op jit(solution)/shard_map/ppermute | solution.py:358
  49.9 17.2 %collective-permute-start.13 = (bf16[4,128,128]{2,1,0:T(8,128)(2,1)S(1)}, bf16[4,128,128]{2,1,0:T(8,128)(2,1)S(1)}, u32[]{:S(2)}, u32[]{:S(2)}) collective-permute-start(bf16[4,128,128]{2,1,0:T(8,128)(2,1)S(1)} %arrange.2.key_ref), channel_id=1, source_target_pairs={{0,1},{1,2},{2,3},{3,4},{4,5},{5,6},{6,7},{7,8},{8,9},{9,10},{10,1... | collective-permute-start | bytes 393224 | tf_op jit(solution)/shard_map/ppermute | solution.py:368
  54.6 9.6 %collective-permute-start.15 = (bf16[16,2880]{1,0:T(8,128)(2,1)S(1)}, bf16[16,2880]{1,0:T(8,128)(2,1)S(1)}, u32[]{:S(2)}, u32[]{:S(2)}) collective-permute-start(bf16[16,2880]{1,0:T(8,128)(2,1)S(1)} %bitcast.60), channel_id=1, source_target_pairs={{0,2},{1,3},{2,0},{3,1},{4,6},{5,7},{6,4},{7,5},{8,10},{9,11},{10,... | collective-permute-start | bytes 276488 | tf_op jit(solution)/shard_map/ppermute | solution.py:358
  56.2 10.0 %collective-permute-start.16 = (bf16[16,2880]{1,0:T(8,128)(2,1)S(1)}, bf16[16,2880]{1,0:T(8,128)(2,1)}, u32[]{:S(2)}, u32[]{:S(2)}) collective-permute-start(bf16[16,2880]{1,0:T(8,128)(2,1)S(1)} %bitcast.61), channel_id=1, source_target_pairs={{0,3},{1,2},{2,1},{3,0},{4,7},{5,6},{6,5},{7,4},{8,11},{9,10},{10,... | collective-permute-start | bytes 276488 | tf_op jit(solution)/shard_map/ppermute | solution.py:358
  57.6 20.3 %collective-permute-start.17 = (bf16[16,2880]{1,0:T(8,128)(2,1)S(1)}, bf16[16,2880]{1,0:T(8,128)(2,1)}, u32[]{:S(2)}, u32[]{:S(2)}) collective-permute-start(bf16[16,2880]{1,0:T(8,128)(2,1)S(1)} %bitcast.62), channel_id=1, source_target_pairs={{0,16},{16,0},{1,17},{17,1},{2,18},{18,2},{3,19},{19,3},{4,20},{20... | collective-permute-start | bytes 276488 | tf_op jit(solution)/shard_map/ppermute | solution.py:358
  62.6 15.3 %collective-permute-start.18 = (bf16[16,2880]{1,0:T(8,128)(2,1)S(1)}, bf16[16,2880]{1,0:T(8,128)(2,1)S(1)}, u32[]{:S(2)}, u32[]{:S(2)}) collective-permute-start(bf16[16,2880]{1,0:T(8,128)(2,1)S(1)} %collective-permute-done.14.refs_1_), channel_id=1, source_target_pairs={{0,16},{16,0},{1,17},{17,1},{2,18},{18,2},{3,19},{19,3},{4,20},{20... | collective-permute-start | bytes 276488 | tf_op jit(solution)/shard_map/ppermute | solution.py:358
  64.2 13.8 %collective-permute-start.19 = (bf16[16,2880]{1,0:T(8,128)(2,1)S(1)}, bf16[16,2880]{1,0:T(8,128)(2,1)S(1)}, u32[]{:S(2)}, u32[]{:S(2)}) collective-permute-start(bf16[16,2880]{1,0:T(8,128)(2,1)S(1)} %collective-permute-done.15.refs_2_), channel_id=1, source_target_pairs={{0,16},{16,0},{1,17},{17,1},{2,18},{18,2},{3,19},{19,3},{4,20},{20... | collective-permute-start | bytes 276488 | tf_op jit(solution)/shard_map/ppermute | solution.py:358
  66.1 11.9 %collective-permute-start.20 = (bf16[16,2880]{1,0:T(8,128)(2,1)}, bf16[16,2880]{1,0:T(8,128)(2,1)S(1)}, u32[]{:S(2)}, u32[]{:S(2)}) collective-permute-start(bf16[16,2880]{1,0:T(8,128)(2,1)} %collective-permute-done.16.refs_3_), channel_id=1, source_target_pairs={{0,16},{16,0},{1,17},{17,1},{2,18},{18,2},{3,19},{19,3},{4,20},{20... | collective-permute-start | bytes 276488 | tf_op jit(solution)/shard_map/ppermute | solution.py:358
  94.6 36.0 %collective-permute-start.43 = (bf16[4,16,2880]{2,1,0:T(8,128)(2,1)}, bf16[4,16,2880]{2,1,0:T(8,128)(2,1)}, u32[]{:S(2)}, u32[]{:S(2)}) collective-permute-start(bf16[4,16,2880]{2,1,0:T(8,128)(2,1)} %get-tuple-element.71), channel_id=1, source_target_pairs={{0,16},{16,0},{1,17},{17,1},{2,18},{18,2},{3,19},{19,3},{4,20},{20... | collective-permute-start | bytes 1105928 | tf_op jit(solution)/shard_map/ppermute | solution.py:358
  116.6 11.4 %collective-permute-start.33 = (bf16[128,128]{1,0:T(8,128)(2,1)}, bf16[128,128]{1,0:T(8,128)(2,1)S(1)}, u32[]{:S(2)}, u32[]{:S(2)}) collective-permute-start(bf16[128,128]{1,0:T(8,128)(2,1)} %get-tuple-element.61), channel_id=1, source_target_pairs={{0,4},{4,0},{8,12},{12,8},{1,5},{5,1},{9,13},{13,9},{2,6},{6,2},{1... | collective-permute-start | bytes 98312 | tf_op jit(solution)/shard_map/ppermute | solution.py:362
  124.0 19.6 %collective-permute-start.31 = (bf16[128,2880]{0,1:T(8,128)(2,1)}, bf16[128,2880]{0,1:T(8,128)(2,1)}, u32[]{:S(2)}, u32[]{:S(2)}) collective-permute-start(bf16[128,2880]{0,1:T(8,128)(2,1)} %copy.13), channel_id=1, source_target_pairs={{0,8},{8,0},{1,9},{9,1},{2,10},{10,2},{3,11},{11,3},{4,12},{12,4},... | collective-permute-start | bytes 2211848 | tf_op jit(solution)/shard_map/ppermute | solution.py:358
  128.0 38.8 %collective-permute-start.30 = (bf16[128,2880]{0,1:T(8,128)(2,1)}, bf16[128,2880]{0,1:T(8,128)(2,1)}, u32[]{:S(2)}, u32[]{:S(2)}) collective-permute-start(bf16[128,2880]{0,1:T(8,128)(2,1)} %copy.13), channel_id=1, source_target_pairs={{0,4},{4,0},{1,5},{5,1},{2,6},{6,2},{3,7},{7,3},{8,12},{12,8},{9,1... | collective-permute-start | bytes 2211848 | tf_op jit(solution)/shard_map/ppermute | solution.py:358
  128.1 30.7 %collective-permute-start.28 = (bf16[128,2880]{0,1:T(8,128)(2,1)}, bf16[128,2880]{0,1:T(8,128)(2,1)}, u32[]{:S(2)}, u32[]{:S(2)}) collective-permute-start(bf16[128,2880]{0,1:T(8,128)(2,1)} %copy.11), channel_id=1, source_target_pairs={{0,8},{8,0},{1,9},{9,1},{2,10},{10,2},{3,11},{11,3},{4,12},{12,4},... | collective-permute-start | bytes 2211848 | tf_op jit(solution)/shard_map/ppermute | solution.py:358
  128.4 40.6 %collective-permute-start.27 = (bf16[128,2880]{0,1:T(8,128)(2,1)}, bf16[128,2880]{0,1:T(8,128)(2,1)}, u32[]{:S(2)}, u32[]{:S(2)}) collective-permute-start(bf16[128,2880]{0,1:T(8,128)(2,1)} %copy.11), channel_id=1, source_target_pairs={{0,4},{4,0},{1,5},{5,1},{2,6},{6,2},{3,7},{7,3},{8,12},{12,8},{9,1... | collective-permute-start | bytes 2211848 | tf_op jit(solution)/shard_map/ppermute | solution.py:358
  130.5 12.0 %collective-permute-start.36 = (bf16[4,16,2880]{2,1,0:T(8,128)(2,1)S(1)}, bf16[4,16,2880]{2,1,0:T(8,128)(2,1)S(1)}, u32[]{:S(2)}, u32[]{:S(2)}) collective-permute-start(bf16[4,16,2880]{2,1,0:T(8,128)(2,1)S(1)} %get-tuple-element.65), channel_id=1, source_target_pairs={{0,16},{16,0},{1,17},{17,1},{2,18},{18,2},{3,19},{19,3},{4,20},{20... | collective-permute-start | bytes 1105928 | tf_op jit(solution)/shard_map/ppermute | solution.py:358
  142.5 28.9 %collective-permute-start.44 = (bf16[16,2880]{1,0:T(8,128)(2,1)S(1)}, bf16[16,2880]{1,0:T(8,128)(2,1)S(1)}, u32[]{:S(2)}, u32[]{:S(2)}) collective-permute-start(bf16[16,2880]{1,0:T(8,128)(2,1)S(1)} %get-tuple-element.76), channel_id=1, source_target_pairs={{0,1},{1,0},{2,3},{3,2},{4,5},{5,4},{6,7},{7,6},{8,9},{9,8},{10,11... | collective-permute-start | bytes 276488 | tf_op jit(solution)/shard_map/ppermute | solution.py:358
  143.7 31.3 %collective-permute-start.45 = (bf16[16,2880]{1,0:T(8,128)(2,1)S(1)}, bf16[16,2880]{1,0:T(8,128)(2,1)S(1)}, u32[]{:S(2)}, u32[]{:S(2)}) collective-permute-start(bf16[16,2880]{1,0:T(8,128)(2,1)S(1)} %get-tuple-element.78), channel_id=1, source_target_pairs={{0,2},{1,3},{2,0},{3,1},{4,6},{5,7},{6,4},{7,5},{8,10},{9,11},{10,... | collective-permute-start | bytes 276488 | tf_op jit(solution)/shard_map/ppermute | solution.py:358
  158.8 16.2 %collective-permute-start.46 = (bf16[16,2880]{1,0:T(8,128)(2,1)S(1)}, bf16[16,2880]{1,0:T(8,128)(2,1)S(1)}, u32[]{:S(2)}, u32[]{:S(2)}) collective-permute-start(bf16[16,2880]{1,0:T(8,128)(2,1)S(1)} %get-tuple-element.77), channel_id=1, source_target_pairs={{0,3},{1,2},{2,1},{3,0},{4,7},{5,6},{6,5},{7,4},{8,11},{9,10},{10,... | collective-permute-start | bytes 276488 | tf_op jit(solution)/shard_map/ppermute | solution.py:358
  166.8 10.5 %collective-permute-start.37 = (bf16[16,2880]{1,0:T(8,128)(2,1)S(1)}, bf16[16,2880]{1,0:T(8,128)(2,1)S(1)}, u32[]{:S(2)}, u32[]{:S(2)}) collective-permute-start(bf16[16,2880]{1,0:T(8,128)(2,1)S(1)} %get-tuple-element.79), channel_id=1, source_target_pairs={{0,1},{1,0},{2,3},{3,2},{4,5},{5,4},{6,7},{7,6},{8,9},{9,8},{10,11... | collective-permute-start | bytes 276488 | tf_op jit(solution)/shard_map/ppermute | solution.py:358
  169.1 10.0 %collective-permute-start.38 = (bf16[16,2880]{1,0:T(8,128)(2,1)S(1)}, bf16[16,2880]{1,0:T(8,128)(2,1)S(1)}, u32[]{:S(2)}, u32[]{:S(2)}) collective-permute-start(bf16[16,2880]{1,0:T(8,128)(2,1)S(1)} %get-tuple-element.81), channel_id=1, source_target_pairs={{0,2},{1,3},{2,0},{3,1},{4,6},{5,7},{6,4},{7,5},{8,10},{9,11},{10,... | collective-permute-start | bytes 276488 | tf_op jit(solution)/shard_map/ppermute | solution.py:358
  (42 other events, 257.3 us)

commit v2 on v1

--- a/solution.py
+++ b/solution.py
@@ -199,17 +199,28 @@
     )(queries, grad_out, keys, halo, values, value_halo, probs, diag)
 
 
+def ring_source(z, steps, size):
+    at = (z ^ (z >> 1)) + size - steps
+    at = jnp.where(at >= size, at - size, at)
+    return at ^ (at >> 1)
+
+
 def project_kernel(place_ref, *refs):
     pieces, hidden = refs[:8], refs[8:12]
     weight_ref, outs = refs[12], refs[13:]
     hi, z = place_ref[0], place_ref[1]
-    step = pieces[0].shape[0]
     depth = len(pieces) // 2
+    step = pieces[0].shape[0] // 2
+    size = pieces[0].shape[1]
+    half = weight_ref.shape[0] // 2
     for r in range(2):
         for k in range(depth):
-            row = ((hi ^ r) * depth + (z ^ k)) * step
-            weight_ref[pl.ds(pl.multiple_of(row, step), step), :] = pieces[r * depth + k][...]
-    weight = weight_ref[...]
+            row = ((hi ^ r) * depth + ring_source(z, k, depth)) * step
+            for kind in range(2):
+                weight_ref[pl.ds(pl.multiple_of(kind * half + row, step), step), :size] = pieces[
+                    r * depth + k
+                ][kind * step : (kind + 1) * step, :]
+    weight = weight_ref[:, :size]
     for h_ref, out_ref in zip(hidden, outs):
         across = jnp.dot(weight, h_ref[...], preferred_element_type=F32)
         out_ref[...] = across.T.astype(BF16)
@@ -218,7 +229,7 @@
 def project(place, pieces, hidden):
     depth, tokens = hidden[0].shape
     cols = sum(p.shape[0] for p in pieces)
-    weight = struct((cols, depth), BF16)
+    weight = struct((cols, -(-depth // LANES) * LANES), BF16)
     out = struct((tokens, cols), BF16)
     return pl.pallas_call(
         project_kernel,
@@ -232,18 +243,21 @@
 
 
 def arrange_kernel(place_ref, *refs):
-    out_ref = refs[-1]
-    for r, ref in enumerate(refs[:-1]):
-        out_ref[place_ref[2] ^ r] = ref[...]
+    key_ref, value_ref = refs[-2:]
+    for r, ref in enumerate(refs[:-2]):
+        key_ref[place_ref[2] ^ r] = ref[:, :LANES]
+        value_ref[place_ref[2] ^ r] = ref[:, LANES:]
 
 
 def arrange(place, parts):
+    out = struct((len(parts), parts[0].shape[0], LANES), BF16)
     return pl.pallas_call(
         arrange_kernel,
         in_specs=[SMEM] + [VMEM] * len(parts),
-        out_specs=VMEM,
-        out_shape=struct((len(parts),) + parts[0].shape, BF16),
-        compiler_params=params(),
+        out_specs=[VMEM] * 2,
+        out_shape=[out] * 2,
+        compiler_params=params(),
+        cost_estimate=cost(0, out, out),
         name="arrange",
     )(place, *parts)
 
@@ -262,30 +276,35 @@
     return blocks
 
 
-def finish_kernel(place_ref, own_ref, back_ref, natural_ref, all_ref, *outs):
-    quarters = []
-    for q in range(QUARTERS):
-        total = (own_ref[q] + back_ref[q].astype(F32)).astype(BF16)
-        all_ref[q] = total
-        quarters.append(total.astype(F32))
-    for m, block in enumerate(natural(quarters)):
-        natural_ref[:, m * LANES : (m + 1) * LANES] = block.astype(BF16)
-    for r, ref in enumerate(outs):
-        ref[...] = all_ref[place_ref[2] ^ r]
-
-
-def finish(place, own, back):
-    rows = own.shape[1]
-    part = struct(own.shape[1:], BF16)
+def finish_kernel(place_ref, *refs):
+    sums, naturals, alls, outs = refs[:4], refs[4:6], refs[6:8], refs[8:]
+    for kind in range(2):
+        own_ref, back_ref = sums[2 * kind : 2 * kind + 2]
+        quarters = []
+        for q in range(QUARTERS):
+            total = (own_ref[q] + back_ref[q].astype(F32)).astype(BF16)
+            alls[kind][q] = total
+            quarters.append(total.astype(F32))
+        for m, block in enumerate(natural(quarters)):
+            naturals[kind][:, m * LANES : (m + 1) * LANES] = block.astype(BF16)
+        for r, ref in enumerate(outs):
+            ref[:, kind * LANES : (kind + 1) * LANES] = alls[kind][place_ref[2] ^ r]
+
+
+def finish(place, key_own, key_back, value_own, value_back):
+    rows = key_own.shape[1]
+    wide = struct((rows, QUARTERS * LANES), BF16)
+    every = struct(key_own.shape, BF16)
+    part = struct((rows, 2 * LANES), BF16)
     return pl.pallas_call(
         finish_kernel,
-        in_specs=[SMEM, VMEM, VMEM],
-        out_specs=[VMEM] * (2 + QUARTERS),
-        out_shape=[struct((rows, QUARTERS * LANES), BF16), struct(own.shape, BF16)]
-        + [part] * QUARTERS,
-        compiler_params=params(),
+        in_specs=[SMEM] + [VMEM] * 4,
+        out_specs=[VMEM] * (4 + QUARTERS),
+        out_shape=[wide, wide, every, every] + [part] * QUARTERS,
+        compiler_params=params(),
+        cost_estimate=cost(0, key_own, key_own),
         name="finish",
-    )(place, own, back)
+    )(place, key_own, key_back, value_own, value_back)
 
 
 def spans(size, step):
@@ -294,64 +313,77 @@
 
 def weight_grad_kernel(place_ref, *refs):
     grads, hidden = refs[:4], refs[4:8]
-    keep_ref, send_ref, wide_ref = refs[8:]
+    outs, wide_ref = refs[8:-1], refs[-1]
     hi, z = place_ref[0], place_ref[1]
     for at, size in spans(hidden[0].shape[0], 256):
         total = jnp.zeros((size, grads[0].shape[1]), F32)
         for g_ref, h_ref in zip(grads, hidden):
             total += jnp.dot(h_ref[at : at + size, :], g_ref[...], preferred_element_type=F32)
         wide_ref[:, at : at + size] = total.T
-    depth, step = keep_ref.shape[:2]
-    for k in range(depth):
-        for r, ref in enumerate((keep_ref, send_ref)):
+    depth = len(outs) // 2
+    step = outs[0].shape[0] // 2
+    half = wide_ref.shape[0] // 2
+    for r in range(2):
+        for k in range(depth):
             row = ((hi ^ r) * depth + (z ^ k)) * step
-            ref[k] = wide_ref[pl.ds(pl.multiple_of(row, step), step), :].astype(BF16)
+            for kind in range(2):
+                at = pl.multiple_of(kind * half + row, step)
+                outs[r * depth + k][kind * step : (kind + 1) * step, :] = wide_ref[
+                    pl.ds(at, step), :
+                ].astype(BF16)
 
 
 def weight_grad(place, grads, hidden, depth):
     size, tokens = hidden[0].shape
     cols = grads[0].shape[1]
-    part = struct((depth, cols // (2 * depth), size), BF16)
+    part = struct((cols // (2 * depth), size), BF16)
     return pl.pallas_call(
         weight_grad_kernel,
         in_specs=[SMEM] + [VMEM] * 8,
-        out_specs=[VMEM] * 2,
-        out_shape=[part] * 2,
+        out_specs=[VMEM] * (2 * depth),
+        out_shape=[part] * (2 * depth),
         scratch_shapes=[pltpu.VMEM((cols, size), F32)],
         compiler_params=params(),
-        cost_estimate=cost(2 * 4 * tokens * cols * size, *hidden, part, part),
+        cost_estimate=cost(2 * 4 * tokens * cols * size, *hidden, *hidden),
         name="weight_grad",
     )(place, *grads, *hidden)
 
 
 def input_grad_kernel(place_ref, key_ref, value_ref, *refs):
     out_ref = refs[-1]
-    weights = (refs[:QUARTERS], refs[QUARTERS:-1])
-    for at, size in spans(out_ref.shape[0], 256):
-        total = jnp.zeros((key_ref.shape[1], size), F32)
-        for grad_ref, group in zip((key_ref, value_ref), weights):
-            for r, w_ref in enumerate(group):
-                total += jnp.dot(
-                    grad_ref[place_ref[2] ^ r],
-                    w_ref[:, at : at + size],
-                    preferred_element_type=F32,
-                )
-        out_ref[at : at + size, :] = total.T.astype(BF16)
-
-
-def input_grad(place, key_all, value_all, key_weights, value_weights):
-    cols, size = key_weights[0].shape
+    total = jnp.zeros((key_ref.shape[1], out_ref.shape[0]), F32)
+    for r, w_ref in enumerate(refs[:-1]):
+        half = w_ref.shape[0] // 2
+        for kind, grad_ref in enumerate((key_ref, value_ref)):
+            total += jnp.dot(
+                grad_ref[place_ref[2] ^ r],
+                w_ref[kind * half : (kind + 1) * half, :],
+                preferred_element_type=F32,
+            )
+    out_ref[...] = total.T.astype(BF16)
+
+
+def input_grad(place, key_all, value_all, weights, size):
+    cols, wide = weights[0].shape
     rows = key_all.shape[1]
+    step = 512
     out = struct((size, rows), BF16)
+    whole = pl.BlockSpec(key_all.shape, lambda i: (0, 0, 0))
     return pl.pallas_call(
         input_grad_kernel,
-        in_specs=[SMEM] + [VMEM] * 10,
-        out_specs=VMEM,
+        grid=(-(-size // step),),
+        in_specs=[SMEM, whole, whole]
+        + [pl.BlockSpec((cols, step), lambda i: (0, i))] * len(weights),
+        out_specs=pl.BlockSpec((step, rows), lambda i: (i, 0)),
         out_shape=out,
         compiler_params=params(),
-        cost_estimate=cost(16 * rows * cols * size, *key_weights, *value_weights, out),
+        cost_estimate=cost(8 * rows * cols * size, *weights, out),
         name="input_grad",
-    )(place, key_all, value_all, *key_weights, *value_weights)
+    )(place, key_all, value_all, *weights)
+
+
+def after(array, *others):
+    return lax.optimization_barrier((array, *others))[0]
 
 
 def flip(array, axis, by):
@@ -360,6 +392,12 @@
 
 def flip_group(array, by):
     return lax.ppermute(array, ("x", "c"), [(i, i ^ by) for i in range(QUARTERS)])
+
+
+def round_ring(array):
+    size = lax.axis_size("z")
+    order = [i ^ (i >> 1) for i in range(size)]
+    return lax.ppermute(array, "z", [(order[i], order[(i + 1) % size]) for i in range(size)])
 
 
 def shifted(array, by):
@@ -368,69 +406,66 @@
     return lax.ppermute(array, AXES, pairs)
 
 
-def gathered(weight):
+def exchanged(parts):
+    return [parts[0]] + [flip_group(parts[r], r) for r in range(1, QUARTERS)]
+
+
+def fast_shards(hidden_in, queries, grad_out, key_weight, value_weight):
+    size = hidden_in.shape[1]
     depth = lax.axis_size("z")
-    mine = [weight] + [flip(weight, "z", k) for k in range(1, depth)]
-    return mine + [flip(piece, "hi", 1) for piece in mine]
-
-
-def scattered(keep, send):
-    got = flip(send, "hi", 1)
-    total = keep.astype(F32) + got.astype(F32)
-    depth = total.shape[0]
-    result = total[0]
-    for k in range(1, depth):
-        result = result + flip(total[k].astype(BF16), "z", k).astype(F32)
-    return result
-
-
-def fast_shards(hidden_in, queries, grad_out, key_weight, value_weight):
-    here = lax.axis_index(AXES)
     group = lax.axis_index(("x", "c"))
     place = jnp.stack([lax.axis_index("hi"), lax.axis_index("z"), group]).astype(jnp.int32)
-    first = (here == 0).astype(jnp.int32).reshape(1)
+    first = (lax.axis_index(AXES) == 0).astype(jnp.int32).reshape(1)
     own = hidden_in.T
-    across = flip(own, "x", 1)
-    hidden = [own, flip(own, "c", 1), across, flip(across, "c", 1)]
-    depth = lax.axis_size("z")
-    key_pieces = gathered(key_weight.T)
-    value_pieces = gathered(value_weight.T)
-
-    def projected(pieces):
-        weight, *parts = project(place, pieces, hidden)
-        parts = [parts[0]] + [flip_group(parts[r], r) for r in range(1, QUARTERS)]
-        rows = arrange(place, parts)
-        return weight, rows, shifted(rows, 1)
-
-    key_mine, keys, key_halo = projected(key_pieces)
-    value_mine, values, value_halo = projected(value_pieces)
-
-    def filled(mine):
-        x_side = flip(mine, "x", 1)
-        return [mine, flip(mine, "c", 1), x_side, flip(x_side, "c", 1)]
-
-    key_weights, value_weights = filled(key_mine), filled(value_mine)
+    x_side = flip(own, "x", 1)
+    pieces = [jnp.concatenate([key_weight.T, value_weight.T], axis=0)]
+    across = [flip(pieces[0], "hi", 1)]
+    for k in range(1, depth):
+        held = pieces[-1] if k < 3 else after(pieces[-1], across[k - 3])
+        pieces.append(round_ring(held))
+        across.append(flip(pieces[-1], "hi", 1))
+    x_side = after(x_side, pieces[-1], across[depth - 2])
+    hidden = [own, flip(own, "c", 1), x_side, flip(x_side, "c", 1)]
+    mine, *parts = project(place, pieces + across, hidden)
+    parts = exchanged(parts)
+    keys, values = arrange(place, parts)
+    key_halo, value_halo = shifted(keys, 1), shifted(values, 1)
+
+    filled = after(mine, keys)
+    x_filled = flip(filled, "x", 1)
+    c_filled = flip(filled, "c", 1)
     probs, diag, value_own, value_back = softmax_part(first, queries, grad_out, keys, key_halo)
-
-    def finished(sums, back):
-        rows, every, *parts = finish(place, sums, shifted(back, -1))
-        parts = [parts[0]] + [flip_group(parts[r], r) for r in range(1, QUARTERS)]
-        return rows, every, scattered(*weight_grad(place, parts, hidden, depth))
-
-    grad_values, value_every, value_total = finished(value_own, value_back)
+    value_back = shifted(value_back, -1)
     grad_queries, key_own, key_back = scores_part(
         queries, grad_out, keys, key_halo, values, value_halo, probs, diag
     )
-    grad_keys, key_every, key_total = finished(key_own, key_back)
-    grad_inputs = input_grad(place, key_every, value_every, key_weights, value_weights).T
+    grad_keys, grad_values, key_every, value_every, *parts = finish(
+        place, key_own, shifted(key_back, -1), value_own, value_back
+    )
+    parts = [after(part, x_filled, c_filled) for part in parts]
+    weights = [mine, c_filled, x_filled, flip(x_filled, "c", 1)]
+    grads = weight_grad(place, exchanged(parts), hidden, depth)
+    keep, send = grads[:depth], grads[depth:]
+    came = [None] * depth
+    total = None
+    for k in reversed(range(depth)):
+        came[k] = flip(send[k], "hi", 1)
+        sum_k = keep[k].astype(F32) + came[k].astype(F32)
+        if k:
+            sum_k = flip(sum_k.astype(BF16), "z", k).astype(F32)
+        total = sum_k if total is None else total + sum_k
+    key_every = after(key_every, came[depth - 2])
+    grad_inputs = input_grad(place, key_every, value_every, weights, size).T
     scale = (hidden_in.shape[0] * lax.axis_size(AXES)) ** (-0.5)
+    total = total * scale
+    rows = total.shape[0] // 2
     return (
         grad_queries,
         grad_keys,
         grad_values,
         grad_inputs,
-        (key_total * scale).T,
-        (value_total * scale).T,
+        total[:rows].T,
+        total[rows:].T,
     )
 
 
@@ -488,7 +523,7 @@
     outer, inner = mesh.shape["seqa"], mesh.shape["seqb"]
     split = Mesh(mesh.devices.reshape(outer // QUARTERS, 2, 2, inner), AXES)
     cols = KV_HEADS * HEAD // (outer * inner)
-    fast = outer == 2 * QUARTERS and inner & (inner - 1) == 0 and cols % SUBLANES == 0
+    fast = outer == 2 * QUARTERS and inner == 4 and cols % SUBLANES == 0
     rows, columns = P(AXES, None), P(None, AXES)
     return jax.shard_map(
         fast_shards if fast else plain_shards,

time: 195 us -> 137 us (0.70)
  starting transfers between devices: 61.1 us -> 36.4 us
  local copies, waits for them, and re-layouts: 28.8 us -> 6.27 us
  other arithmetic: 6.43 us -> 1.31 us
  waiting for transfers between devices: 61.8 us -> 57.3 us
    ppermute x31 -> x17, waiting for transfers between devices: 53.1 us -> 27.1 us  [flip(): lax.ppermute(array, axis, [(i, i ^ by) for i in range(lax.axis_size(axis))])]
    ppermute x31 -> x17, starting transfers between devices: 39.2 us -> 18.4 us  [flip(): lax.ppermute(array, axis, [(i, i ^ by) for i in range(lax.axis_size(axis))])]
    ppermute x0 -> x3, waiting for transfers between devices: none -> 13.3 us  [round_ring(): lax.ppermute(array, 'z', [(order[i], order[(i + 1) % size]) for i in rang...]
    ppermute x6 -> x0, local copies, waits for them, and re-layouts: 12.8 us -> none  [flip(): lax.ppermute(array, axis, [(i, i ^ by) for i in range(lax.axis_size(axis))])]
    ppermute x12 -> x6, starting transfers between devices: 13.7 us -> 5.22 us  [flip_group(): lax.ppermute(array, ('x', 'c'), [(i, i ^ by) for i in range(QUARTERS)])]
    unnamed x38 -> x20, local copies, waits for them, and re-layouts: 11.4 us -> 5.51 us
    pallas_call x2 -> x0, local copies, waits for them, and re-layouts: 4.57 us -> none  [project(): pl.pallas_call(project_kernel, in_specs=[SMEM] + [VMEM] * (len(pieces) +...]
    ppermute x12 -> x6, waiting for transfers between devices: 3.29 us -> 7.57 us  [flip_group(): lax.ppermute(array, ('x', 'c'), [(i, i ^ by) for i in range(QUARTERS)])]
  transfers between devices with their start and end apart: 47 -> 30, of which waited for: 16 -> 16; matrix products, arithmetic and copies ran while one was open for 11% -> 2% of each run, Pallas kernels for 15% -> 15%
where the time goes in v2:
time: 137 us; the launch traced here: 136 us
  waiting for transfers between devices  57.3 us (42%)
  starting transfers between devices  36.4 us (27%)
  Pallas kernels  34.1 us (25%)
  local copies, waits for them, and re-layouts  6.27 us (5%)
    ppermute x17, waiting for transfers between devices, flip(): lax.ppermute(array, axis, [(i, i ^ by) for i in range(lax.axis_size(axis))])  27.1 us
    ppermute x17, starting transfers between devices, flip(): lax.ppermute(array, axis, [(i, i ^ by) for i in range(lax.axis_size(axis))])  18.4 us
    ppermute x3, waiting for transfers between devices, round_ring(): lax.ppermute(array, 'z', [(order[i], order[(i + 1) % size]) for i in rang...  13.3 us
    pallas_call x1, Pallas kernels, scores_part(): pl.pallas_call(scores_kernel, grid=(QUARTERS, 2), in_specs=[by_head(queri...  11.9 us
    ppermute x4, starting transfers between devices, shifted(): return lax.ppermute(array, AXES, pairs)  9.55 us
    ppermute x4, waiting for transfers between devices, shifted(): return lax.ppermute(array, AXES, pairs)  9.36 us
    ppermute x6, waiting for transfers between devices, flip_group(): lax.ppermute(array, ('x', 'c'), [(i, i ^ by) for i in range(QUARTERS)])  7.57 us
    pallas_call x1, Pallas kernels, softmax_part(): pl.pallas_call(softmax_kernel, grid=(QUARTERS, 2), in_specs=[SMEM] + [by_...  7.08 us
  transfers between devices with their start and end apart: 30, of which 16 were waited for; matrix products, arithmetic and copies ran while one was open for 2% of the time, Pallas kernels for 15%

profile of v2, /device:TPU:0, one launch (start us, length us, event | category | flops | bytes accessed | tf_op | source)
XLA Modules:
  0.0 136.2 jit_solution(3721362414834382678)
XLA Ops:
  0.6 3.0 %collective-permute-start.8 = (bf16[2880,128]{1,0:T(8,128)(2,1)}, bf16[2880,128]{1,0:T(8,128)(2,1)S(1)}, u32[]{:S(2)}, u32[]{:S(2)}) collective-permute-start(bf16[2880,128]{1,0:T(8,128)(2,1)} %bitcast.12), channel_id=1, source_target_pairs={{0,8},{8,0},{1,9},{9,1},{2,10},{10,2},{3,11},{11,3},{4,12},{12,4},... | collective-permute-start | bytes 2211848 | tf_op jit(solution)/shard_map/ppermute | solution.py:390
  7.7 4.0 %collective-permute-done.refs_1_ = bf16[32,2880]{1,0:T(8,128)(2,1)S(1)} collective-permute-done((bf16[32,2880]{1,0:T(8,128)(2,1)S(1)}, bf16[32,2880]{1,0:T(8,128)(2,1)S(1)}, u32[]{:S(2)}, u32[]{:S(2)}) %collective-permute-start) | collective-permute-done | bytes 184352 | tf_op jit(solution)/shard_map/ppermute | solution.py:400
  12.5 5.7 %collective-permute-done.1.refs_2_ = bf16[32,2880]{1,0:T(8,128)(2,1)S(1)} collective-permute-done((bf16[32,2880]{1,0:T(8,128)(2,1)S(1)}, bf16[32,2880]{1,0:T(8,128)(2,1)S(1)}, u32[]{:S(2)}, u32[]{:S(2)}) %collective-permute-start.1) | collective-permute-done | bytes 184352 | tf_op jit(solution)/shard_map/ppermute | solution.py:400
  21.2 3.6 %collective-permute-done.3.refs_3_ = bf16[32,2880]{1,0:T(8,128)(2,1)} collective-permute-done((bf16[32,2880]{1,0:T(8,128)(2,1)S(1)}, bf16[32,2880]{1,0:T(8,128)(2,1)}, u32[]{:S(2)}, u32[]{:S(2)}) %collective-permute-start.3) | collective-permute-done | bytes 184352 | tf_op jit(solution)/shard_map/ppermute | solution.py:400
  27.6 5.5 %collective-permute-done.4.refs_5_ = bf16[32,2880]{1,0:T(8,128)(2,1)} collective-permute-done((bf16[32,2880]{1,0:T(8,128)(2,1)S(1)}, bf16[32,2880]{1,0:T(8,128)(2,1)}, u32[]{:S(2)}, u32[]{:S(2)}) %collective-permute-start.4) | collective-permute-done | bytes 184352 | tf_op jit(solution)/shard_map/ppermute | solution.py:390
  33.1 3.7 %collective-permute-done.6.refs_7_ = bf16[32,2880]{1,0:T(8,128)(2,1)} collective-permute-done((bf16[32,2880]{1,0:T(8,128)(2,1)}, bf16[32,2880]{1,0:T(8,128)(2,1)}, u32[]{:S(2)}, u32[]{:S(2)}) %collective-permute-start.6) | collective-permute-done | bytes 184352 | tf_op jit(solution)/shard_map/ppermute | solution.py:390
  39.7 3.5 %project.1 = (bf16[256,2944]{1,0:T(8,128)(2,1)}, bf16[128,256]{1,0:T(8,128)(2,1)S(1)}, bf16[128,256]{1,0:T(8,128)(2,1)S(1)}, bf16[128,256]{1,0:T(8,128)(2,1)S(1)}, bf16[128,256]{1,0:T(8,128)(2,1)S(1)}) custom-call(s32[3]{0:T(128)S(1)} %pad_add_fusion.place_ref, bf16[32,2880]{1,0:T(8,128)(2,1)S(1)} %pad_maximum_fusion.refs_0_, ...), custom_call_target="tpu_custom_call" | custom-call | flops 754974720 | bytes 5963776 | tf_op jit(solution)/shard_map/project/pallas_call | solution.py:234
  45.2 3.1 %collective-permute-done.11.refs_2_ = bf16[128,256]{1,0:T(8,128)(2,1)S(1)} collective-permute-done((bf16[128,256]{1,0:T(8,128)(2,1)S(1)}, bf16[128,256]{1,0:T(8,128)(2,1)S(1)}, u32[]{:S(2)}, u32[]{:S(2)}) %collective-permute-start.11) | collective-permute-done | bytes 65568 | tf_op jit(solution)/shard_map/ppermute | solution.py:394
  50.1 5.1 %collective-permute-start.13 = (bf16[4,128,128]{2,1,0:T(8,128)(2,1)S(1)}, bf16[4,128,128]{2,1,0:T(8,128)(2,1)S(1)}, u32[]{:S(2)}, u32[]{:S(2)}) collective-permute-start(bf16[4,128,128]{2,1,0:T(8,128)(2,1)S(1)} %get-tuple-element.50.key_ref), channel_id=1, source_target_pairs={{0,1},{1,2},{2,3},{3,4},{4,5},{5,6},{6,7},{7,8},{8,9},{9,10},{10,1... | collective-permute-start | bytes 393224 | tf_op jit(solution)/shard_map/ppermute | solution.py:406
  55.2 1.9 %collective-permute-start.14 = (bf16[4,128,128]{2,1,0:T(8,128)(2,1)S(1)}, bf16[4,128,128]{2,1,0:T(8,128)(2,1)S(1)}, u32[]{:S(2)}, u32[]{:S(2)}) collective-permute-start(bf16[4,128,128]{2,1,0:T(8,128)(2,1)S(1)} %get-tuple-element.51.value_ref), channel_id=1, source_target_pairs={{0,1},{1,2},{2,3},{3,4},{4,5},{5,6},{6,7},{7,8},{8,9},{9,10},{10,1... | collective-permute-start | bytes 393224 | tf_op jit(solution)/shard_map/ppermute | solution.py:406
  59.0 7.1 %softmax_part.1 = (bf16[8,8,128,128]{3,2,1,0:T(8,128)(2,1)S(1)}, f32[8,8,128]{2,1,0:T(8,128)S(1)}, f32[4,128,128]{2,1,0:T(8,128)S(1)}, bf16[4,128,128]{2,1,0:T(8,128)(2,1)S(1)}) custom-call(s32[1]{0:T(128)} %bitcast.6.first_ref, bf16[128,4096]{1,0:T(8,128)(2,1)S(1)} %copy-done, bf16[128,4096]{1,0:T(8,128)(2,1)S(1)} %copy-done.1, ...), custom_call_target="tpu_custom_call" | custom-call | flops 536870912 | bytes 4194304 | tf_op jit(solution)/shard_map/softmax_part/pallas_call | solution.py:172
  66.1 11.9 %scores_part.1 = (bf16[128,4096]{1,0:T(8,128)(2,1)}, f32[4,128,128]{2,1,0:T(8,128)S(1)}, bf16[4,128,128]{2,1,0:T(8,128)(2,1)S(1)}) custom-call(bf16[128,4096]{1,0:T(8,128)(2,1)S(1)} %copy-done, bf16[128,4096]{1,0:T(8,128)(2,1)S(1)} %copy-done.1, bf16[4,128,128]{2,1,0:T(8,128)(2,1)S(1)} %get-tuple-element.50.key_ref, ...), custom_call_target="tpu_custom_call" | custom-call | flops 805306368 | bytes 5242880 | tf_op jit(solution)/shard_map/scores_part/pallas_call | solution.py:188
  80.6 5.7 %collective-permute-done.15.refs_1_ = bf16[4,128,128]{2,1,0:T(8,128)(2,1)S(1)} collective-permute-done((bf16[4,128,128]{2,1,0:T(8,128)(2,1)S(1)}, bf16[4,128,128]{2,1,0:T(8,128)(2,1)S(1)}, u32[]{:S(2)}, u32[]{:S(2)}) %collective-permute-start.15) | collective-permute-done | bytes 131104 | tf_op jit(solution)/shard_map/ppermute | solution.py:406
  90.4 2.3 %collective-permute-start.20 = (bf16[128,256]{1,0:T(8,128)(2,1)S(1)}, bf16[128,256]{1,0:T(8,128)(2,1)S(1)}, u32[]{:S(2)}, u32[]{:S(2)}) collective-permute-start(bf16[128,256]{1,0:T(8,128)(2,1)S(1)} %get-tuple-element.69), channel_id=1, source_target_pairs={{0,8},{4,12},{8,0},{12,4},{1,9},{5,13},{9,1},{13,5},{2,10},{6,14},... | collective-permute-start | bytes 196616 | tf_op jit(solution)/shard_map/ppermute | solution.py:394
  92.8 2.6 %collective-permute-done.20.refs_2_ = bf16[128,256]{1,0:T(8,128)(2,1)S(1)} collective-permute-done((bf16[128,256]{1,0:T(8,128)(2,1)S(1)}, bf16[128,256]{1,0:T(8,128)(2,1)S(1)}, u32[]{:S(2)}, u32[]{:S(2)}) %collective-permute-start.20) | collective-permute-done | bytes 65568 | tf_op jit(solution)/shard_map/ppermute | solution.py:394
  96.8 3.3 %weight_grad.1 = (bf16[32,2880]{1,0:T(8,128)(2,1)S(1)}, bf16[32,2880]{1,0:T(8,128)(2,1)S(1)}, bf16[32,2880]{1,0:T(8,128)(2,1)S(1)}, bf16[32,2880]{1,0:T(8,128)(2...) custom-call(s32[3]{0:T(128)S(1)} %pad_add_fusion.place_ref, ...), custom_call_target="tpu_custom_call" | custom-call | flops 754974720 | bytes 5898240 | tf_op jit(solution)/shard_map/weight_grad/pallas_call | solution.py:340
  100.1 2.3 %collective-permute-start.27 = (bf16[32,2880]{1,0:T(8,128)(2,1)S(1)}, bf16[32,2880]{1,0:T(8,128)(2,1)S(1)}, u32[]{:S(2)}, u32[]{:S(2)}) collective-permute-start(bf16[32,2880]{1,0:T(8,128)(2,1)S(1)} %get-tuple-element.79), channel_id=1, source_target_pairs={{0,16},{16,0},{1,17},{17,1},{2,18},{18,2},{3,19},{19,3},{4,20},{20... | collective-permute-start | bytes 552968 | tf_op jit(solution)/shard_map/ppermute | solution.py:390
  102.4 1.9 %collective-permute-start.29 = (bf16[32,2880]{1,0:T(8,128)(2,1)S(1)}, bf16[32,2880]{1,0:T(8,128)(2,1)S(1)}, u32[]{:S(2)}, u32[]{:S(2)}) collective-permute-start(bf16[32,2880]{1,0:T(8,128)(2,1)S(1)} %get-tuple-element.81), channel_id=1, source_target_pairs={{0,16},{16,0},{1,17},{17,1},{2,18},{18,2},{3,19},{19,3},{4,20},{20... | collective-permute-start | bytes 552968 | tf_op jit(solution)/shard_map/ppermute | solution.py:390
  104.5 3.4 %collective-permute-done.27 = bf16[32,2880]{1,0:T(8,128)(2,1)S(1)} collective-permute-done((bf16[32,2880]{1,0:T(8,128)(2,1)S(1)}, bf16[32,2880]{1,0:T(8,128)(2,1)S(1)}, u32[]{:S(2)}, u32[]{:S(2)}) %collective-permute-start.27) | collective-permute-done | bytes 184352 | tf_op jit(solution)/shard_map/ppermute | solution.py:390
  108.3 3.6 %collective-permute-done.22 = bf16[32,2880]{1,0:T(8,128)(2,1)S(1)} collective-permute-done((bf16[32,2880]{1,0:T(8,128)(2,1)S(1)}, bf16[32,2880]{1,0:T(8,128)(2,1)S(1)}, u32[]{:S(2)}, u32[]{:S(2)}) %collective-permute-start.22) | collective-permute-done | bytes 184352 | tf_op jit(solution)/shard_map/ppermute | solution.py:390
  112.9 6.5 %collective-permute-done.24 = bf16[32,2880]{1,0:T(8,128)(2,1)S(1)} collective-permute-done((bf16[32,2880]{1,0:T(8,128)(2,1)S(1)}, bf16[32,2880]{1,0:T(8,128)(2,1)S(1)}, u32[]{:S(2)}, u32[]{:S(2)}) %collective-permute-start.24) | collective-permute-done | bytes 184352 | tf_op jit(solution)/shard_map/ppermute | solution.py:390
  119.5 3.9 %collective-permute-start.25 = (bf16[32,2880]{1,0:T(8,128)(2,1)S(1)}, bf16[32,2880]{1,0:T(8,128)(2,1)S(1)}, u32[]{:S(2)}, u32[]{:S(2)}) collective-permute-start(bf16[32,2880]{1,0:T(8,128)(2,1)S(1)} %add_convert_fusion.2), channel_id=1, source_target_pairs={{0,3},{1,2},{2,1},{3,0},{4,7},{5,6},{6,5},{7,4},{8,11},{9,10},{10,... | collective-permute-start | bytes 552968 | tf_op jit(solution)/shard_map/ppermute | solution.py:390
  123.4 4.3 %collective-permute-done.25 = bf16[32,2880]{1,0:T(8,128)(2,1)S(1)} collective-permute-done((bf16[32,2880]{1,0:T(8,128)(2,1)S(1)}, bf16[32,2880]{1,0:T(8,128)(2,1)S(1)}, u32[]{:S(2)}, u32[]{:S(2)}) %collective-permute-start.25) | collective-permute-done | bytes 184352 | tf_op jit(solution)/shard_map/ppermute | solution.py:390
  129.8 6.3 %input_grad.1 = bf16[2880,128]{1,0:T(8,128)(2,1)} custom-call(s32[3]{0:T(128)S(1)} %pad_add_fusion.place_ref, bf16[4,128,128]{2,1,0:T(8,128)(2,1)S(1)} %get-tuple-element.73.key_ref, bf16[4,128,128]{2,1,0:T(8,128)(2,1)S(1)} %get-tuple-element.74.value_ref, bf16[256,2944]{1,0:T(8,128)(2,1)S(1)} %copy-done.4, ...), custom_call_target="tpu_custom_call" | custom-call | flops 754974720 | bytes 6766592 | tf_op jit(solution)/shard_map/input_grad/pallas_call | solution.py:372
  (70 shorter events, 31.0 us)
Async XLA Ops:
  0.6 24.8 %collective-permute-start.8 = (bf16[2880,128]{1,0:T(8,128)(2,1)}, bf16[2880,128]{1,0:T(8,128)(2,1)S(1)}, u32[]{:S(2)}, u32[]{:S(2)}) collective-permute-start(bf16[2880,128]{1,0:T(8,128)(2,1)} %bitcast.12), channel_id=1, source_target_pairs={{0,8},{8,0},{1,9},{9,1},{2,10},{10,2},{3,11},{11,3},{4,12},{12,4},... | collective-permute-start | bytes 2211848 | tf_op jit(solution)/shard_map/ppermute | solution.py:390
  4.6 7.1 %collective-permute-start = (bf16[32,2880]{1,0:T(8,128)(2,1)S(1)}, bf16[32,2880]{1,0:T(8,128)(2,1)S(1)}, u32[]{:S(2)}, u32[]{:S(2)}) collective-permute-start(bf16[32,2880]{1,0:T(8,128)(2,1)S(1)} %pad_maximum_fusion.refs_0_), channel_id=1, source_target_pairs={{0,1},{1,3},{3,2},{2,0},{4,5},{5,7},{7,6},{6,4},{8,9},{9,11},{11,1... | collective-permute-start | bytes 552968 | tf_op jit(solution)/shard_map/ppermute | solution.py:400
  6.2 6.3 %collective-permute-start.2 = (bf16[32,2880]{1,0:T(8,128)(2,1)S(1)}, bf16[32,2880]{1,0:T(8,128)(2,1)S(1)}, u32[]{:S(2)}, u32[]{:S(2)}) collective-permute-start(bf16[32,2880]{1,0:T(8,128)(2,1)S(1)} %pad_maximum_fusion.refs_0_), channel_id=1, source_target_pairs={{0,16},{16,0},{1,17},{17,1},{2,18},{18,2},{3,19},{19,3},{4,20},{20... | collective-permute-start | bytes 552968 | tf_op jit(solution)/shard_map/ppermute | solution.py:390
  11.7 6.5 %collective-permute-start.1 = (bf16[32,2880]{1,0:T(8,128)(2,1)S(1)}, bf16[32,2880]{1,0:T(8,128)(2,1)S(1)}, u32[]{:S(2)}, u32[]{:S(2)}) collective-permute-start(bf16[32,2880]{1,0:T(8,128)(2,1)S(1)} %collective-permute-done.refs_1_), channel_id=1, source_target_pairs={{0,1},{1,3},{3,2},{2,0},{4,5},{5,7},{7,6},{6,4},{8,9},{9,11},{11,1... | collective-permute-start | bytes 552968 | tf_op jit(solution)/shard_map/ppermute | solution.py:400
  18.2 6.6 %collective-permute-start.3 = (bf16[32,2880]{1,0:T(8,128)(2,1)S(1)}, bf16[32,2880]{1,0:T(8,128)(2,1)}, u32[]{:S(2)}, u32[]{:S(2)}) collective-permute-start(bf16[32,2880]{1,0:T(8,128)(2,1)S(1)} %collective-permute-done.1.refs_2_), channel_id=1, source_target_pairs={{0,1},{1,3},{3,2},{2,0},{4,5},{5,7},{7,6},{6,4},{8,9},{9,11},{11,1... | collective-permute-start | bytes 552968 | tf_op jit(solution)/shard_map/ppermute | solution.py:400
  19.0 5.8 %collective-permute-start.5 = (bf16[32,2880]{1,0:T(8,128)(2,1)S(1)}, bf16[32,2880]{1,0:T(8,128)(2,1)S(1)}, u32[]{:S(2)}, u32[]{:S(2)}) collective-permute-start(bf16[32,2880]{1,0:T(8,128)(2,1)S(1)} %collective-permute-done.1.refs_2_), channel_id=1, source_target_pairs={{0,16},{16,0},{1,17},{17,1},{2,18},{18,2},{3,19},{19,3},{4,20},{20... | collective-permute-start | bytes 552968 | tf_op jit(solution)/shard_map/ppermute | solution.py:390
  21.2 15.6 %collective-permute-start.7 = (bf16[2880,128]{1,0:T(8,128)(2,1)}, bf16[2880,128]{1,0:T(8,128)(2,1)}, u32[]{:S(2)}, u32[]{:S(2)}) collective-permute-start(bf16[2880,128]{1,0:T(8,128)(2,1)} %bitcast.13), channel_id=1, source_target_pairs={{0,4},{4,0},{1,5},{5,1},{2,6},{6,2},{3,7},{7,3},{8,12},{12,8},{9,1... | collective-permute-start | bytes 2211848 | tf_op jit(solution)/shard_map/ppermute | solution.py:390
  25.5 11.3 %collective-permute-start.9 = (bf16[2880,128]{1,0:T(8,128)(2,1)S(1)}, bf16[2880,128]{1,0:T(8,128)(2,1)}, u32[]{:S(2)}, u32[]{:S(2)}) collective-permute-start(bf16[2880,128]{1,0:T(8,128)(2,1)S(1)} %collective-permute-done.8.refs_10_.refs_6_), channel_id=1, source_target_pairs={{0,4},{4,0},{1,5},{5,1},{2,6},{6,2},{3,7},{7,3},{8,12},{12,8},{9,1... | collective-permute-start | bytes 2211848 | tf_op jit(solution)/shard_map/ppermute | solution.py:390
  25.5 7.6 %collective-permute-start.4 = (bf16[32,2880]{1,0:T(8,128)(2,1)S(1)}, bf16[32,2880]{1,0:T(8,128)(2,1)}, u32[]{:S(2)}, u32[]{:S(2)}) collective-permute-start(bf16[32,2880]{1,0:T(8,128)(2,1)S(1)} %collective-permute-done.refs_1_), channel_id=1, source_target_pairs={{0,16},{16,0},{1,17},{17,1},{2,18},{18,2},{3,19},{19,3},{4,20},{20... | collective-permute-start | bytes 552968 | tf_op jit(solution)/shard_map/ppermute | solution.py:390
  27.0 9.8 %collective-permute-start.6 = (bf16[32,2880]{1,0:T(8,128)(2,1)}, bf16[32,2880]{1,0:T(8,128)(2,1)}, u32[]{:S(2)}, u32[]{:S(2)}) collective-permute-start(bf16[32,2880]{1,0:T(8,128)(2,1)} %collective-permute-done.3.refs_3_), channel_id=1, source_target_pairs={{0,16},{16,0},{1,17},{17,1},{2,18},{18,2},{3,19},{19,3},{4,20},{20... | collective-permute-start | bytes 552968 | tf_op jit(solution)/shard_map/ppermute | solution.py:390
  49.3 40.2 %collective-permute-start.17 = (bf16[256,2944]{1,0:T(8,128)(2,1)}, bf16[256,2944]{1,0:T(8,128)(2,1)}, u32[]{:S(2)}, u32[]{:S(2)}) collective-permute-start(bf16[256,2944]{1,0:T(8,128)(2,1)} %get-tuple-element.64.refs_0_), channel_id=1, source_target_pairs={{0,8},{8,0},{1,9},{9,1},{2,10},{10,2},{3,11},{11,3},{4,12},{12,4},... | collective-permute-start | bytes 4521992 | tf_op jit(solution)/shard_map/ppermute | solution.py:390
  50.1 39.4 %collective-permute-start.18 = (bf16[256,2944]{1,0:T(8,128)(2,1)}, bf16[256,2944]{1,0:T(8,128)(2,1)}, u32[]{:S(2)}, u32[]{:S(2)}) collective-permute-start(bf16[256,2944]{1,0:T(8,128)(2,1)} %get-tuple-element.64.refs_0_), channel_id=1, source_target_pairs={{0,4},{4,0},{1,5},{5,1},{2,6},{6,2},{3,7},{7,3},{8,12},{12,8},{9,1... | collective-permute-start | bytes 4521992 | tf_op jit(solution)/shard_map/ppermute | solution.py:390
  50.1 8.9 %collective-permute-start.13 = (bf16[4,128,128]{2,1,0:T(8,128)(2,1)S(1)}, bf16[4,128,128]{2,1,0:T(8,128)(2,1)S(1)}, u32[]{:S(2)}, u32[]{:S(2)}) collective-permute-start(bf16[4,128,128]{2,1,0:T(8,128)(2,1)S(1)} %get-tuple-element.50.key_ref), channel_id=1, source_target_pairs={{0,1},{1,2},{2,3},{3,4},{4,5},{5,6},{6,7},{7,8},{8,9},{9,10},{10,1... | collective-permute-start | bytes 393224 | tf_op jit(solution)/shard_map/ppermute | solution.py:406
  55.2 10.9 %collective-permute-start.14 = (bf16[4,128,128]{2,1,0:T(8,128)(2,1)S(1)}, bf16[4,128,128]{2,1,0:T(8,128)(2,1)S(1)}, u32[]{:S(2)}, u32[]{:S(2)}) collective-permute-start(bf16[4,128,128]{2,1,0:T(8,128)(2,1)S(1)} %get-tuple-element.51.value_ref), channel_id=1, source_target_pairs={{0,1},{1,2},{2,3},{3,4},{4,5},{5,6},{6,7},{7,8},{8,9},{9,10},{10,1... | collective-permute-start | bytes 393224 | tf_op jit(solution)/shard_map/ppermute | solution.py:406
  78.0 8.3 %collective-permute-start.15 = (bf16[4,128,128]{2,1,0:T(8,128)(2,1)S(1)}, bf16[4,128,128]{2,1,0:T(8,128)(2,1)S(1)}, u32[]{:S(2)}, u32[]{:S(2)}) collective-permute-start(bf16[4,128,128]{2,1,0:T(8,128)(2,1)S(1)} %get-tuple-element.56), channel_id=1, source_target_pairs={{1,0},{2,1},{3,2},{4,3},{5,4},{6,5},{7,6},{8,7},{9,8},{10,9},{11,1... | collective-permute-start | bytes 393224 | tf_op jit(solution)/shard_map/ppermute | solution.py:406
  79.3 8.8 %collective-permute-start.16 = (bf16[4,128,128]{2,1,0:T(8,128)(2,1)S(1)}, bf16[4,128,128]{2,1,0:T(8,128)(2,1)S(1)}, u32[]{:S(2)}, u32[]{:S(2)}) collective-permute-start(bf16[4,128,128]{2,1,0:T(8,128)(2,1)S(1)} %get-tuple-element.58), channel_id=1, source_target_pairs={{1,0},{2,1},{3,2},{4,3},{5,4},{6,5},{7,6},{8,7},{9,8},{10,9},{11,1... | collective-permute-start | bytes 393224 | tf_op jit(solution)/shard_map/ppermute | solution.py:406
  100.1 7.8 %collective-permute-start.27 = (bf16[32,2880]{1,0:T(8,128)(2,1)S(1)}, bf16[32,2880]{1,0:T(8,128)(2,1)S(1)}, u32[]{:S(2)}, u32[]{:S(2)}) collective-permute-start(bf16[32,2880]{1,0:T(8,128)(2,1)S(1)} %get-tuple-element.79), channel_id=1, source_target_pairs={{0,16},{16,0},{1,17},{17,1},{2,18},{18,2},{3,19},{19,3},{4,20},{20... | collective-permute-start | bytes 552968 | tf_op jit(solution)/shard_map/ppermute | solution.py:390
  102.3 9.6 %collective-permute-start.22 = (bf16[32,2880]{1,0:T(8,128)(2,1)S(1)}, bf16[32,2880]{1,0:T(8,128)(2,1)S(1)}, u32[]{:S(2)}, u32[]{:S(2)}) collective-permute-start(bf16[32,2880]{1,0:T(8,128)(2,1)S(1)} %get-tuple-element.72), channel_id=1, source_target_pairs={{0,16},{16,0},{1,17},{17,1},{2,18},{18,2},{3,19},{19,3},{4,20},{20... | collective-permute-start | bytes 552968 | tf_op jit(solution)/shard_map/ppermute | solution.py:390
  102.4 21.0 %collective-permute-start.29 = (bf16[32,2880]{1,0:T(8,128)(2,1)S(1)}, bf16[32,2880]{1,0:T(8,128)(2,1)S(1)}, u32[]{:S(2)}, u32[]{:S(2)}) collective-permute-start(bf16[32,2880]{1,0:T(8,128)(2,1)S(1)} %get-tuple-element.81), channel_id=1, source_target_pairs={{0,16},{16,0},{1,17},{17,1},{2,18},{18,2},{3,19},{19,3},{4,20},{20... | collective-permute-start | bytes 552968 | tf_op jit(solution)/shard_map/ppermute | solution.py:390
  104.4 15.1 %collective-permute-start.24 = (bf16[32,2880]{1,0:T(8,128)(2,1)S(1)}, bf16[32,2880]{1,0:T(8,128)(2,1)S(1)}, u32[]{:S(2)}, u32[]{:S(2)}) collective-permute-start(bf16[32,2880]{1,0:T(8,128)(2,1)S(1)} %get-tuple-element.76), channel_id=1, source_target_pairs={{0,16},{16,0},{1,17},{17,1},{2,18},{18,2},{3,19},{19,3},{4,20},{20... | collective-permute-start | bytes 552968 | tf_op jit(solution)/shard_map/ppermute | solution.py:390
  107.9 15.5 %collective-permute-start.28 = (bf16[32,2880]{1,0:T(8,128)(2,1)S(1)}, bf16[32,2880]{1,0:T(8,128)(2,1)S(1)}, u32[]{:S(2)}, u32[]{:S(2)}) collective-permute-start(bf16[32,2880]{1,0:T(8,128)(2,1)S(1)} %add_convert_fusion), channel_id=1, source_target_pairs={{0,1},{1,0},{2,3},{3,2},{4,5},{5,4},{6,7},{7,6},{8,9},{9,8},{10,11... | collective-permute-start | bytes 552968 | tf_op jit(solution)/shard_map/ppermute | solution.py:390
  112.0 11.5 %collective-permute-start.26 = (bf16[32,2880]{1,0:T(8,128)(2,1)S(1)}, bf16[32,2880]{1,0:T(8,128)(2,1)S(1)}, u32[]{:S(2)}, u32[]{:S(2)}) collective-permute-start(bf16[32,2880]{1,0:T(8,128)(2,1)S(1)} %add_convert_fusion.1), channel_id=1, source_target_pairs={{0,2},{1,3},{2,0},{3,1},{4,6},{5,7},{6,4},{7,5},{8,10},{9,11},{10,... | collective-permute-start | bytes 552968 | tf_op jit(solution)/shard_map/ppermute | solution.py:390
  119.5 8.2 %collective-permute-start.25 = (bf16[32,2880]{1,0:T(8,128)(2,1)S(1)}, bf16[32,2880]{1,0:T(8,128)(2,1)S(1)}, u32[]{:S(2)}, u32[]{:S(2)}) collective-permute-start(bf16[32,2880]{1,0:T(8,128)(2,1)S(1)} %add_convert_fusion.2), channel_id=1, source_target_pairs={{0,3},{1,2},{2,1},{3,0},{4,7},{5,6},{6,5},{7,4},{8,11},{9,10},{10,... | collective-permute-start | bytes 552968 | tf_op jit(solution)/shard_map/ppermute | solution.py:390
  123.4 5.2 %collective-permute-start.23 = (bf16[256,2944]{1,0:T(8,128)(2,1)}, bf16[256,2944]{1,0:T(8,128)(2,1)S(1)}, u32[]{:S(2)}, u32[]{:S(2)}) collective-permute-start(bf16[256,2944]{1,0:T(8,128)(2,1)} %collective-permute-done.17.refs_2_), channel_id=1, source_target_pairs={{0,4},{4,0},{1,5},{5,1},{2,6},{6,2},{3,7},{7,3},{8,12},{12,8},{9,1... | collective-permute-start | bytes 4521992 | tf_op jit(solution)/shard_map/ppermute | solution.py:390
  (16 other events, 141.0 us)

commit v3 on v2

v3 whole, which is shorter than its diff:
```python
import functools
import math

import jax
import jax.numpy as jnp
from jax import lax
from jax.experimental import pallas as pl
from jax.experimental.pallas import tpu as pltpu
from jax.sharding import Mesh, PartitionSpec as P

KV_HEADS = 8
HEAD = 64
WIN = 128
LANES = 128
QUARTERS = 4
SUBLANES = 16

F32 = jnp.float32
BF16 = jnp.bfloat16
NT = (((1,), (1,)), ((), ()))
AXES = ("hi", "x", "c", "z")


def params(megabytes=20):
    return pltpu.CompilerParams(vmem_limit_bytes=megabytes * 1024 * 1024)


def cost(flops, *arrays):
    size = sum(math.prod(a.shape) * a.dtype.itemsize for a in arrays)
    return pl.CostEstimate(flops=int(flops), bytes_accessed=int(size), transcendentals=0)


def struct(shape, dtype):
    return jax.ShapeDtypeStruct(shape, dtype)


VMEM = pl.BlockSpec(memory_space=pltpu.VMEM)


def entire(array):
    return pl.BlockSpec(array.shape, lambda *step: (0,) * len(array.shape))


SMEM = pl.BlockSpec(memory_space=pltpu.SMEM)


def padded_pair(block, half):
    lane = lax.broadcasted_iota(jnp.int32, block.shape, 1)
    here = jnp.where(lane // HEAD == half, block.astype(F32), 0.0)
    there = pltpu.roll(here, HEAD, 1)
    even, odd = jnp.where(half == 0, here, there), jnp.where(half == 0, there, here)
    return even.astype(BF16), odd.astype(BF16)


def stacked(own, halo, half):
    own_even, own_odd = padded_pair(own, half)
    halo_even, halo_odd = padded_pair(halo, half)
    return jnp.concatenate([own_even, halo_even, own_odd, halo_odd], axis=0)


def folded(total):
    rows = total.shape[0] // 4
    lane = lax.broadcasted_iota(jnp.int32, (rows, LANES), 1)
    out = []
    for part in range(2):
        even = total[part * rows : (part + 1) * rows]
        odd = total[(2 + part) * rows : (3 + part) * rows]
        both = jnp.where(lane < HEAD, even, odd)
        out.append(both + pltpu.roll(both, HEAD, 1))
    return out


def store_half(ref, kind, value, half):
    lane = lax.broadcasted_iota(jnp.int32, value.shape, 1)
    old = ref[0, kind].astype(F32)
    ref[0, kind] = jnp.where(lane // HEAD == half, value, old).astype(ref.dtype)


def both_triangles(rows, width, dtype):
    u = lax.broadcasted_iota(jnp.int32, (rows, width), 0).astype(dtype)
    t = (lax.broadcasted_iota(jnp.int32, (rows, width), 1) % rows).astype(dtype)
    return u > t, u == t


def pair_of_blocks(ref, at):
    return jnp.concatenate(
        [ref[:, at : at + LANES], ref[:, at + LANES : at + 2 * LANES]], axis=0
    )


def attention_kernel(first_ref, q_ref, go_ref, own_ref, halo_ref, *refs):
    gq_ref, sums_ref, back_ref = refs[-3:]
    rows = own_ref.shape[2]
    later, same = both_triangles(rows, 2 * rows, jnp.int32)
    later_low, same_low = both_triangles(rows, 2 * rows, jnp.int16)
    zero = jnp.zeros((), BF16)
    factor = HEAD ** (-0.5)
    rate = factor * math.log2(math.e)
    shift = jnp.where(first_ref[0] == 1, -1e30, 0.0).astype(F32)
    half = pl.program_id(1)
    keys = stacked(own_ref[0, 0], halo_ref[0, 0], half)
    keys_across = keys.astype(F32).T.astype(BF16)
    values = stacked(own_ref[0, 1], halo_ref[0, 1], half)
    key_total = jnp.zeros((4 * rows, LANES), F32)
    value_total = jnp.zeros((4 * rows, LANES), F32)

    def split(mixed, diag):
        mixed, diag = mixed.astype(BF16), diag.astype(BF16)
        return [
            jnp.where(later_low, zero, mixed),
            jnp.where(later_low, mixed, jnp.where(same_low, diag, zero)),
        ]

    def merged(both, head):
        own = both[2 * head * rows : (2 * head + 1) * rows]
        halo = both[(2 * head + 1) * rows : (2 * head + 2) * rows]
        mixed = jnp.where(later, halo, own)
        return mixed, jnp.sum(jnp.where(same, halo, 0.0), axis=0, keepdims=True)

    hidden = jnp.where(later, shift, 0.0)
    for step in range(q_ref.shape[1] // (2 * LANES)):
        at = step * 2 * LANES
        q_pair, go_pair = pair_of_blocks(q_ref, at), pair_of_blocks(go_ref, at)
        scores = lax.dot_general(keys, q_pair, NT, preferred_element_type=F32)
        grads = lax.dot_general(values, go_pair, NT, preferred_element_type=F32)
        weights, terms = [], []
        for head in range(2):
            probs, diag = merged(scores, head)
            probs, diag = probs + hidden, diag + shift
            peak = jnp.maximum(jnp.max(probs, axis=0, keepdims=True), diag)
            probs = jnp.exp2((probs - peak) * rate)
            diag = jnp.exp2((diag - peak) * rate)
            inverse = 1.0 / (jnp.sum(probs, axis=0, keepdims=True) + diag)
            probs = probs * inverse
            diag = diag * inverse
            weights += split(probs, diag)
            mixed, edge = merged(grads, head)
            delta = jnp.sum(probs * mixed, axis=0, keepdims=True) + diag * edge
            terms += split(probs * (mixed - delta), diag * (edge - delta))
        value_total += jnp.dot(
            jnp.concatenate(weights, axis=0), go_pair, preferred_element_type=F32
        )
        stack = jnp.concatenate(terms, axis=0)
        key_total += jnp.dot(stack, q_pair, preferred_element_type=F32)
        across = jnp.dot(keys_across, stack, preferred_element_type=F32)
        for part in range(2):
            block = across[:, part * rows : (part + 1) * rows].T * factor
            gq_ref[:, at + part * LANES : at + (part + 1) * LANES] = block.astype(BF16)
    own, back = folded(key_total * factor)
    store_half(sums_ref, 0, own, half)
    store_half(back_ref, 0, back, half)
    own, back = folded(value_total)
    store_half(sums_ref, 1, own, half)
    store_half(back_ref, 1, back, half)


def attention(first, queries, grad_out, own, halo, at=0, before=None):
    rows, width = queries.shape
    sums, back = struct(own.shape, F32), struct(own.shape, BF16)
    by_head = pl.BlockSpec((rows, width // KV_HEADS), lambda q, h: (0, h * QUARTERS + at + q))
    by_quarter = pl.BlockSpec((1,) + own.shape[1:], lambda q, h: (q, 0, 0, 0))
    more = [] if before is None else [before]
    return pl.pallas_call(
        attention_kernel,
        grid=(own.shape[0], 2),
        in_specs=[SMEM] + [by_head] * 2 + [by_quarter] * 2 + [pl.BlockSpec(memory_space=pl.ANY)] * len(more),
        out_specs=[by_head, by_quarter, by_quarter],
        out_shape=[struct(queries.shape, BF16), sums, back],
        input_output_aliases={5: 0} if more else {},
        compiler_params=params(20),
        cost_estimate=cost(5 * own.shape[0] * rows * rows * width, queries, grad_out),
        name="attention",
    )(first, queries, grad_out, own, halo, *more)


def project_kernel(place_ref, *refs):
    pieces, hidden = refs[:8], refs[8:12]
    weight_ref, outs = refs[12], refs[13:]
    hi, z = place_ref[0], place_ref[1]
    depth = len(pieces) // 2
    step = pieces[0].shape[0] // 2
    size = pieces[0].shape[1]
    half = weight_ref.shape[0] // 2
    for r in range(2):
        for k in range(depth):
            row = ((hi ^ r) * depth + (z ^ k)) * step
            for kind in range(2):
                weight_ref[pl.ds(pl.multiple_of(kind * half + row, step), step), :size] = pieces[
                    r * depth + k
                ][kind * step : (kind + 1) * step, :]
    weight = weight_ref[:, :size]
    tokens = hidden[0].shape[1]
    for at in range(0, len(hidden), 2):
        pair = jnp.concatenate([hidden[at][...], hidden[at + 1][...]], axis=1)
        across = jnp.dot(weight, pair, preferred_element_type=F32)
        for k in range(2):
            outs[at + k][...] = across[:, k * tokens : (k + 1) * tokens].T.astype(BF16)


def project(place, pieces, hidden):
    depth, tokens = hidden[0].shape
    cols = sum(p.shape[0] for p in pieces)
    weight = struct((cols, -(-depth // LANES) * LANES), BF16)
    out = struct((tokens, cols), BF16)
    return pl.pallas_call(
        project_kernel,
        in_specs=[SMEM] + [entire(a) for a in pieces + hidden],
        out_specs=[VMEM] * (1 + len(hidden)),
        out_shape=[weight] + [out] * len(hidden),
        compiler_params=params(),
        cost_estimate=cost(2 * 4 * tokens * cols * depth, *hidden, weight, weight),
        name="project",
    )(place, *pieces, *hidden)


def arrange_kernel(place_ref, *refs):
    parts, outs, all_ref = refs[:QUARTERS], refs[QUARTERS:-1], refs[-1]
    for r, ref in enumerate(parts):
        for kind in range(2):
            all_ref[place_ref[2] ^ r, kind] = ref[:, kind * LANES : (kind + 1) * LANES]
    count = outs[0].shape[0]
    for k, out_ref in enumerate(outs):
        out_ref[...] = all_ref[k * count : (k + 1) * count]


def arrange(place, parts, chunks):
    shape = (2, parts[0].shape[0], LANES)
    out = struct((QUARTERS // chunks,) + shape, BF16)
    return pl.pallas_call(
        arrange_kernel,
        in_specs=[SMEM] + [entire(p) for p in parts],
        out_specs=[entire(out)] * chunks,
        out_shape=[out] * chunks,
        scratch_shapes=[pltpu.VMEM((QUARTERS,) + shape, BF16)],
        compiler_params=params(),
        cost_estimate=cost(0, out, out),
        name="arrange",
    )(place, *parts)


def natural(quarters):
    lane = lax.broadcasted_iota(jnp.int32, quarters[0].shape, 1)
    blocks = []
    for half in range(2):
        for first in range(0, QUARTERS, 2):
            left, right = quarters[first], quarters[first + 1]
            if half == 0:
                right = pltpu.roll(right, HEAD, 1)
            else:
                left = pltpu.roll(left, HEAD, 1)
            blocks.append(jnp.where(lane < HEAD, left, right))
    return blocks


def finish_kernel(chunks, place_ref, *refs):
    sums, backs = refs[:chunks], refs[chunks : 2 * chunks]
    key_ref, value_ref, all_ref = refs[2 * chunks : 2 * chunks + 3]
    outs = refs[2 * chunks + 3 :]
    count = QUARTERS // chunks
    for kind, natural_ref in enumerate((key_ref, value_ref)):
        lanes = slice(kind * LANES, (kind + 1) * LANES)
        quarters = []
        for q in range(QUARTERS):
            own = sums[q // count][q % count, kind]
            total = (own + backs[q // count][q % count, kind].astype(F32)).astype(BF16)
            all_ref[q, :, lanes] = total
            quarters.append(total.astype(F32))
        for m, block in enumerate(natural(quarters)):
            natural_ref[:, m * LANES : (m + 1) * LANES] = block.astype(BF16)
    for r, ref in enumerate(outs):
        ref[...] = all_ref[place_ref[2] ^ r]


def finish(place, sums, backs):
    rows = sums[0].shape[2]
    wide = struct((rows, QUARTERS * LANES), BF16)
    every = struct((QUARTERS, rows, 2 * LANES), BF16)
    part = struct((rows, 2 * LANES), BF16)
    shapes = [wide, wide, every] + [part] * QUARTERS
    return pl.pallas_call(
        functools.partial(finish_kernel, len(sums)),
        in_specs=[SMEM] + [entire(a) for a in sums + backs],
        out_specs=[entire(a) for a in shapes],
        out_shape=shapes,
        compiler_params=params(),
        cost_estimate=cost(0, *sums),
        name="finish",
    )(place, *sums, *backs)


def spans(size, step):
    return [(at, min(step, size - at)) for at in range(0, size, step)]


def weight_grad_kernel(place_ref, *refs):
    grads, hidden = refs[:4], refs[4:8]
    outs, wide_ref = refs[8:-1], refs[-1]
    hi, z = place_ref[0], place_ref[1]
    for at, size in spans(hidden[0].shape[0], 256):
        total = jnp.zeros((size, grads[0].shape[1]), F32)
        for k in range(0, len(grads), 2):
            rows = jnp.concatenate([h[at : at + size, :] for h in hidden[k : k + 2]], axis=1)
            cols = jnp.concatenate([g[...] for g in grads[k : k + 2]], axis=0)
            total += jnp.dot(rows, cols, preferred_element_type=F32)
        wide_ref[:, at : at + size] = total.T
    depth = len(outs) // 2
    step = outs[0].shape[0] // 2
    half = wide_ref.shape[0] // 2
    for r in range(2):
        for k in range(depth):
            row = ((hi ^ r) * depth + (z ^ k)) * step
            for kind in range(2):
                at = pl.multiple_of(kind * half + row, step)
                outs[r * depth + k][kind * step : (kind + 1) * step, :] = wide_ref[
                    pl.ds(at, step), :
                ].astype(BF16)


def weight_grad(place, grads, hidden, depth):
    size, tokens = hidden[0].shape
    cols = grads[0].shape[1]
    part = struct((cols // (2 * depth), size), BF16)
    return pl.pallas_call(
        weight_grad_kernel,
        in_specs=[SMEM] + [entire(a) for a in grads + hidden],
        out_specs=[VMEM] * (2 * depth),
        out_shape=[part] * (2 * depth),
        scratch_shapes=[pltpu.VMEM((cols, size), F32)],
        compiler_params=params(),
        cost_estimate=cost(2 * 4 * tokens * cols * size, *hidden, *hidden),
        name="weight_grad",
    )(place, *grads, *hidden)


def input_grad_kernel(place_ref, all_ref, *refs):
    out_ref = refs[-1]
    total = jnp.zeros((all_ref.shape[1], out_ref.shape[0]), F32)
    for r, w_ref in enumerate(refs[:-1]):
        total += jnp.dot(all_ref[place_ref[2] ^ r], w_ref[...], preferred_element_type=F32)
    out_ref[...] = total.T.astype(BF16)


def input_grad(place, every, weights, size):
    cols, wide = weights[0].shape
    rows = every.shape[1]
    step = 512
    out = struct((size, rows), BF16)
    return pl.pallas_call(
        input_grad_kernel,
        grid=(-(-size // step),),
        in_specs=[SMEM, entire(every)]
        + [pl.BlockSpec((cols, step), lambda i: (0, i))] * len(weights),
        out_specs=pl.BlockSpec((step, rows), lambda i: (i, 0)),
        out_shape=out,
        compiler_params=params(),
        cost_estimate=cost(8 * rows * cols * size, *weights, out),
        name="input_grad",
    )(place, every, *weights)


def after(array, *others):
    return lax.optimization_barrier((array, *others))[0]


def flip(array, axis, by):
    return lax.ppermute(array, axis, [(i, i ^ by) for i in range(lax.axis_size(axis))])


def flip_group(array, by):
    return lax.ppermute(array, ("x", "c"), [(i, i ^ by) for i in range(QUARTERS)])


def shifted(array, by):
    size = lax.axis_size(AXES)
    pairs = [(i, i + by) for i in range(size) if 0 <= i + by < size]
    return lax.ppermute(array, AXES, pairs)


def exchanged(parts):
    return [parts[0]] + [flip_group(parts[r], r) for r in range(1, QUARTERS)]


def fast_shards(hidden_in, queries, grad_out, key_weight, value_weight):
    size = hidden_in.shape[1]
    depth = lax.axis_size("z")
    group = lax.axis_index(("x", "c"))
    place = jnp.stack([lax.axis_index("hi"), lax.axis_index("z"), group]).astype(jnp.int32)
    first = (lax.axis_index(AXES) == 0).astype(jnp.int32).reshape(1)
    pieces = [jnp.concatenate([key_weight.T, value_weight.T], axis=0)]
    own = after(hidden_in.T, pieces[0])
    x_side = flip(own, "x", 1)
    pieces += [flip(pieces[0], "z", k) for k in range(1, depth)]
    across = [flip(piece, "hi", 1) for piece in pieces]
    x_side = after(x_side, pieces[-1], *across[: depth - 1])
    hidden = [own, flip(own, "c", 1), x_side, flip(x_side, "c", 1)]
    mine, *parts = project(place, pieces + across, hidden)
    chunks = 1
    rows = arrange(place, exchanged(parts), chunks)
    filled = after(mine, *rows)
    x_filled = flip(filled, "x", 1)
    c_filled = flip(filled, "c", 1)
    halos = [shifted(part, 1) for part in rows]
    grad_queries = None
    sums, backs = [], []
    for k in range(chunks):
        grad_queries, own_sums, back = attention(
            first, queries, grad_out, rows[k], halos[k], k * rows[k].shape[0], grad_queries
        )
        sums.append(own_sums)
        backs.append(shifted(after(back, *backs), -1))
    grad_keys, grad_values, every, *parts = finish(place, sums, backs)
    parts = exchanged(parts)
    parts[0] = after(parts[0], x_filled, c_filled)
    weights = [mine, c_filled, x_filled, flip(x_filled, "c", 1)]
    grads = weight_grad(place, parts, hidden, depth)
    keep, send = grads[:depth], grads[depth:]
    grad_inputs = input_grad(place, every, weights, size)
    came = []
    total = None
    for k in reversed(range(depth)):
        came.append(flip(send[k] if k else after(send[k], came[0]), "hi", 1))
        kept = keep[k] if k else after(keep[k], grad_inputs)
        sum_k = kept.astype(F32) + came[-1].astype(F32)
        if k:
            sum_k = flip(sum_k.astype(BF16), "z", k).astype(F32)
        total = sum_k if total is None else total + sum_k
    grad_inputs = grad_inputs.T
    scale = (hidden_in.shape[0] * lax.axis_size(AXES)) ** (-0.5)
    total = total * scale
    rows = total.shape[0] // 2
    return (
        grad_queries,
        grad_keys,
        grad_values,
        grad_inputs,
        total[:rows].T,
        total[rows:].T,
    )


def to_quarters(rows):
    count = rows.shape[0]
    split = rows.reshape(count, 2, QUARTERS, HEAD)
    return jnp.transpose(split, (2, 0, 1, 3)).reshape(QUARTERS, count, 2 * HEAD)


def from_quarters(quarters):
    count = quarters.shape[1]
    split = quarters.reshape(QUARTERS, count, 2, HEAD)
    return jnp.transpose(split, (1, 2, 0, 3)).reshape(count, 2 * QUARTERS * HEAD)


def plain_shards(hidden_in, queries, grad_out, key_weight, value_weight):
    key_full = lax.all_gather(key_weight.T, AXES, axis=0, tiled=True)
    value_full = lax.all_gather(value_weight.T, AXES, axis=0, tiled=True)
    first = (lax.axis_index(AXES) == 0).astype(jnp.int32).reshape(1)

    def rows_of(weight):
        rows = lax.dot_general(hidden_in, weight, NT, preferred_element_type=F32)
        return to_quarters(rows.astype(BF16))

    own = jnp.stack([rows_of(key_full), rows_of(value_full)], axis=1)
    grad_queries, sums, back = attention(first, queries, grad_out, own, shifted(own, 1))
    sums = sums + shifted(back, -1).astype(F32)
    grad_keys = from_quarters(sums[:, 0]).astype(BF16)
    grad_values = from_quarters(sums[:, 1]).astype(BF16)
    grad_inputs = (
        jnp.dot(grad_keys, key_full, preferred_element_type=F32)
        + jnp.dot(grad_values, value_full, preferred_element_type=F32)
    ).astype(BF16)
    scale = (hidden_in.shape[0] * lax.axis_size(AXES)) ** (-0.5)

    def summed(grad):
        rows = (((0,), (0,)), ((), ()))
        part = lax.dot_general(grad, hidden_in, rows, preferred_element_type=F32)
        return (lax.psum_scatter(part, AXES, scatter_dimension=0, tiled=True) * scale).T

    return (
        grad_queries,
        grad_keys,
        grad_values,
        grad_inputs,
        summed(grad_keys),
        summed(grad_values),
    )


def solution(mesh):
    outer, inner = mesh.shape["seqa"], mesh.shape["seqb"]
    split = Mesh(mesh.devices.reshape(outer // QUARTERS, 2, 2, inner), AXES)
    cols = KV_HEADS * HEAD // (outer * inner)
    fast = outer == 2 * QUARTERS and inner == 4 and cols % SUBLANES == 0
    rows, columns = P(AXES, None), P(None, AXES)
    return jax.shard_map(
        fast_shards if fast else plain_shards,
        mesh=split,
        in_specs=(rows, rows, rows, columns, columns),
        out_specs=(rows, rows, rows, rows, columns, columns),
        check_vma=False,
    )
```

time: 137 us -> 117 us (0.85)
  Pallas kernels: 34.1 us -> 23.7 us
  waiting for transfers between devices: 57.3 us -> 51.9 us
  local copies, waits for them, and re-layouts: 6.27 us -> 4.33 us
  starting transfers between devices: 36.4 us -> 34.9 us
    ppermute x3 -> x0, waiting for transfers between devices: 13.3 us -> none  [round_ring(): lax.ppermute(array, 'z', [(order[i], order[(i + 1) % size]) for i in rang...]
    pallas_call x6 -> x5, Pallas kernels: 27.7 us -> 17.8 us  [the longest x1 11.1 us: attention(): pl.pallas_call(attention_kernel, grid=(own.shape[0], 2), in_specs=[SMEM]...]
    ppermute x4 -> x2, starting transfers between devices: 9.55 us -> 2.64 us  [shifted(): return lax.ppermute(array, AXES, pairs)]
    ppermute x17 -> x20, starting transfers between devices: 18.4 us -> 23.9 us  [flip(): lax.ppermute(array, axis, [(i, i ^ by) for i in range(lax.axis_size(axis))])]
    ppermute x4 -> x2, waiting for transfers between devices: 9.36 us -> 14.5 us  [shifted(): return lax.ppermute(array, AXES, pairs)]
    ppermute x3 -> x0, starting transfers between devices: 3.2 us -> none  [round_ring(): lax.ppermute(array, 'z', [(order[i], order[(i + 1) % size]) for i in rang...]
    ppermute x6, starting transfers between devices: 5.22 us -> 8.36 us  [flip_group(): lax.ppermute(array, ('x', 'c'), [(i, i ^ by) for i in range(QUARTERS)])]
    ppermute x17 -> x20, waiting for transfers between devices: 27.1 us -> 29.8 us  [flip(): lax.ppermute(array, axis, [(i, i ^ by) for i in range(lax.axis_size(axis))])]
  transfers between devices with their start and end apart: 30 -> 28, of which waited for: 16 -> 15; matrix products, arithmetic and copies ran while one was open for 2% -> 0% of each run, Pallas kernels for 15% -> 16%
where the time goes in v3:
time: 117 us
  waiting for transfers between devices  51.9 us (44%)
  starting transfers between devices  34.9 us (30%)
  Pallas kernels  23.7 us (20%)
  local copies, waits for them, and re-layouts  4.33 us (4%)
  other arithmetic  1.3 us (1%)
    ppermute x20, waiting for transfers between devices, flip(): lax.ppermute(array, axis, [(i, i ^ by) for i in range(lax.axis_size(axis))])  29.8 us
    ppermute x20, starting transfers between devices, flip(): lax.ppermute(array, axis, [(i, i ^ by) for i in range(lax.axis_size(axis))])  23.9 us
    ppermute x2, waiting for transfers between devices, shifted(): return lax.ppermute(array, AXES, pairs)  14.5 us
    pallas_call x1, Pallas kernels, attention(): pl.pallas_call(attention_kernel, grid=(own.shape[0], 2), in_specs=[SMEM]...  11.1 us
    ppermute x6, starting transfers between devices, flip_group(): lax.ppermute(array, ('x', 'c'), [(i, i ^ by) for i in range(QUARTERS)])  8.36 us
    ppermute x6, waiting for transfers between devices, flip_group(): lax.ppermute(array, ('x', 'c'), [(i, i ^ by) for i in range(QUARTERS)])  7.57 us
    pallas_call x1, Pallas kernels, input_grad(): pl.pallas_call(input_grad_kernel, grid=(-(-size // step),), in_specs=[SME...  5.91 us
    unnamed x8, local copies, waits for them, and re-layouts  3.57 us
  transfers between devices with their start and end apart: 28, of which 15 were waited for; matrix products, arithmetic and copies ran while one was open for 0% of the time, Pallas kernels for 16%

profile of v3, /device:TPU:0, one launch (start us, length us, event | category | flops | bytes accessed | tf_op | source)
XLA Modules:
  0.0 116.8 jit_solution(13565196524254756500)
XLA Ops:
  1.6 3.0 %collective-permute-start.8 = (bf16[2880,128]{1,0:T(8,128)(2,1)}, bf16[2880,128]{1,0:T(8,128)(2,1)S(1)}, u32[]{:S(2)}, u32[]{:S(2)}) collective-permute-start(bf16[2880,128]{1,0:T(8,128)(2,1)} %bitcast.12), channel_id=1, source_target_pairs={{0,8},{8,0},{1,9},{9,1},{2,10},{10,2},{3,11},{11,3},{4,12},{12,4},... | collective-permute-start | bytes 2211848 | tf_op jit(solution)/shard_map/ppermute | solution.py:366
  4.6 1.6 %collective-permute-start = (bf16[32,2880]{1,0:T(8,128)(2,1)S(1)}, bf16[32,2880]{1,0:T(8,128)(2,1)S(1)}, u32[]{:S(2)}, u32[]{:S(2)}) collective-permute-start(bf16[32,2880]{1,0:T(8,128)(2,1)S(1)} %pad_maximum_fusion.refs_0_), channel_id=1, source_target_pairs={{0,1},{1,0},{2,3},{3,2},{4,5},{5,4},{6,7},{7,6},{8,9},{9,8},{10,11... | collective-permute-start | bytes 552968 | tf_op jit(solution)/shard_map/ppermute | solution.py:366
  6.2 2.6 %collective-permute-start.1 = (bf16[32,2880]{1,0:T(8,128)(2,1)S(1)}, bf16[32,2880]{1,0:T(8,128)(2,1)S(1)}, u32[]{:S(2)}, u32[]{:S(2)}) collective-permute-start(bf16[32,2880]{1,0:T(8,128)(2,1)S(1)} %pad_maximum_fusion.refs_0_), channel_id=1, source_target_pairs={{0,2},{1,3},{2,0},{3,1},{4,6},{5,7},{6,4},{7,5},{8,10},{9,11},{10,... | collective-permute-start | bytes 552968 | tf_op jit(solution)/shard_map/ppermute | solution.py:366
  10.5 3.2 %collective-permute-done.refs_1_ = bf16[32,2880]{1,0:T(8,128)(2,1)S(1)} collective-permute-done((bf16[32,2880]{1,0:T(8,128)(2,1)S(1)}, bf16[32,2880]{1,0:T(8,128)(2,1)S(1)}, u32[]{:S(2)}, u32[]{:S(2)}) %collective-permute-start) | collective-permute-done | bytes 184352 | tf_op jit(solution)/shard_map/ppermute | solution.py:366
  15.2 7.6 %collective-permute-done.1.refs_2_ = bf16[32,2880]{1,0:T(8,128)(2,1)S(1)} collective-permute-done((bf16[32,2880]{1,0:T(8,128)(2,1)S(1)}, bf16[32,2880]{1,0:T(8,128)(2,1)S(1)}, u32[]{:S(2)}, u32[]{:S(2)}) %collective-permute-start.1) | collective-permute-done | bytes 184352 | tf_op jit(solution)/shard_map/ppermute | solution.py:366
  24.4 4.0 %collective-permute-done.5.refs_6_ = bf16[32,2880]{1,0:T(8,128)(2,1)S(1)} collective-permute-done((bf16[32,2880]{1,0:T(8,128)(2,1)S(1)}, bf16[32,2880]{1,0:T(8,128)(2,1)S(1)}, u32[]{:S(2)}, u32[]{:S(2)}) %collective-permute-start.5) | collective-permute-done | bytes 184352 | tf_op jit(solution)/shard_map/ppermute | solution.py:366
  28.4 1.5 %collective-permute-start.6 = (bf16[32,2880]{1,0:T(8,128)(2,1)S(1)}, bf16[32,2880]{1,0:T(8,128)(2,1)}, u32[]{:S(2)}, u32[]{:S(2)}) collective-permute-start(bf16[32,2880]{1,0:T(8,128)(2,1)S(1)} %collective-permute-done.2.refs_3_), channel_id=1, source_target_pairs={{0,16},{16,0},{1,17},{17,1},{2,18},{18,2},{3,19},{19,3},{4,20},{20... | collective-permute-start | bytes 552968 | tf_op jit(solution)/shard_map/ppermute | solution.py:366
  30.0 5.6 %collective-permute-done.6.refs_7_ = bf16[32,2880]{1,0:T(8,128)(2,1)} collective-permute-done((bf16[32,2880]{1,0:T(8,128)(2,1)S(1)}, bf16[32,2880]{1,0:T(8,128)(2,1)}, u32[]{:S(2)}, u32[]{:S(2)}) %collective-permute-start.6) | collective-permute-done | bytes 184352 | tf_op jit(solution)/shard_map/ppermute | solution.py:366
  36.8 2.9 %project.1 = (bf16[256,2944]{1,0:T(8,128)(2,1)}, bf16[128,256]{1,0:T(8,128)(2,1)S(1)}, bf16[128,256]{1,0:T(8,128)(2,1)S(1)}, bf16[128,256]{1,0:T(8,128)(2,1)S(1)}, bf16[128,256]{1,0:T(8,128)(2,1)S(1)}) custom-call(s32[3]{0:T(128)S(1)} %pad_add_fusion.place_ref, bf16[32,2880]{1,0:T(8,128)(2,1)S(1)} %pad_maximum_fusion.refs_0_, ...), custom_call_target="tpu_custom_call" | custom-call | flops 754974720 | bytes 5963776 | tf_op jit(solution)/shard_map/project/pallas_call | solution.py:205
  41.5 3.0 %collective-permute-done.11.refs_2_ = bf16[128,256]{1,0:T(8,128)(2,1)S(1)} collective-permute-done((bf16[128,256]{1,0:T(8,128)(2,1)S(1)}, bf16[128,256]{1,0:T(8,128)(2,1)S(1)}, u32[]{:S(2)}, u32[]{:S(2)}) %collective-permute-start.11) | collective-permute-done | bytes 65568 | tf_op jit(solution)/shard_map/ppermute | solution.py:370
  48.0 6.6 %collective-permute-done.13.halo_ref = bf16[4,2,128,128]{3,2,1,0:T(8,128)(2,1)S(1)} collective-permute-done((bf16[4,2,128,128]{3,2,1,0:T(8,128)(2,1)S(1)}, bf16[4,2,128,128]{3,2,1,0:T(8,128)(2,1)S(1)}, u32[]{:S(2)}, u32[]{:S(2)}) %collective-permute-start.13) | collective-permute-done | bytes 262176 | tf_op jit(solution)/shard_map/ppermute | solution.py:376
  57.1 11.1 %attention.1 = (bf16[128,4096]{1,0:T(8,128)(2,1)}, f32[4,2,128,128]{3,2,1,0:T(8,128)S(1)}, bf16[4,2,128,128]{3,2,1,0:T(8,128)(2,1)S(1)}) custom-call(s32[1]{0:T(128)} %bitcast.first_ref, bf16[128,4096]{1,0:T(8,128)(2,1)S(1)} %copy-done.2, bf16[128,4096]{1,0:T(8,128)(2,1)S(1)} %copy-done.3, bf16[4,2,128,128]{3,2,1,0:T(8,128)(2,1)S(1)} %arrange.1.own_ref, ...), custom_call_target="tpu_custom_call" | custom-call | flops 1342177280 | bytes 2097152 | tf_op jit(solution)/shard_map/attention/pallas_call | solution.py:163
  69.5 7.8 %collective-permute-done.14.refs_1_ = bf16[4,2,128,128]{3,2,1,0:T(8,128)(2,1)S(1)} collective-permute-done((bf16[4,2,128,128]{3,2,1,0:T(8,128)(2,1)S(1)}, bf16[4,2,128,128]{3,2,1,0:T(8,128)(2,1)S(1)}, u32[]{:S(2)}, u32[]{:S(2)}) %collective-permute-start.14) | collective-permute-done | bytes 262176 | tf_op jit(solution)/shard_map/ppermute | solution.py:376
  78.7 2.6 %collective-permute-start.18 = (bf16[128,256]{1,0:T(8,128)(2,1)S(1)}, bf16[128,256]{1,0:T(8,128)(2,1)S(1)}, u32[]{:S(2)}, u32[]{:S(2)}) collective-permute-start(bf16[128,256]{1,0:T(8,128)(2,1)S(1)} %get-tuple-element.51), channel_id=1, source_target_pairs={{0,4},{4,0},{8,12},{12,8},{1,5},{5,1},{9,13},{13,9},{2,6},{6,2},{1... | collective-permute-start | bytes 196616 | tf_op jit(solution)/shard_map/ppermute | solution.py:370
  81.3 3.7 %collective-permute-start.19 = (bf16[128,256]{1,0:T(8,128)(2,1)S(1)}, bf16[128,256]{1,0:T(8,128)(2,1)S(1)}, u32[]{:S(2)}, u32[]{:S(2)}) collective-permute-start(bf16[128,256]{1,0:T(8,128)(2,1)S(1)} %get-tuple-element.52), channel_id=1, source_target_pairs={{0,8},{4,12},{8,0},{12,4},{1,9},{5,13},{9,1},{13,5},{2,10},{6,14},... | collective-permute-start | bytes 196616 | tf_op jit(solution)/shard_map/ppermute | solution.py:370
  85.2 2.6 %collective-permute-done.19.refs_2_ = bf16[128,256]{1,0:T(8,128)(2,1)S(1)} collective-permute-done((bf16[128,256]{1,0:T(8,128)(2,1)S(1)}, bf16[128,256]{1,0:T(8,128)(2,1)S(1)}, u32[]{:S(2)}, u32[]{:S(2)}) %collective-permute-start.19) | collective-permute-done | bytes 65568 | tf_op jit(solution)/shard_map/ppermute | solution.py:370
  89.1 1.8 %weight_grad.1 = (bf16[32,2880]{1,0:T(8,128)(2,1)S(1)}, bf16[32,2880]{1,0:T(8,128)(2,1)S(1)}, bf16[32,2880]{1,0:T(8,128)(2,1)S(1)}, bf16[32,2880]{1,0:T(8,128)(2...) custom-call(s32[3]{0:T(128)S(1)} %pad_add_fusion.place_ref, ...), custom_call_target="tpu_custom_call" | custom-call | flops 754974720 | bytes 5898240 | tf_op jit(solution)/shard_map/weight_grad/pallas_call | solution.py:323
  90.9 1.7 %collective-permute-start.21 = (bf16[32,2880]{1,0:T(8,128)(2,1)S(1)}, bf16[32,2880]{1,0:T(8,128)(2,1)S(1)}, u32[]{:S(2)}, u32[]{:S(2)}) collective-permute-start(bf16[32,2880]{1,0:T(8,128)(2,1)S(1)} %get-tuple-element.55), channel_id=1, source_target_pairs={{0,16},{16,0},{1,17},{17,1},{2,18},{18,2},{3,19},{19,3},{4,20},{20... | collective-permute-start | bytes 552968 | tf_op jit(solution)/shard_map/ppermute | solution.py:366
  93.0 1.7 %collective-permute-start.25 = (bf16[32,2880]{1,0:T(8,128)(2,1)S(1)}, bf16[32,2880]{1,0:T(8,128)(2,1)S(1)}, u32[]{:S(2)}, u32[]{:S(2)}) collective-permute-start(bf16[32,2880]{1,0:T(8,128)(2,1)S(1)} %get-tuple-element.59), channel_id=1, source_target_pairs={{0,16},{16,0},{1,17},{17,1},{2,18},{18,2},{3,19},{19,3},{4,20},{20... | collective-permute-start | bytes 552968 | tf_op jit(solution)/shard_map/ppermute | solution.py:366
  94.6 3.9 %collective-permute-done.21 = bf16[32,2880]{1,0:T(8,128)(2,1)S(1)} collective-permute-done((bf16[32,2880]{1,0:T(8,128)(2,1)S(1)}, bf16[32,2880]{1,0:T(8,128)(2,1)S(1)}, u32[]{:S(2)}, u32[]{:S(2)}) %collective-permute-start.21) | collective-permute-done | bytes 184352 | tf_op jit(solution)/shard_map/ppermute | solution.py:366
  98.6 3.9 %collective-permute-start.22 = (bf16[32,2880]{1,0:T(8,128)(2,1)S(1)}, bf16[32,2880]{1,0:T(8,128)(2,1)S(1)}, u32[]{:S(2)}, u32[]{:S(2)}) collective-permute-start(bf16[32,2880]{1,0:T(8,128)(2,1)S(1)} %add_convert_fusion.2), channel_id=1, source_target_pairs={{0,3},{1,2},{2,1},{3,0},{4,7},{5,6},{6,5},{7,4},{8,11},{9,10},{10,... | collective-permute-start | bytes 552968 | tf_op jit(solution)/shard_map/ppermute | solution.py:366
  102.7 3.1 %collective-permute-done.25 = bf16[32,2880]{1,0:T(8,128)(2,1)S(1)} collective-permute-done((bf16[32,2880]{1,0:T(8,128)(2,1)S(1)}, bf16[32,2880]{1,0:T(8,128)(2,1)S(1)}, u32[]{:S(2)}, u32[]{:S(2)}) %collective-permute-start.25) | collective-permute-done | bytes 184352 | tf_op jit(solution)/shard_map/ppermute | solution.py:366
  107.7 5.9 %input_grad.1 = bf16[2880,128]{1,0:T(8,128)(2,1)} custom-call(s32[3]{0:T(128)S(1)} %pad_add_fusion.place_ref, bf16[4,128,256]{2,1,0:T(8,128)(2,1)S(1)} %get-tuple-element.46.all_ref, bf16[256,2944]{1,0:T(8,128)(2,1)} %get-tuple-element.48.refs_0_, bf16[256,2944]{1,0:T(8,128)(2,1)} %collective-permute-done.15.refs_1_, ...), custom_call_target="tpu_custom_call" | custom-call | flops 754974720 | bytes 6766592 | tf_op jit(solution)/shard_map/input_grad/pallas_call | solution.py:348
  113.6 1.8 %collective-permute-done.24 = bf16[32,2880]{1,0:T(8,128)(2,1)S(1)} collective-permute-done((bf16[32,2880]{1,0:T(8,128)(2,1)S(1)}, bf16[32,2880]{1,0:T(8,128)(2,1)S(1)}, u32[]{:S(2)}, u32[]{:S(2)}) %collective-permute-start.24) | collective-permute-done | bytes 184352 | tf_op jit(solution)/shard_map/ppermute | solution.py:366
  (53 shorter events, 22.7 us)
Async XLA Ops:
  1.6 26.8 %collective-permute-start.8 = (bf16[2880,128]{1,0:T(8,128)(2,1)}, bf16[2880,128]{1,0:T(8,128)(2,1)S(1)}, u32[]{:S(2)}, u32[]{:S(2)}) collective-permute-start(bf16[2880,128]{1,0:T(8,128)(2,1)} %bitcast.12), channel_id=1, source_target_pairs={{0,8},{8,0},{1,9},{9,1},{2,10},{10,2},{3,11},{11,3},{4,12},{12,4},... | collective-permute-start | bytes 2211848 | tf_op jit(solution)/shard_map/ppermute | solution.py:366
  4.6 9.1 %collective-permute-start = (bf16[32,2880]{1,0:T(8,128)(2,1)S(1)}, bf16[32,2880]{1,0:T(8,128)(2,1)S(1)}, u32[]{:S(2)}, u32[]{:S(2)}) collective-permute-start(bf16[32,2880]{1,0:T(8,128)(2,1)S(1)} %pad_maximum_fusion.refs_0_), channel_id=1, source_target_pairs={{0,1},{1,0},{2,3},{3,2},{4,5},{5,4},{6,7},{7,6},{8,9},{9,8},{10,11... | collective-permute-start | bytes 552968 | tf_op jit(solution)/shard_map/ppermute | solution.py:366
  6.2 16.6 %collective-permute-start.1 = (bf16[32,2880]{1,0:T(8,128)(2,1)S(1)}, bf16[32,2880]{1,0:T(8,128)(2,1)S(1)}, u32[]{:S(2)}, u32[]{:S(2)}) collective-permute-start(bf16[32,2880]{1,0:T(8,128)(2,1)S(1)} %pad_maximum_fusion.refs_0_), channel_id=1, source_target_pairs={{0,2},{1,3},{2,0},{3,1},{4,6},{5,7},{6,4},{7,5},{8,10},{9,11},{10,... | collective-permute-start | bytes 552968 | tf_op jit(solution)/shard_map/ppermute | solution.py:366
  8.8 15.6 %collective-permute-start.2 = (bf16[32,2880]{1,0:T(8,128)(2,1)S(1)}, bf16[32,2880]{1,0:T(8,128)(2,1)S(1)}, u32[]{:S(2)}, u32[]{:S(2)}) collective-permute-start(bf16[32,2880]{1,0:T(8,128)(2,1)S(1)} %pad_maximum_fusion.refs_0_), channel_id=1, source_target_pairs={{0,3},{1,2},{2,1},{3,0},{4,7},{5,6},{6,5},{7,4},{8,11},{9,10},{10,... | collective-permute-start | bytes 552968 | tf_op jit(solution)/shard_map/ppermute | solution.py:366
  9.0 15.4 %collective-permute-start.3 = (bf16[32,2880]{1,0:T(8,128)(2,1)S(1)}, bf16[32,2880]{1,0:T(8,128)(2,1)S(1)}, u32[]{:S(2)}, u32[]{:S(2)}) collective-permute-start(bf16[32,2880]{1,0:T(8,128)(2,1)S(1)} %pad_maximum_fusion.refs_0_), channel_id=1, source_target_pairs={{0,16},{16,0},{1,17},{17,1},{2,18},{18,2},{3,19},{19,3},{4,20},{20... | collective-permute-start | bytes 552968 | tf_op jit(solution)/shard_map/ppermute | solution.py:366
  13.7 10.6 %collective-permute-start.4 = (bf16[32,2880]{1,0:T(8,128)(2,1)S(1)}, bf16[32,2880]{1,0:T(8,128)(2,1)S(1)}, u32[]{:S(2)}, u32[]{:S(2)}) collective-permute-start(bf16[32,2880]{1,0:T(8,128)(2,1)S(1)} %collective-permute-done.refs_1_), channel_id=1, source_target_pairs={{0,16},{16,0},{1,17},{17,1},{2,18},{18,2},{3,19},{19,3},{4,20},{20... | collective-permute-start | bytes 552968 | tf_op jit(solution)/shard_map/ppermute | solution.py:366
  22.8 5.6 %collective-permute-start.5 = (bf16[32,2880]{1,0:T(8,128)(2,1)S(1)}, bf16[32,2880]{1,0:T(8,128)(2,1)S(1)}, u32[]{:S(2)}, u32[]{:S(2)}) collective-permute-start(bf16[32,2880]{1,0:T(8,128)(2,1)S(1)} %collective-permute-done.1.refs_2_), channel_id=1, source_target_pairs={{0,16},{16,0},{1,17},{17,1},{2,18},{18,2},{3,19},{19,3},{4,20},{20... | collective-permute-start | bytes 552968 | tf_op jit(solution)/shard_map/ppermute | solution.py:366
  24.3 11.3 %collective-permute-start.7 = (bf16[2880,128]{1,0:T(8,128)(2,1)}, bf16[2880,128]{1,0:T(8,128)(2,1)S(1)}, u32[]{:S(2)}, u32[]{:S(2)}) collective-permute-start(bf16[2880,128]{1,0:T(8,128)(2,1)} %bitcast.13), channel_id=1, source_target_pairs={{0,4},{4,0},{1,5},{5,1},{2,6},{6,2},{3,7},{7,3},{8,12},{12,8},{9,1... | collective-permute-start | bytes 2211848 | tf_op jit(solution)/shard_map/ppermute | solution.py:366
  28.4 7.3 %collective-permute-start.9 = (bf16[2880,128]{1,0:T(8,128)(2,1)S(1)}, bf16[2880,128]{1,0:T(8,128)(2,1)S(1)}, u32[]{:S(2)}, u32[]{:S(2)}) collective-permute-start(bf16[2880,128]{1,0:T(8,128)(2,1)S(1)} %collective-permute-done.8.refs_10_.refs_6_), channel_id=1, source_target_pairs={{0,4},{4,0},{1,5},{5,1},{2,6},{6,2},{3,7},{7,3},{8,12},{12,8},{9,1... | collective-permute-start | bytes 2211848 | tf_op jit(solution)/shard_map/ppermute | solution.py:366
  28.4 7.2 %collective-permute-start.6 = (bf16[32,2880]{1,0:T(8,128)(2,1)S(1)}, bf16[32,2880]{1,0:T(8,128)(2,1)}, u32[]{:S(2)}, u32[]{:S(2)}) collective-permute-start(bf16[32,2880]{1,0:T(8,128)(2,1)S(1)} %collective-permute-done.2.refs_3_), channel_id=1, source_target_pairs={{0,16},{16,0},{1,17},{17,1},{2,18},{18,2},{3,19},{19,3},{4,20},{20... | collective-permute-start | bytes 552968 | tf_op jit(solution)/shard_map/ppermute | solution.py:366
  45.8 39.3 %collective-permute-start.15 = (bf16[256,2944]{1,0:T(8,128)(2,1)}, bf16[256,2944]{1,0:T(8,128)(2,1)}, u32[]{:S(2)}, u32[]{:S(2)}) collective-permute-start(bf16[256,2944]{1,0:T(8,128)(2,1)} %get-tuple-element.48.refs_0_), channel_id=1, source_target_pairs={{0,4},{4,0},{1,5},{5,1},{2,6},{6,2},{3,7},{7,3},{8,12},{12,8},{9,1... | collective-permute-start | bytes 4521992 | tf_op jit(solution)/shard_map/ppermute | solution.py:366
  46.1 39.1 %collective-permute-start.16 = (bf16[256,2944]{1,0:T(8,128)(2,1)}, bf16[256,2944]{1,0:T(8,128)(2,1)}, u32[]{:S(2)}, u32[]{:S(2)}) collective-permute-start(bf16[256,2944]{1,0:T(8,128)(2,1)} %get-tuple-element.48.refs_0_), channel_id=1, source_target_pairs={{0,8},{8,0},{1,9},{9,1},{2,10},{10,2},{3,11},{11,3},{4,12},{12,4},... | collective-permute-start | bytes 4521992 | tf_op jit(solution)/shard_map/ppermute | solution.py:366
  46.6 8.0 %collective-permute-start.13 = (bf16[4,2,128,128]{3,2,1,0:T(8,128)(2,1)S(1)}, bf16[4,2,128,128]{3,2,1,0:T(8,128)(2,1)S(1)}, u32[]{:S(2)}, u32[]{:S(2)}) collective-permute-start(bf16[4,2,128,128]{3,2,1,0:T(8,128)(2,1)S(1)} %arrange.1.own_ref), channel_id=1, source_target_pairs={{0,1},{1,2},{2,3},{3,4},{4,5},{5,6},{6,7},{7,8},{8,9},{9,10},{10,1... | collective-permute-start | bytes 786440 | tf_op jit(solution)/shard_map/ppermute | solution.py:376
  68.2 9.1 %collective-permute-start.14 = (bf16[4,2,128,128]{3,2,1,0:T(8,128)(2,1)S(1)}, bf16[4,2,128,128]{3,2,1,0:T(8,128)(2,1)S(1)}, u32[]{:S(2)}, u32[]{:S(2)}) collective-permute-start(bf16[4,2,128,128]{3,2,1,0:T(8,128)(2,1)S(1)} %get-tuple-element.43), channel_id=1, source_target_pairs={{1,0},{2,1},{3,2},{4,3},{5,4},{6,5},{7,6},{8,7},{9,8},{10,9},{11,1... | collective-permute-start | bytes 786440 | tf_op jit(solution)/shard_map/ppermute | solution.py:376
  78.7 6.5 %collective-permute-start.18 = (bf16[128,256]{1,0:T(8,128)(2,1)S(1)}, bf16[128,256]{1,0:T(8,128)(2,1)S(1)}, u32[]{:S(2)}, u32[]{:S(2)}) collective-permute-start(bf16[128,256]{1,0:T(8,128)(2,1)S(1)} %get-tuple-element.51), channel_id=1, source_target_pairs={{0,4},{4,0},{8,12},{12,8},{1,5},{5,1},{9,13},{13,9},{2,6},{6,2},{1... | collective-permute-start | bytes 196616 | tf_op jit(solution)/shard_map/ppermute | solution.py:370
  81.3 6.5 %collective-permute-start.19 = (bf16[128,256]{1,0:T(8,128)(2,1)S(1)}, bf16[128,256]{1,0:T(8,128)(2,1)S(1)}, u32[]{:S(2)}, u32[]{:S(2)}) collective-permute-start(bf16[128,256]{1,0:T(8,128)(2,1)S(1)} %get-tuple-element.52), channel_id=1, source_target_pairs={{0,8},{4,12},{8,0},{12,4},{1,9},{5,13},{9,1},{13,5},{2,10},{6,14},... | collective-permute-start | bytes 196616 | tf_op jit(solution)/shard_map/ppermute | solution.py:370
  90.9 7.6 %collective-permute-start.21 = (bf16[32,2880]{1,0:T(8,128)(2,1)S(1)}, bf16[32,2880]{1,0:T(8,128)(2,1)S(1)}, u32[]{:S(2)}, u32[]{:S(2)}) collective-permute-start(bf16[32,2880]{1,0:T(8,128)(2,1)S(1)} %get-tuple-element.55), channel_id=1, source_target_pairs={{0,16},{16,0},{1,17},{17,1},{2,18},{18,2},{3,19},{19,3},{4,20},{20... | collective-permute-start | bytes 552968 | tf_op jit(solution)/shard_map/ppermute | solution.py:366
  92.6 10.0 %collective-permute-start.23 = (bf16[32,2880]{1,0:T(8,128)(2,1)S(1)}, bf16[32,2880]{1,0:T(8,128)(2,1)S(1)}, u32[]{:S(2)}, u32[]{:S(2)}) collective-permute-start(bf16[32,2880]{1,0:T(8,128)(2,1)S(1)} %get-tuple-element.57), channel_id=1, source_target_pairs={{0,16},{16,0},{1,17},{17,1},{2,18},{18,2},{3,19},{19,3},{4,20},{20... | collective-permute-start | bytes 552968 | tf_op jit(solution)/shard_map/ppermute | solution.py:366
  93.0 12.8 %collective-permute-start.25 = (bf16[32,2880]{1,0:T(8,128)(2,1)S(1)}, bf16[32,2880]{1,0:T(8,128)(2,1)S(1)}, u32[]{:S(2)}, u32[]{:S(2)}) collective-permute-start(bf16[32,2880]{1,0:T(8,128)(2,1)S(1)} %get-tuple-element.59), channel_id=1, source_target_pairs={{0,16},{16,0},{1,17},{17,1},{2,18},{18,2},{3,19},{19,3},{4,20},{20... | collective-permute-start | bytes 552968 | tf_op jit(solution)/shard_map/ppermute | solution.py:366
  94.6 13.1 %collective-permute-start.17 = (bf16[256,2944]{1,0:T(8,128)(2,1)}, bf16[256,2944]{1,0:T(8,128)(2,1)S(1)}, u32[]{:S(2)}, u32[]{:S(2)}) collective-permute-start(bf16[256,2944]{1,0:T(8,128)(2,1)} %collective-permute-done.16.refs_2_), channel_id=1, source_target_pairs={{0,4},{4,0},{1,5},{5,1},{2,6},{6,2},{3,7},{7,3},{8,12},{12,8},{9,1... | collective-permute-start | bytes 4521992 | tf_op jit(solution)/shard_map/ppermute | solution.py:366
  98.6 15.1 %collective-permute-start.22 = (bf16[32,2880]{1,0:T(8,128)(2,1)S(1)}, bf16[32,2880]{1,0:T(8,128)(2,1)S(1)}, u32[]{:S(2)}, u32[]{:S(2)}) collective-permute-start(bf16[32,2880]{1,0:T(8,128)(2,1)S(1)} %add_convert_fusion.2), channel_id=1, source_target_pairs={{0,3},{1,2},{2,1},{3,0},{4,7},{5,6},{6,5},{7,4},{8,11},{9,10},{10,... | collective-permute-start | bytes 552968 | tf_op jit(solution)/shard_map/ppermute | solution.py:366
  102.6 12.8 %collective-permute-start.24 = (bf16[32,2880]{1,0:T(8,128)(2,1)S(1)}, bf16[32,2880]{1,0:T(8,128)(2,1)S(1)}, u32[]{:S(2)}, u32[]{:S(2)}) collective-permute-start(bf16[32,2880]{1,0:T(8,128)(2,1)S(1)} %add_convert_fusion.1), channel_id=1, source_target_pairs={{0,2},{1,3},{2,0},{3,1},{4,6},{5,7},{6,4},{7,5},{8,10},{9,11},{10,... | collective-permute-start | bytes 552968 | tf_op jit(solution)/shard_map/ppermute | solution.py:366
  105.9 10.0 %collective-permute-start.26 = (bf16[32,2880]{1,0:T(8,128)(2,1)S(1)}, bf16[32,2880]{1,0:T(8,128)(2,1)S(1)}, u32[]{:S(2)}, u32[]{:S(2)}) collective-permute-start(bf16[32,2880]{1,0:T(8,128)(2,1)S(1)} %add_convert_fusion), channel_id=1, source_target_pairs={{0,1},{1,0},{2,3},{3,2},{4,5},{5,4},{6,7},{7,6},{8,9},{9,8},{10,11... | collective-permute-start | bytes 552968 | tf_op jit(solution)/shard_map/ppermute | solution.py:366
  107.2 8.7 %collective-permute-start.27 = (bf16[32,2880]{1,0:T(8,128)(2,1)S(1)}, bf16[32,2880]{1,0:T(8,128)(2,1)S(1)}, u32[]{:S(2)}, u32[]{:S(2)}) collective-permute-start(bf16[32,2880]{1,0:T(8,128)(2,1)S(1)} %get-tuple-element.63), channel_id=1, source_target_pairs={{0,16},{16,0},{1,17},{17,1},{2,18},{18,2},{3,19},{19,3},{4,20},{20... | collective-permute-start | bytes 552968 | tf_op jit(solution)/shard_map/ppermute | solution.py:366
  (8 other events, 51.4 us)

commit v4 on v3

--- a/solution.py
+++ b/solution.py
@@ -35,6 +35,7 @@
 
 
 VMEM = pl.BlockSpec(memory_space=pltpu.VMEM)
+HBM = pl.BlockSpec(memory_space=pltpu.HBM)
 
 
 def entire(array):
@@ -88,9 +89,34 @@
     )
 
 
-def attention_kernel(first_ref, q_ref, go_ref, own_ref, halo_ref, *refs):
-    gq_ref, sums_ref, back_ref = refs[-3:]
+def attention_kernel(at, first_ref, queries_ref, grads_ref, own_ref, halo_ref, *refs):
+    gq_ref, sums_ref, back_ref, q_buffer, go_buffer, sems = refs[-6:]
     rows = own_ref.shape[2]
+    width = q_buffer.shape[2]
+    now = pl.program_id(0) * 2 + pl.program_id(1)
+
+    def fetches(turn):
+        slot = turn % 2
+        col = ((turn % 2) * QUARTERS + at + turn // 2) * width
+        cols = pl.ds(pl.multiple_of(col, width), width)
+        return [
+            pltpu.make_async_copy(ref.at[:, cols], buffer.at[slot], sems.at[slot, k])
+            for k, (ref, buffer) in enumerate(((queries_ref, q_buffer), (grads_ref, go_buffer)))
+        ]
+
+    @pl.when(now == 0)
+    def _():
+        for copy in fetches(now):
+            copy.start()
+
+    @pl.when(now + 1 < pl.num_programs(0) * 2)
+    def _():
+        for copy in fetches(now + 1):
+            copy.start()
+
+    for copy in fetches(now):
+        copy.wait()
+    q_ref, go_ref = q_buffer.at[now % 2], go_buffer.at[now % 2]
     later, same = both_triangles(rows, 2 * rows, jnp.int32)
     later_low, same_low = both_triangles(rows, 2 * rows, jnp.int16)
     zero = jnp.zeros((), BF16)
@@ -118,9 +144,9 @@
         return mixed, jnp.sum(jnp.where(same, halo, 0.0), axis=0, keepdims=True)
 
     hidden = jnp.where(later, shift, 0.0)
-    for step in range(q_ref.shape[1] // (2 * LANES)):
-        at = step * 2 * LANES
-        q_pair, go_pair = pair_of_blocks(q_ref, at), pair_of_blocks(go_ref, at)
+    for step in range(width // (2 * LANES)):
+        left = step * 2 * LANES
+        q_pair, go_pair = pair_of_blocks(q_ref, left), pair_of_blocks(go_ref, left)
         scores = lax.dot_general(keys, q_pair, NT, preferred_element_type=F32)
         grads = lax.dot_general(values, go_pair, NT, preferred_element_type=F32)
         weights, terms = [], []
@@ -145,7 +171,7 @@
         across = jnp.dot(keys_across, stack, preferred_element_type=F32)
         for part in range(2):
             block = across[:, part * rows : (part + 1) * rows].T * factor
-            gq_ref[:, at + part * LANES : at + (part + 1) * LANES] = block.astype(BF16)
+            gq_ref[:, left + part * LANES : left + (part + 1) * LANES] = block.astype(BF16)
     own, back = folded(key_total * factor)
     store_half(sums_ref, 0, own, half)
     store_half(back_ref, 0, back, half)
@@ -161,11 +187,16 @@
     by_quarter = pl.BlockSpec((1,) + own.shape[1:], lambda q, h: (q, 0, 0, 0))
     more = [] if before is None else [before]
     return pl.pallas_call(
-        attention_kernel,
+        functools.partial(attention_kernel, at),
         grid=(own.shape[0], 2),
-        in_specs=[SMEM] + [by_head] * 2 + [by_quarter] * 2 + [pl.BlockSpec(memory_space=pl.ANY)] * len(more),
+        in_specs=[SMEM, HBM, HBM, by_quarter, by_quarter] + [HBM] * len(more),
         out_specs=[by_head, by_quarter, by_quarter],
         out_shape=[struct(queries.shape, BF16), sums, back],
+        scratch_shapes=[
+            pltpu.VMEM((2, rows, width // KV_HEADS), BF16),
+            pltpu.VMEM((2, rows, width // KV_HEADS), BF16),
+            pltpu.SemaphoreType.DMA((2, 2)),
+        ],
         input_output_aliases={5: 0} if more else {},
         compiler_params=params(20),
         cost_estimate=cost(5 * own.shape[0] * rows * rows * width, queries, grad_out),
@@ -389,9 +420,10 @@
     pieces = [jnp.concatenate([key_weight.T, value_weight.T], axis=0)]
     own = after(hidden_in.T, pieces[0])
     x_side = flip(own, "x", 1)
-    pieces += [flip(pieces[0], "z", k) for k in range(1, depth)]
+    pieces += [flip(pieces[0], "z", 1), flip(pieces[0], "z", 2)]
+    pieces.append(flip(pieces[2], "z", 1))
     across = [flip(piece, "hi", 1) for piece in pieces]
-    x_side = after(x_side, pieces[-1], *across[: depth - 1])
+    x_side = after(x_side, *pieces, *across[:2])
     hidden = [own, flip(own, "c", 1), x_side, flip(x_side, "c", 1)]
     mine, *parts = project(place, pieces + across, hidden)
     chunks = 1

time: 117 us -> 116 us (level)
  waiting for transfers between devices: 51.9 us -> 49.3 us
  starting transfers between devices: 34.9 us -> 36.1 us
    ppermute x20, waiting for transfers between devices: 29.8 us -> 26.9 us  [flip(): lax.ppermute(array, axis, [(i, i ^ by) for i in range(lax.axis_size(axis))])]
    ppermute x6, starting transfers between devices: 8.36 us -> 6.03 us  [flip_group(): lax.ppermute(array, ('x', 'c'), [(i, i ^ by) for i in range(QUARTERS)])]
    ppermute x2, starting transfers between devices: 2.64 us -> 4.47 us  [shifted(): return lax.ppermute(array, AXES, pairs)]
    ppermute x20, starting transfers between devices: 23.9 us -> 25.6 us  [flip(): lax.ppermute(array, axis, [(i, i ^ by) for i in range(lax.axis_size(axis))])]
where the time goes in v4:
time: 116 us
  waiting for transfers between devices  49.3 us (42%)
  starting transfers between devices  36.1 us (31%)
  Pallas kernels  23.9 us (21%)
  local copies, waits for them, and re-layouts  4.33 us (4%)
  other arithmetic  1.3 us (1%)
    ppermute x20, waiting for transfers between devices, flip(): lax.ppermute(array, axis, [(i, i ^ by) for i in range(lax.axis_size(axis))])  26.9 us
    ppermute x20, starting transfers between devices, flip(): lax.ppermute(array, axis, [(i, i ^ by) for i in range(lax.axis_size(axis))])  25.6 us
    ppermute x2, waiting for transfers between devices, shifted(): return lax.ppermute(array, AXES, pairs)  14.9 us
    pallas_call x1, Pallas kernels, attention(): pl.pallas_call(functools.partial(attention_kernel, at), grid=(own.shape[0...  11.4 us
    ppermute x6, waiting for transfers between devices, flip_group(): lax.ppermute(array, ('x', 'c'), [(i, i ^ by) for i in range(QUARTERS)])  7.57 us
    ppermute x6, starting transfers between devices, flip_group(): lax.ppermute(array, ('x', 'c'), [(i, i ^ by) for i in range(QUARTERS)])  6.03 us
    pallas_call x1, Pallas kernels, input_grad(): pl.pallas_call(input_grad_kernel, grid=(-(-size // step),), in_specs=[SME...  5.91 us
    ppermute x2, starting transfers between devices, shifted(): return lax.ppermute(array, AXES, pairs)  4.47 us
  transfers between devices with their start and end apart: 28, of which 15 were waited for; matrix products, arithmetic and copies ran while one was open for 0% of the time, Pallas kernels for 16%

profile of v4, /device:TPU:0, one launch (start us, length us, event | category | flops | bytes accessed | tf_op | source)
XLA Modules:
  0.0 115.7 jit_solution(13202758457006295088)
XLA Ops:
  1.6 3.0 %collective-permute-start.8 = (bf16[2880,128]{1,0:T(8,128)(2,1)}, bf16[2880,128]{1,0:T(8,128)(2,1)S(1)}, u32[]{:S(2)}, u32[]{:S(2)}) collective-permute-start(bf16[2880,128]{1,0:T(8,128)(2,1)} %bitcast.12), channel_id=1, source_target_pairs={{0,8},{8,0},{1,9},{9,1},{2,10},{10,2},{3,11},{11,3},{4,12},{12,4},... | collective-permute-start | bytes 2211848 | tf_op jit(solution)/shard_map/ppermute | solution.py:397
  4.6 2.6 %collective-permute-start.1 = (bf16[32,2880]{1,0:T(8,128)(2,1)S(1)}, bf16[32,2880]{1,0:T(8,128)(2,1)S(1)}, u32[]{:S(2)}, u32[]{:S(2)}) collective-permute-start(bf16[32,2880]{1,0:T(8,128)(2,1)S(1)} %pad_maximum_fusion.refs_0_), channel_id=1, source_target_pairs={{0,2},{1,3},{2,0},{3,1},{4,6},{5,7},{6,4},{7,5},{8,10},{9,11},{10,... | collective-permute-start | bytes 552968 | tf_op jit(solution)/shard_map/ppermute | solution.py:397
  7.2 1.6 %collective-permute-start = (bf16[32,2880]{1,0:T(8,128)(2,1)S(1)}, bf16[32,2880]{1,0:T(8,128)(2,1)S(1)}, u32[]{:S(2)}, u32[]{:S(2)}) collective-permute-start(bf16[32,2880]{1,0:T(8,128)(2,1)S(1)} %pad_maximum_fusion.refs_0_), channel_id=1, source_target_pairs={{0,1},{1,0},{2,3},{3,2},{4,5},{5,4},{6,7},{7,6},{8,9},{9,8},{10,11... | collective-permute-start | bytes 552968 | tf_op jit(solution)/shard_map/ppermute | solution.py:397
  10.3 5.5 %collective-permute-done.1.refs_2_ = bf16[32,2880]{1,0:T(8,128)(2,1)S(1)} collective-permute-done((bf16[32,2880]{1,0:T(8,128)(2,1)S(1)}, bf16[32,2880]{1,0:T(8,128)(2,1)S(1)}, u32[]{:S(2)}, u32[]{:S(2)}) %collective-permute-start.1) | collective-permute-done | bytes 184352 | tf_op jit(solution)/shard_map/ppermute | solution.py:397
  17.9 3.5 %collective-permute-done.2.refs_3_ = bf16[32,2880]{1,0:T(8,128)(2,1)S(1)} collective-permute-done((bf16[32,2880]{1,0:T(8,128)(2,1)S(1)}, bf16[32,2880]{1,0:T(8,128)(2,1)S(1)}, u32[]{:S(2)}, u32[]{:S(2)}) %collective-permute-start.2) | collective-permute-done | bytes 184352 | tf_op jit(solution)/shard_map/ppermute | solution.py:397
  22.8 1.5 %collective-permute-start.5 = (bf16[32,2880]{1,0:T(8,128)(2,1)S(1)}, bf16[32,2880]{1,0:T(8,128)(2,1)S(1)}, u32[]{:S(2)}, u32[]{:S(2)}) collective-permute-start(bf16[32,2880]{1,0:T(8,128)(2,1)S(1)} %collective-permute-done.1.refs_2_), channel_id=1, source_target_pairs={{0,16},{16,0},{1,17},{17,1},{2,18},{18,2},{3,19},{19,3},{4,20},{20... | collective-permute-start | bytes 552968 | tf_op jit(solution)/shard_map/ppermute | solution.py:397
  24.9 5.4 %collective-permute-done.5.refs_6_ = bf16[32,2880]{1,0:T(8,128)(2,1)S(1)} collective-permute-done((bf16[32,2880]{1,0:T(8,128)(2,1)S(1)}, bf16[32,2880]{1,0:T(8,128)(2,1)S(1)}, u32[]{:S(2)}, u32[]{:S(2)}) %collective-permute-start.5) | collective-permute-done | bytes 184352 | tf_op jit(solution)/shard_map/ppermute | solution.py:397
  30.3 3.8 %collective-permute-done.6.refs_7_ = bf16[32,2880]{1,0:T(8,128)(2,1)} collective-permute-done((bf16[32,2880]{1,0:T(8,128)(2,1)S(1)}, bf16[32,2880]{1,0:T(8,128)(2,1)}, u32[]{:S(2)}, u32[]{:S(2)}) %collective-permute-start.6) | collective-permute-done | bytes 184352 | tf_op jit(solution)/shard_map/ppermute | solution.py:397
  35.2 2.9 %project.1 = (bf16[256,2944]{1,0:T(8,128)(2,1)}, bf16[128,256]{1,0:T(8,128)(2,1)S(1)}, bf16[128,256]{1,0:T(8,128)(2,1)S(1)}, bf16[128,256]{1,0:T(8,128)(2,1)S(1)}, bf16[128,256]{1,0:T(8,128)(2,1)S(1)}) custom-call(s32[3]{0:T(128)S(1)} %pad_add_fusion.place_ref, bf16[32,2880]{1,0:T(8,128)(2,1)S(1)} %pad_maximum_fusion.refs_0_, ...), custom_call_target="tpu_custom_call" | custom-call | flops 754974720 | bytes 5963776 | tf_op jit(solution)/shard_map/project/pallas_call | solution.py:236
  39.9 3.0 %collective-permute-done.11.refs_2_ = bf16[128,256]{1,0:T(8,128)(2,1)S(1)} collective-permute-done((bf16[128,256]{1,0:T(8,128)(2,1)S(1)}, bf16[128,256]{1,0:T(8,128)(2,1)S(1)}, u32[]{:S(2)}, u32[]{:S(2)}) %collective-permute-start.11) | collective-permute-done | bytes 65568 | tf_op jit(solution)/shard_map/ppermute | solution.py:401
  45.1 3.2 %collective-permute-start.13 = (bf16[4,2,128,128]{3,2,1,0:T(8,128)(2,1)S(1)}, bf16[4,2,128,128]{3,2,1,0:T(8,128)(2,1)S(1)}, u32[]{:S(2)}, u32[]{:S(2)}) collective-permute-start(bf16[4,2,128,128]{3,2,1,0:T(8,128)(2,1)S(1)} %arrange.1.own_ref), channel_id=1, source_target_pairs={{0,1},{1,2},{2,3},{3,4},{4,5},{5,6},{6,7},{7,8},{8,9},{9,10},{10,1... | collective-permute-start | bytes 786440 | tf_op jit(solution)/shard_map/ppermute | solution.py:407
  48.3 5.7 %collective-permute-done.13.halo_ref = bf16[4,2,128,128]{3,2,1,0:T(8,128)(2,1)S(1)} collective-permute-done((bf16[4,2,128,128]{3,2,1,0:T(8,128)(2,1)S(1)}, bf16[4,2,128,128]{3,2,1,0:T(8,128)(2,1)S(1)}, u32[]{:S(2)}, u32[]{:S(2)}) %collective-permute-start.13) | collective-permute-done | bytes 262176 | tf_op jit(solution)/shard_map/ppermute | solution.py:407
  56.4 11.4 %attention.1 = (bf16[128,4096]{1,0:T(8,128)(2,1)}, f32[4,2,128,128]{3,2,1,0:T(8,128)S(1)}, bf16[4,2,128,128]{3,2,1,0:T(8,128)(2,1)S(1)}) custom-call(s32[1]{0:T(128)} %bitcast.first_ref, bf16[128,4096]{1,0:T(8,128)(2,1)S(1)} %copy-done.2, bf16[128,4096]{1,0:T(8,128)(2,1)S(1)} %copy-done.3, bf16[4,2,128,128]{3,2,1,0:T(8,128)(2,1)S(1)} %arrange.1.own_ref, ...), custom_call_target="tpu_custom_call" | custom-call | flops 1342177280 | bytes 2097152 | tf_op jit(solution)/shard_map/attention/pallas_call | solution.py:189
  69.1 9.2 %collective-permute-done.14.refs_1_ = bf16[4,2,128,128]{3,2,1,0:T(8,128)(2,1)S(1)} collective-permute-done((bf16[4,2,128,128]{3,2,1,0:T(8,128)(2,1)S(1)}, bf16[4,2,128,128]{3,2,1,0:T(8,128)(2,1)S(1)}, u32[]{:S(2)}, u32[]{:S(2)}) %collective-permute-start.14) | collective-permute-done | bytes 262176 | tf_op jit(solution)/shard_map/ppermute | solution.py:407
  81.1 2.5 %collective-permute-start.19 = (bf16[128,256]{1,0:T(8,128)(2,1)S(1)}, bf16[128,256]{1,0:T(8,128)(2,1)S(1)}, u32[]{:S(2)}, u32[]{:S(2)}) collective-permute-start(bf16[128,256]{1,0:T(8,128)(2,1)S(1)} %get-tuple-element.52), channel_id=1, source_target_pairs={{0,8},{4,12},{8,0},{12,4},{1,9},{5,13},{9,1},{13,5},{2,10},{6,14},... | collective-permute-start | bytes 196616 | tf_op jit(solution)/shard_map/ppermute | solution.py:401
  83.8 2.6 %collective-permute-done.19.refs_2_ = bf16[128,256]{1,0:T(8,128)(2,1)S(1)} collective-permute-done((bf16[128,256]{1,0:T(8,128)(2,1)S(1)}, bf16[128,256]{1,0:T(8,128)(2,1)S(1)}, u32[]{:S(2)}, u32[]{:S(2)}) %collective-permute-start.19) | collective-permute-done | bytes 65568 | tf_op jit(solution)/shard_map/ppermute | solution.py:401
  87.7 1.8 %weight_grad.1 = (bf16[32,2880]{1,0:T(8,128)(2,1)S(1)}, bf16[32,2880]{1,0:T(8,128)(2,1)S(1)}, bf16[32,2880]{1,0:T(8,128)(2,1)S(1)}, bf16[32,2880]{1,0:T(8,128)(2...) custom-call(s32[3]{0:T(128)S(1)} %pad_add_fusion.place_ref, ...), custom_call_target="tpu_custom_call" | custom-call | flops 754974720 | bytes 5898240 | tf_op jit(solution)/shard_map/weight_grad/pallas_call | solution.py:354
  89.5 1.9 %collective-permute-start.21 = (bf16[32,2880]{1,0:T(8,128)(2,1)S(1)}, bf16[32,2880]{1,0:T(8,128)(2,1)S(1)}, u32[]{:S(2)}, u32[]{:S(2)}) collective-permute-start(bf16[32,2880]{1,0:T(8,128)(2,1)S(1)} %get-tuple-element.55), channel_id=1, source_target_pairs={{0,16},{16,0},{1,17},{17,1},{2,18},{18,2},{3,19},{19,3},{4,20},{20... | collective-permute-start | bytes 552968 | tf_op jit(solution)/shard_map/ppermute | solution.py:397
  91.6 1.8 %collective-permute-start.25 = (bf16[32,2880]{1,0:T(8,128)(2,1)S(1)}, bf16[32,2880]{1,0:T(8,128)(2,1)S(1)}, u32[]{:S(2)}, u32[]{:S(2)}) collective-permute-start(bf16[32,2880]{1,0:T(8,128)(2,1)S(1)} %get-tuple-element.59), channel_id=1, source_target_pairs={{0,16},{16,0},{1,17},{17,1},{2,18},{18,2},{3,19},{19,3},{4,20},{20... | collective-permute-start | bytes 552968 | tf_op jit(solution)/shard_map/ppermute | solution.py:397
  93.4 3.7 %collective-permute-done.21 = bf16[32,2880]{1,0:T(8,128)(2,1)S(1)} collective-permute-done((bf16[32,2880]{1,0:T(8,128)(2,1)S(1)}, bf16[32,2880]{1,0:T(8,128)(2,1)S(1)}, u32[]{:S(2)}, u32[]{:S(2)}) %collective-permute-start.21) | collective-permute-done | bytes 184352 | tf_op jit(solution)/shard_map/ppermute | solution.py:397
  97.2 5.0 %collective-permute-start.22 = (bf16[32,2880]{1,0:T(8,128)(2,1)S(1)}, bf16[32,2880]{1,0:T(8,128)(2,1)S(1)}, u32[]{:S(2)}, u32[]{:S(2)}) collective-permute-start(bf16[32,2880]{1,0:T(8,128)(2,1)S(1)} %add_convert_fusion.2), channel_id=1, source_target_pairs={{0,3},{1,2},{2,1},{3,0},{4,7},{5,6},{6,5},{7,4},{8,11},{9,10},{10,... | collective-permute-start | bytes 552968 | tf_op jit(solution)/shard_map/ppermute | solution.py:397
  102.5 2.1 %collective-permute-done.25 = bf16[32,2880]{1,0:T(8,128)(2,1)S(1)} collective-permute-done((bf16[32,2880]{1,0:T(8,128)(2,1)S(1)}, bf16[32,2880]{1,0:T(8,128)(2,1)S(1)}, u32[]{:S(2)}, u32[]{:S(2)}) %collective-permute-start.25) | collective-permute-done | bytes 184352 | tf_op jit(solution)/shard_map/ppermute | solution.py:397
  104.6 2.3 %collective-permute-start.26 = (bf16[32,2880]{1,0:T(8,128)(2,1)S(1)}, bf16[32,2880]{1,0:T(8,128)(2,1)S(1)}, u32[]{:S(2)}, u32[]{:S(2)}) collective-permute-start(bf16[32,2880]{1,0:T(8,128)(2,1)S(1)} %add_convert_fusion), channel_id=1, source_target_pairs={{0,1},{1,0},{2,3},{3,2},{4,5},{5,4},{6,7},{7,6},{8,9},{9,8},{10,11... | collective-permute-start | bytes 552968 | tf_op jit(solution)/shard_map/ppermute | solution.py:397
  107.4 5.9 %input_grad.1 = bf16[2880,128]{1,0:T(8,128)(2,1)} custom-call(s32[3]{0:T(128)S(1)} %pad_add_fusion.place_ref, bf16[4,128,256]{2,1,0:T(8,128)(2,1)S(1)} %get-tuple-element.46.all_ref, bf16[256,2944]{1,0:T(8,128)(2,1)} %get-tuple-element.48.refs_0_, bf16[256,2944]{1,0:T(8,128)(2,1)} %collective-permute-done.15.refs_1_, ...), custom_call_target="tpu_custom_call" | custom-call | flops 754974720 | bytes 6766592 | tf_op jit(solution)/shard_map/input_grad/pallas_call | solution.py:379
  (53 shorter events, 23.2 us)
Async XLA Ops:
  1.6 21.2 %collective-permute-start.8 = (bf16[2880,128]{1,0:T(8,128)(2,1)}, bf16[2880,128]{1,0:T(8,128)(2,1)S(1)}, u32[]{:S(2)}, u32[]{:S(2)}) collective-permute-start(bf16[2880,128]{1,0:T(8,128)(2,1)} %bitcast.12), channel_id=1, source_target_pairs={{0,8},{8,0},{1,9},{9,1},{2,10},{10,2},{3,11},{11,3},{4,12},{12,4},... | collective-permute-start | bytes 2211848 | tf_op jit(solution)/shard_map/ppermute | solution.py:397
  4.6 11.2 %collective-permute-start.1 = (bf16[32,2880]{1,0:T(8,128)(2,1)S(1)}, bf16[32,2880]{1,0:T(8,128)(2,1)S(1)}, u32[]{:S(2)}, u32[]{:S(2)}) collective-permute-start(bf16[32,2880]{1,0:T(8,128)(2,1)S(1)} %pad_maximum_fusion.refs_0_), channel_id=1, source_target_pairs={{0,2},{1,3},{2,0},{3,1},{4,6},{5,7},{6,4},{7,5},{8,10},{9,11},{10,... | collective-permute-start | bytes 552968 | tf_op jit(solution)/shard_map/ppermute | solution.py:397
  7.2 9.2 %collective-permute-start = (bf16[32,2880]{1,0:T(8,128)(2,1)S(1)}, bf16[32,2880]{1,0:T(8,128)(2,1)S(1)}, u32[]{:S(2)}, u32[]{:S(2)}) collective-permute-start(bf16[32,2880]{1,0:T(8,128)(2,1)S(1)} %pad_maximum_fusion.refs_0_), channel_id=1, source_target_pairs={{0,1},{1,0},{2,3},{3,2},{4,5},{5,4},{6,7},{7,6},{8,9},{9,8},{10,11... | collective-permute-start | bytes 552968 | tf_op jit(solution)/shard_map/ppermute | solution.py:397
  8.8 9.2 %collective-permute-start.3 = (bf16[32,2880]{1,0:T(8,128)(2,1)S(1)}, bf16[32,2880]{1,0:T(8,128)(2,1)S(1)}, u32[]{:S(2)}, u32[]{:S(2)}) collective-permute-start(bf16[32,2880]{1,0:T(8,128)(2,1)S(1)} %pad_maximum_fusion.refs_0_), channel_id=1, source_target_pairs={{0,16},{16,0},{1,17},{17,1},{2,18},{18,2},{3,19},{19,3},{4,20},{20... | collective-permute-start | bytes 552968 | tf_op jit(solution)/shard_map/ppermute | solution.py:397
  15.8 5.6 %collective-permute-start.2 = (bf16[32,2880]{1,0:T(8,128)(2,1)S(1)}, bf16[32,2880]{1,0:T(8,128)(2,1)S(1)}, u32[]{:S(2)}, u32[]{:S(2)}) collective-permute-start(bf16[32,2880]{1,0:T(8,128)(2,1)S(1)} %collective-permute-done.1.refs_2_), channel_id=1, source_target_pairs={{0,1},{1,0},{2,3},{3,2},{4,5},{5,4},{6,7},{7,6},{8,9},{9,8},{10,11... | collective-permute-start | bytes 552968 | tf_op jit(solution)/shard_map/ppermute | solution.py:397
  16.4 6.4 %collective-permute-start.4 = (bf16[32,2880]{1,0:T(8,128)(2,1)S(1)}, bf16[32,2880]{1,0:T(8,128)(2,1)S(1)}, u32[]{:S(2)}, u32[]{:S(2)}) collective-permute-start(bf16[32,2880]{1,0:T(8,128)(2,1)S(1)} %collective-permute-done.refs_1_), channel_id=1, source_target_pairs={{0,16},{16,0},{1,17},{17,1},{2,18},{18,2},{3,19},{19,3},{4,20},{20... | collective-permute-start | bytes 552968 | tf_op jit(solution)/shard_map/ppermute | solution.py:397
  17.9 16.1 %collective-permute-start.7 = (bf16[2880,128]{1,0:T(8,128)(2,1)}, bf16[2880,128]{1,0:T(8,128)(2,1)S(1)}, u32[]{:S(2)}, u32[]{:S(2)}) collective-permute-start(bf16[2880,128]{1,0:T(8,128)(2,1)} %bitcast.13), channel_id=1, source_target_pairs={{0,4},{4,0},{1,5},{5,1},{2,6},{6,2},{3,7},{7,3},{8,12},{12,8},{9,1... | collective-permute-start | bytes 2211848 | tf_op jit(solution)/shard_map/ppermute | solution.py:397
  22.8 11.3 %collective-permute-start.9 = (bf16[2880,128]{1,0:T(8,128)(2,1)S(1)}, bf16[2880,128]{1,0:T(8,128)(2,1)S(1)}, u32[]{:S(2)}, u32[]{:S(2)}) collective-permute-start(bf16[2880,128]{1,0:T(8,128)(2,1)S(1)} %collective-permute-done.8.refs_10_.refs_6_), channel_id=1, source_target_pairs={{0,4},{4,0},{1,5},{5,1},{2,6},{6,2},{3,7},{7,3},{8,12},{12,8},{9,1... | collective-permute-start | bytes 2211848 | tf_op jit(solution)/shard_map/ppermute | solution.py:397
  22.8 7.5 %collective-permute-start.5 = (bf16[32,2880]{1,0:T(8,128)(2,1)S(1)}, bf16[32,2880]{1,0:T(8,128)(2,1)S(1)}, u32[]{:S(2)}, u32[]{:S(2)}) collective-permute-start(bf16[32,2880]{1,0:T(8,128)(2,1)S(1)} %collective-permute-done.1.refs_2_), channel_id=1, source_target_pairs={{0,16},{16,0},{1,17},{17,1},{2,18},{18,2},{3,19},{19,3},{4,20},{20... | collective-permute-start | bytes 552968 | tf_op jit(solution)/shard_map/ppermute | solution.py:397
  24.3 9.8 %collective-permute-start.6 = (bf16[32,2880]{1,0:T(8,128)(2,1)S(1)}, bf16[32,2880]{1,0:T(8,128)(2,1)}, u32[]{:S(2)}, u32[]{:S(2)}) collective-permute-start(bf16[32,2880]{1,0:T(8,128)(2,1)S(1)} %collective-permute-done.2.refs_3_), channel_id=1, source_target_pairs={{0,16},{16,0},{1,17},{17,1},{2,18},{18,2},{3,19},{19,3},{4,20},{20... | collective-permute-start | bytes 552968 | tf_op jit(solution)/shard_map/ppermute | solution.py:397
  38.6 5.0 %collective-permute-start.12 = (bf16[128,256]{1,0:T(8,128)(2,1)S(1)}, bf16[128,256]{1,0:T(8,128)(2,1)S(1)}, u32[]{:S(2)}, u32[]{:S(2)}) collective-permute-start(bf16[128,256]{1,0:T(8,128)(2,1)S(1)} %get-tuple-element.40), channel_id=1, source_target_pairs={{0,12},{4,8},{8,4},{12,0},{1,13},{5,9},{9,5},{13,1},{2,14},{6,10},... | collective-permute-start | bytes 196616 | tf_op jit(solution)/shard_map/ppermute | solution.py:401
  44.2 39.6 %collective-permute-start.15 = (bf16[256,2944]{1,0:T(8,128)(2,1)}, bf16[256,2944]{1,0:T(8,128)(2,1)}, u32[]{:S(2)}, u32[]{:S(2)}) collective-permute-start(bf16[256,2944]{1,0:T(8,128)(2,1)} %get-tuple-element.48.refs_0_), channel_id=1, source_target_pairs={{0,4},{4,0},{1,5},{5,1},{2,6},{6,2},{3,7},{7,3},{8,12},{12,8},{9,1... | collective-permute-start | bytes 4521992 | tf_op jit(solution)/shard_map/ppermute | solution.py:397
  44.5 39.3 %collective-permute-start.16 = (bf16[256,2944]{1,0:T(8,128)(2,1)}, bf16[256,2944]{1,0:T(8,128)(2,1)}, u32[]{:S(2)}, u32[]{:S(2)}) collective-permute-start(bf16[256,2944]{1,0:T(8,128)(2,1)} %get-tuple-element.48.refs_0_), channel_id=1, source_target_pairs={{0,8},{8,0},{1,9},{9,1},{2,10},{10,2},{3,11},{11,3},{4,12},{12,4},... | collective-permute-start | bytes 4521992 | tf_op jit(solution)/shard_map/ppermute | solution.py:397
  45.1 8.9 %collective-permute-start.13 = (bf16[4,2,128,128]{3,2,1,0:T(8,128)(2,1)S(1)}, bf16[4,2,128,128]{3,2,1,0:T(8,128)(2,1)S(1)}, u32[]{:S(2)}, u32[]{:S(2)}) collective-permute-start(bf16[4,2,128,128]{3,2,1,0:T(8,128)(2,1)S(1)} %arrange.1.own_ref), channel_id=1, source_target_pairs={{0,1},{1,2},{2,3},{3,4},{4,5},{5,6},{6,7},{7,8},{8,9},{9,10},{10,1... | collective-permute-start | bytes 786440 | tf_op jit(solution)/shard_map/ppermute | solution.py:407
  67.8 10.5 %collective-permute-start.14 = (bf16[4,2,128,128]{3,2,1,0:T(8,128)(2,1)S(1)}, bf16[4,2,128,128]{3,2,1,0:T(8,128)(2,1)S(1)}, u32[]{:S(2)}, u32[]{:S(2)}) collective-permute-start(bf16[4,2,128,128]{3,2,1,0:T(8,128)(2,1)S(1)} %get-tuple-element.43), channel_id=1, source_target_pairs={{1,0},{2,1},{3,2},{4,3},{5,4},{6,5},{7,6},{8,7},{9,8},{10,9},{11,1... | collective-permute-start | bytes 786440 | tf_op jit(solution)/shard_map/ppermute | solution.py:407
  81.1 5.3 %collective-permute-start.19 = (bf16[128,256]{1,0:T(8,128)(2,1)S(1)}, bf16[128,256]{1,0:T(8,128)(2,1)S(1)}, u32[]{:S(2)}, u32[]{:S(2)}) collective-permute-start(bf16[128,256]{1,0:T(8,128)(2,1)S(1)} %get-tuple-element.52), channel_id=1, source_target_pairs={{0,8},{4,12},{8,0},{12,4},{1,9},{5,13},{9,1},{13,5},{2,10},{6,14},... | collective-permute-start | bytes 196616 | tf_op jit(solution)/shard_map/ppermute | solution.py:401
  89.5 7.6 %collective-permute-start.21 = (bf16[32,2880]{1,0:T(8,128)(2,1)S(1)}, bf16[32,2880]{1,0:T(8,128)(2,1)S(1)}, u32[]{:S(2)}, u32[]{:S(2)}) collective-permute-start(bf16[32,2880]{1,0:T(8,128)(2,1)S(1)} %get-tuple-element.55), channel_id=1, source_target_pairs={{0,16},{16,0},{1,17},{17,1},{2,18},{18,2},{3,19},{19,3},{4,20},{20... | collective-permute-start | bytes 552968 | tf_op jit(solution)/shard_map/ppermute | solution.py:397
  91.4 10.8 %collective-permute-start.23 = (bf16[32,2880]{1,0:T(8,128)(2,1)S(1)}, bf16[32,2880]{1,0:T(8,128)(2,1)S(1)}, u32[]{:S(2)}, u32[]{:S(2)}) collective-permute-start(bf16[32,2880]{1,0:T(8,128)(2,1)S(1)} %get-tuple-element.57), channel_id=1, source_target_pairs={{0,16},{16,0},{1,17},{17,1},{2,18},{18,2},{3,19},{19,3},{4,20},{20... | collective-permute-start | bytes 552968 | tf_op jit(solution)/shard_map/ppermute | solution.py:397
  91.6 12.9 %collective-permute-start.25 = (bf16[32,2880]{1,0:T(8,128)(2,1)S(1)}, bf16[32,2880]{1,0:T(8,128)(2,1)S(1)}, u32[]{:S(2)}, u32[]{:S(2)}) collective-permute-start(bf16[32,2880]{1,0:T(8,128)(2,1)S(1)} %get-tuple-element.59), channel_id=1, source_target_pairs={{0,16},{16,0},{1,17},{17,1},{2,18},{18,2},{3,19},{19,3},{4,20},{20... | collective-permute-start | bytes 552968 | tf_op jit(solution)/shard_map/ppermute | solution.py:397
  93.4 14.0 %collective-permute-start.17 = (bf16[256,2944]{1,0:T(8,128)(2,1)}, bf16[256,2944]{1,0:T(8,128)(2,1)S(1)}, u32[]{:S(2)}, u32[]{:S(2)}) collective-permute-start(bf16[256,2944]{1,0:T(8,128)(2,1)} %collective-permute-done.16.refs_2_), channel_id=1, source_target_pairs={{0,4},{4,0},{1,5},{5,1},{2,6},{6,2},{3,7},{7,3},{8,12},{12,8},{9,1... | collective-permute-start | bytes 4521992 | tf_op jit(solution)/shard_map/ppermute | solution.py:397
  97.2 16.1 %collective-permute-start.22 = (bf16[32,2880]{1,0:T(8,128)(2,1)S(1)}, bf16[32,2880]{1,0:T(8,128)(2,1)S(1)}, u32[]{:S(2)}, u32[]{:S(2)}) collective-permute-start(bf16[32,2880]{1,0:T(8,128)(2,1)S(1)} %add_convert_fusion.2), channel_id=1, source_target_pairs={{0,3},{1,2},{2,1},{3,0},{4,7},{5,6},{6,5},{7,4},{8,11},{9,10},{10,... | collective-permute-start | bytes 552968 | tf_op jit(solution)/shard_map/ppermute | solution.py:397
  102.2 12.3 %collective-permute-start.24 = (bf16[32,2880]{1,0:T(8,128)(2,1)S(1)}, bf16[32,2880]{1,0:T(8,128)(2,1)S(1)}, u32[]{:S(2)}, u32[]{:S(2)}) collective-permute-start(bf16[32,2880]{1,0:T(8,128)(2,1)S(1)} %add_convert_fusion.1), channel_id=1, source_target_pairs={{0,2},{1,3},{2,0},{3,1},{4,6},{5,7},{6,4},{7,5},{8,10},{9,11},{10,... | collective-permute-start | bytes 552968 | tf_op jit(solution)/shard_map/ppermute | solution.py:397
  104.6 10.2 %collective-permute-start.26 = (bf16[32,2880]{1,0:T(8,128)(2,1)S(1)}, bf16[32,2880]{1,0:T(8,128)(2,1)S(1)}, u32[]{:S(2)}, u32[]{:S(2)}) collective-permute-start(bf16[32,2880]{1,0:T(8,128)(2,1)S(1)} %add_convert_fusion), channel_id=1, source_target_pairs={{0,1},{1,0},{2,3},{3,2},{4,5},{5,4},{6,7},{7,6},{8,9},{9,8},{10,11... | collective-permute-start | bytes 552968 | tf_op jit(solution)/shard_map/ppermute | solution.py:397
  106.9 7.9 %collective-permute-start.27 = (bf16[32,2880]{1,0:T(8,128)(2,1)S(1)}, bf16[32,2880]{1,0:T(8,128)(2,1)S(1)}, u32[]{:S(2)}, u32[]{:S(2)}) collective-permute-start(bf16[32,2880]{1,0:T(8,128)(2,1)S(1)} %get-tuple-element.63), channel_id=1, source_target_pairs={{0,16},{16,0},{1,17},{17,1},{2,18},{18,2},{3,19},{19,3},{4,20},{20... | collective-permute-start | bytes 552968 | tf_op jit(solution)/shard_map/ppermute | solution.py:397
  (8 other events, 49.9 us)

commit v5 on v4

--- a/solution.py
+++ b/solution.py
@@ -421,9 +421,10 @@
     own = after(hidden_in.T, pieces[0])
     x_side = flip(own, "x", 1)
     pieces += [flip(pieces[0], "z", 1), flip(pieces[0], "z", 2)]
-    pieces.append(flip(pieces[2], "z", 1))
-    across = [flip(piece, "hi", 1) for piece in pieces]
-    x_side = after(x_side, *pieces, *across[:2])
+    across = [flip(pieces[0], "hi", 1)]
+    pieces.append(flip(after(pieces[2], across[0]), "z", 1))
+    across += [flip(piece, "hi", 1) for piece in pieces[1:]]
+    x_side = after(x_side, *pieces, across[0], across[2])
     hidden = [own, flip(own, "c", 1), x_side, flip(x_side, "c", 1)]
     mine, *parts = project(place, pieces + across, hidden)
     chunks = 1

time: 116 us -> 116 us (level)
  no operation moved by 1% of the time
where the time goes in v5:
time: 116 us
  waiting for transfers between devices  49.7 us (43%)
  starting transfers between devices  35.6 us (31%)
  Pallas kernels  23.9 us (21%)
  local copies, waits for them, and re-layouts  4.33 us (4%)
  other arithmetic  1.3 us (1%)
    ppermute x20, waiting for transfers between devices, flip(): lax.ppermute(array, axis, [(i, i ^ by) for i in range(lax.axis_size(axis))])  27.1 us
    ppermute x20, starting transfers between devices, flip(): lax.ppermute(array, axis, [(i, i ^ by) for i in range(lax.axis_size(axis))])  25.1 us
    ppermute x2, waiting for transfers between devices, shifted(): return lax.ppermute(array, AXES, pairs)  15.1 us
    pallas_call x1, Pallas kernels, attention(): pl.pallas_call(functools.partial(attention_kernel, at), grid=(own.shape[0...  11.4 us
    ppermute x6, waiting for transfers between devices, flip_group(): lax.ppermute(array, ('x', 'c'), [(i, i ^ by) for i in range(QUARTERS)])  7.57 us
    ppermute x6, starting transfers between devices, flip_group(): lax.ppermute(array, ('x', 'c'), [(i, i ^ by) for i in range(QUARTERS)])  6.01 us
    pallas_call x1, Pallas kernels, input_grad(): pl.pallas_call(input_grad_kernel, grid=(-(-size // step),), in_specs=[SME...  5.91 us
    ppermute x2, starting transfers between devices, shifted(): return lax.ppermute(array, AXES, pairs)  4.45 us
  transfers between devices with their start and end apart: 28, of which 15 were waited for; matrix products, arithmetic and copies ran while one was open for 0% of the time, Pallas kernels for 16%

profile of v5, /device:TPU:0, one launch (start us, length us, event | category | flops | bytes accessed | tf_op | source)
XLA Modules:
  0.0 115.6 jit_solution(1355777601779871032)
XLA Ops:
  1.6 3.0 %collective-permute-start.8 = (bf16[2880,128]{1,0:T(8,128)(2,1)}, bf16[2880,128]{1,0:T(8,128)(2,1)S(1)}, u32[]{:S(2)}, u32[]{:S(2)}) collective-permute-start(bf16[2880,128]{1,0:T(8,128)(2,1)} %bitcast.12), channel_id=1, source_target_pairs={{0,8},{8,0},{1,9},{9,1},{2,10},{10,2},{3,11},{11,3},{4,12},{12,4},... | collective-permute-start | bytes 2211848 | tf_op jit(solution)/shard_map/ppermute | solution.py:397
  4.6 2.6 %collective-permute-start.1 = (bf16[32,2880]{1,0:T(8,128)(2,1)S(1)}, bf16[32,2880]{1,0:T(8,128)(2,1)S(1)}, u32[]{:S(2)}, u32[]{:S(2)}) collective-permute-start(bf16[32,2880]{1,0:T(8,128)(2,1)S(1)} %pad_maximum_fusion.refs_0_), channel_id=1, source_target_pairs={{0,2},{1,3},{2,0},{3,1},{4,6},{5,7},{6,4},{7,5},{8,10},{9,11},{10,... | collective-permute-start | bytes 552968 | tf_op jit(solution)/shard_map/ppermute | solution.py:397
  7.2 1.5 %collective-permute-start.2 = (bf16[32,2880]{1,0:T(8,128)(2,1)S(1)}, bf16[32,2880]{1,0:T(8,128)(2,1)S(1)}, u32[]{:S(2)}, u32[]{:S(2)}) collective-permute-start(bf16[32,2880]{1,0:T(8,128)(2,1)S(1)} %pad_maximum_fusion.refs_0_), channel_id=1, source_target_pairs={{0,16},{16,0},{1,17},{17,1},{2,18},{18,2},{3,19},{19,3},{4,20},{20... | collective-permute-start | bytes 552968 | tf_op jit(solution)/shard_map/ppermute | solution.py:397
  8.7 1.6 %collective-permute-start = (bf16[32,2880]{1,0:T(8,128)(2,1)S(1)}, bf16[32,2880]{1,0:T(8,128)(2,1)S(1)}, u32[]{:S(2)}, u32[]{:S(2)}) collective-permute-start(bf16[32,2880]{1,0:T(8,128)(2,1)S(1)} %pad_maximum_fusion.refs_0_), channel_id=1, source_target_pairs={{0,1},{1,0},{2,3},{3,2},{4,5},{5,4},{6,7},{7,6},{8,9},{9,8},{10,11... | collective-permute-start | bytes 552968 | tf_op jit(solution)/shard_map/ppermute | solution.py:397
  10.3 5.5 %collective-permute-done.1.refs_2_ = bf16[32,2880]{1,0:T(8,128)(2,1)S(1)} collective-permute-done((bf16[32,2880]{1,0:T(8,128)(2,1)S(1)}, bf16[32,2880]{1,0:T(8,128)(2,1)S(1)}, u32[]{:S(2)}, u32[]{:S(2)}) %collective-permute-start.1) | collective-permute-done | bytes 184352 | tf_op jit(solution)/shard_map/ppermute | solution.py:397
  17.9 3.5 %collective-permute-done.3.refs_3_ = bf16[32,2880]{1,0:T(8,128)(2,1)S(1)} collective-permute-done((bf16[32,2880]{1,0:T(8,128)(2,1)S(1)}, bf16[32,2880]{1,0:T(8,128)(2,1)S(1)}, u32[]{:S(2)}, u32[]{:S(2)}) %collective-permute-start.3) | collective-permute-done | bytes 184352 | tf_op jit(solution)/shard_map/ppermute | solution.py:397
  24.9 5.4 %collective-permute-done.4.refs_5_ = bf16[32,2880]{1,0:T(8,128)(2,1)S(1)} collective-permute-done((bf16[32,2880]{1,0:T(8,128)(2,1)S(1)}, bf16[32,2880]{1,0:T(8,128)(2,1)S(1)}, u32[]{:S(2)}, u32[]{:S(2)}) %collective-permute-start.4) | collective-permute-done | bytes 184352 | tf_op jit(solution)/shard_map/ppermute | solution.py:397
  30.3 3.8 %collective-permute-done.6.refs_7_ = bf16[32,2880]{1,0:T(8,128)(2,1)} collective-permute-done((bf16[32,2880]{1,0:T(8,128)(2,1)S(1)}, bf16[32,2880]{1,0:T(8,128)(2,1)}, u32[]{:S(2)}, u32[]{:S(2)}) %collective-permute-start.6) | collective-permute-done | bytes 184352 | tf_op jit(solution)/shard_map/ppermute | solution.py:397
  35.2 2.9 %project.1 = (bf16[256,2944]{1,0:T(8,128)(2,1)}, bf16[128,256]{1,0:T(8,128)(2,1)S(1)}, bf16[128,256]{1,0:T(8,128)(2,1)S(1)}, bf16[128,256]{1,0:T(8,128)(2,1)S(1)}, bf16[128,256]{1,0:T(8,128)(2,1)S(1)}) custom-call(s32[3]{0:T(128)S(1)} %pad_add_fusion.place_ref, bf16[32,2880]{1,0:T(8,128)(2,1)S(1)} %pad_maximum_fusion.refs_0_, ...), custom_call_target="tpu_custom_call" | custom-call | flops 754974720 | bytes 5963776 | tf_op jit(solution)/shard_map/project/pallas_call | solution.py:236
  40.0 3.0 %collective-permute-done.11.refs_2_ = bf16[128,256]{1,0:T(8,128)(2,1)S(1)} collective-permute-done((bf16[128,256]{1,0:T(8,128)(2,1)S(1)}, bf16[128,256]{1,0:T(8,128)(2,1)S(1)}, u32[]{:S(2)}, u32[]{:S(2)}) %collective-permute-start.11) | collective-permute-done | bytes 65568 | tf_op jit(solution)/shard_map/ppermute | solution.py:401
  45.1 3.2 %collective-permute-start.13 = (bf16[4,2,128,128]{3,2,1,0:T(8,128)(2,1)S(1)}, bf16[4,2,128,128]{3,2,1,0:T(8,128)(2,1)S(1)}, u32[]{:S(2)}, u32[]{:S(2)}) collective-permute-start(bf16[4,2,128,128]{3,2,1,0:T(8,128)(2,1)S(1)} %arrange.1.own_ref), channel_id=1, source_target_pairs={{0,1},{1,2},{2,3},{3,4},{4,5},{5,6},{6,7},{7,8},{8,9},{9,10},{10,1... | collective-permute-start | bytes 786440 | tf_op jit(solution)/shard_map/ppermute | solution.py:407
  48.3 5.7 %collective-permute-done.13.halo_ref = bf16[4,2,128,128]{3,2,1,0:T(8,128)(2,1)S(1)} collective-permute-done((bf16[4,2,128,128]{3,2,1,0:T(8,128)(2,1)S(1)}, bf16[4,2,128,128]{3,2,1,0:T(8,128)(2,1)S(1)}, u32[]{:S(2)}, u32[]{:S(2)}) %collective-permute-start.13) | collective-permute-done | bytes 262176 | tf_op jit(solution)/shard_map/ppermute | solution.py:407
  56.4 11.4 %attention.1 = (bf16[128,4096]{1,0:T(8,128)(2,1)}, f32[4,2,128,128]{3,2,1,0:T(8,128)S(1)}, bf16[4,2,128,128]{3,2,1,0:T(8,128)(2,1)S(1)}) custom-call(s32[1]{0:T(128)} %bitcast.first_ref, bf16[128,4096]{1,0:T(8,128)(2,1)S(1)} %copy-done.2, bf16[128,4096]{1,0:T(8,128)(2,1)S(1)} %copy-done.3, bf16[4,2,128,128]{3,2,1,0:T(8,128)(2,1)S(1)} %arrange.1.own_ref, ...), custom_call_target="tpu_custom_call" | custom-call | flops 1342177280 | bytes 2097152 | tf_op jit(solution)/shard_map/attention/pallas_call | solution.py:189
  69.1 9.4 %collective-permute-done.14.refs_1_ = bf16[4,2,128,128]{3,2,1,0:T(8,128)(2,1)S(1)} collective-permute-done((bf16[4,2,128,128]{3,2,1,0:T(8,128)(2,1)S(1)}, bf16[4,2,128,128]{3,2,1,0:T(8,128)(2,1)S(1)}, u32[]{:S(2)}, u32[]{:S(2)}) %collective-permute-start.14) | collective-permute-done | bytes 262176 | tf_op jit(solution)/shard_map/ppermute | solution.py:407
  81.2 2.6 %collective-permute-start.19 = (bf16[128,256]{1,0:T(8,128)(2,1)S(1)}, bf16[128,256]{1,0:T(8,128)(2,1)S(1)}, u32[]{:S(2)}, u32[]{:S(2)}) collective-permute-start(bf16[128,256]{1,0:T(8,128)(2,1)S(1)} %get-tuple-element.54), channel_id=1, source_target_pairs={{0,8},{4,12},{8,0},{12,4},{1,9},{5,13},{9,1},{13,5},{2,10},{6,14},... | collective-permute-start | bytes 196616 | tf_op jit(solution)/shard_map/ppermute | solution.py:401
  84.0 2.6 %collective-permute-done.19.refs_2_ = bf16[128,256]{1,0:T(8,128)(2,1)S(1)} collective-permute-done((bf16[128,256]{1,0:T(8,128)(2,1)S(1)}, bf16[128,256]{1,0:T(8,128)(2,1)S(1)}, u32[]{:S(2)}, u32[]{:S(2)}) %collective-permute-start.19) | collective-permute-done | bytes 65568 | tf_op jit(solution)/shard_map/ppermute | solution.py:401
  87.9 1.8 %weight_grad.1 = (bf16[32,2880]{1,0:T(8,128)(2,1)S(1)}, bf16[32,2880]{1,0:T(8,128)(2,1)S(1)}, bf16[32,2880]{1,0:T(8,128)(2,1)S(1)}, bf16[32,2880]{1,0:T(8,128)(2...) custom-call(s32[3]{0:T(128)S(1)} %pad_add_fusion.place_ref, ...), custom_call_target="tpu_custom_call" | custom-call | flops 754974720 | bytes 5898240 | tf_op jit(solution)/shard_map/weight_grad/pallas_call | solution.py:354
  89.7 1.6 %collective-permute-start.21 = (bf16[32,2880]{1,0:T(8,128)(2,1)S(1)}, bf16[32,2880]{1,0:T(8,128)(2,1)S(1)}, u32[]{:S(2)}, u32[]{:S(2)}) collective-permute-start(bf16[32,2880]{1,0:T(8,128)(2,1)S(1)} %get-tuple-element.57), channel_id=1, source_target_pairs={{0,16},{16,0},{1,17},{17,1},{2,18},{18,2},{3,19},{19,3},{4,20},{20... | collective-permute-start | bytes 552968 | tf_op jit(solution)/shard_map/ppermute | solution.py:397
  91.8 1.6 %collective-permute-start.25 = (bf16[32,2880]{1,0:T(8,128)(2,1)S(1)}, bf16[32,2880]{1,0:T(8,128)(2,1)S(1)}, u32[]{:S(2)}, u32[]{:S(2)}) collective-permute-start(bf16[32,2880]{1,0:T(8,128)(2,1)S(1)} %get-tuple-element.61), channel_id=1, source_target_pairs={{0,16},{16,0},{1,17},{17,1},{2,18},{18,2},{3,19},{19,3},{4,20},{20... | collective-permute-start | bytes 552968 | tf_op jit(solution)/shard_map/ppermute | solution.py:397
  93.3 4.0 %collective-permute-done.21 = bf16[32,2880]{1,0:T(8,128)(2,1)S(1)} collective-permute-done((bf16[32,2880]{1,0:T(8,128)(2,1)S(1)}, bf16[32,2880]{1,0:T(8,128)(2,1)S(1)}, u32[]{:S(2)}, u32[]{:S(2)}) %collective-permute-start.21) | collective-permute-done | bytes 184352 | tf_op jit(solution)/shard_map/ppermute | solution.py:397
  97.4 4.8 %collective-permute-start.22 = (bf16[32,2880]{1,0:T(8,128)(2,1)S(1)}, bf16[32,2880]{1,0:T(8,128)(2,1)S(1)}, u32[]{:S(2)}, u32[]{:S(2)}) collective-permute-start(bf16[32,2880]{1,0:T(8,128)(2,1)S(1)} %add_convert_fusion.2), channel_id=1, source_target_pairs={{0,3},{1,2},{2,1},{3,0},{4,7},{5,6},{6,5},{7,4},{8,11},{9,10},{10,... | collective-permute-start | bytes 552968 | tf_op jit(solution)/shard_map/ppermute | solution.py:397
  102.6 2.0 %collective-permute-done.25 = bf16[32,2880]{1,0:T(8,128)(2,1)S(1)} collective-permute-done((bf16[32,2880]{1,0:T(8,128)(2,1)S(1)}, bf16[32,2880]{1,0:T(8,128)(2,1)S(1)}, u32[]{:S(2)}, u32[]{:S(2)}) %collective-permute-start.25) | collective-permute-done | bytes 184352 | tf_op jit(solution)/shard_map/ppermute | solution.py:397
  104.7 2.3 %collective-permute-start.26 = (bf16[32,2880]{1,0:T(8,128)(2,1)S(1)}, bf16[32,2880]{1,0:T(8,128)(2,1)S(1)}, u32[]{:S(2)}, u32[]{:S(2)}) collective-permute-start(bf16[32,2880]{1,0:T(8,128)(2,1)S(1)} %add_convert_fusion), channel_id=1, source_target_pairs={{0,1},{1,0},{2,3},{3,2},{4,5},{5,4},{6,7},{7,6},{8,9},{9,8},{10,11... | collective-permute-start | bytes 552968 | tf_op jit(solution)/shard_map/ppermute | solution.py:397
  107.4 5.9 %input_grad.1 = bf16[2880,128]{1,0:T(8,128)(2,1)} custom-call(s32[3]{0:T(128)S(1)} %pad_add_fusion.place_ref, bf16[4,128,256]{2,1,0:T(8,128)(2,1)S(1)} %get-tuple-element.48.all_ref, bf16[256,2944]{1,0:T(8,128)(2,1)} %get-tuple-element.50.refs_0_, bf16[256,2944]{1,0:T(8,128)(2,1)} %collective-permute-done.15.refs_1_, ...), custom_call_target="tpu_custom_call" | custom-call | flops 754974720 | bytes 6766592 | tf_op jit(solution)/shard_map/input_grad/pallas_call | solution.py:379
  (53 shorter events, 23.2 us)
Async XLA Ops:
  1.6 21.2 %collective-permute-start.8 = (bf16[2880,128]{1,0:T(8,128)(2,1)}, bf16[2880,128]{1,0:T(8,128)(2,1)S(1)}, u32[]{:S(2)}, u32[]{:S(2)}) collective-permute-start(bf16[2880,128]{1,0:T(8,128)(2,1)} %bitcast.12), channel_id=1, source_target_pairs={{0,8},{8,0},{1,9},{9,1},{2,10},{10,2},{3,11},{11,3},{4,12},{12,4},... | collective-permute-start | bytes 2211848 | tf_op jit(solution)/shard_map/ppermute | solution.py:397
  4.6 11.2 %collective-permute-start.1 = (bf16[32,2880]{1,0:T(8,128)(2,1)S(1)}, bf16[32,2880]{1,0:T(8,128)(2,1)S(1)}, u32[]{:S(2)}, u32[]{:S(2)}) collective-permute-start(bf16[32,2880]{1,0:T(8,128)(2,1)S(1)} %pad_maximum_fusion.refs_0_), channel_id=1, source_target_pairs={{0,2},{1,3},{2,0},{3,1},{4,6},{5,7},{6,4},{7,5},{8,10},{9,11},{10,... | collective-permute-start | bytes 552968 | tf_op jit(solution)/shard_map/ppermute | solution.py:397
  7.2 8.6 %collective-permute-start.2 = (bf16[32,2880]{1,0:T(8,128)(2,1)S(1)}, bf16[32,2880]{1,0:T(8,128)(2,1)S(1)}, u32[]{:S(2)}, u32[]{:S(2)}) collective-permute-start(bf16[32,2880]{1,0:T(8,128)(2,1)S(1)} %pad_maximum_fusion.refs_0_), channel_id=1, source_target_pairs={{0,16},{16,0},{1,17},{17,1},{2,18},{18,2},{3,19},{19,3},{4,20},{20... | collective-permute-start | bytes 552968 | tf_op jit(solution)/shard_map/ppermute | solution.py:397
  8.7 9.2 %collective-permute-start = (bf16[32,2880]{1,0:T(8,128)(2,1)S(1)}, bf16[32,2880]{1,0:T(8,128)(2,1)S(1)}, u32[]{:S(2)}, u32[]{:S(2)}) collective-permute-start(bf16[32,2880]{1,0:T(8,128)(2,1)S(1)} %pad_maximum_fusion.refs_0_), channel_id=1, source_target_pairs={{0,1},{1,0},{2,3},{3,2},{4,5},{5,4},{6,7},{7,6},{8,9},{9,8},{10,11... | collective-permute-start | bytes 552968 | tf_op jit(solution)/shard_map/ppermute | solution.py:397
  15.8 5.6 %collective-permute-start.3 = (bf16[32,2880]{1,0:T(8,128)(2,1)S(1)}, bf16[32,2880]{1,0:T(8,128)(2,1)S(1)}, u32[]{:S(2)}, u32[]{:S(2)}) collective-permute-start(bf16[32,2880]{1,0:T(8,128)(2,1)S(1)} %collective-permute-done.1.refs_2_), channel_id=1, source_target_pairs={{0,1},{1,0},{2,3},{3,2},{4,5},{5,4},{6,7},{7,6},{8,9},{9,8},{10,11... | collective-permute-start | bytes 552968 | tf_op jit(solution)/shard_map/ppermute | solution.py:397
  16.4 6.4 %collective-permute-start.5 = (bf16[32,2880]{1,0:T(8,128)(2,1)S(1)}, bf16[32,2880]{1,0:T(8,128)(2,1)S(1)}, u32[]{:S(2)}, u32[]{:S(2)}) collective-permute-start(bf16[32,2880]{1,0:T(8,128)(2,1)S(1)} %collective-permute-done.1.refs_2_), channel_id=1, source_target_pairs={{0,16},{16,0},{1,17},{17,1},{2,18},{18,2},{3,19},{19,3},{4,20},{20... | collective-permute-start | bytes 552968 | tf_op jit(solution)/shard_map/ppermute | solution.py:397
  17.9 16.2 %collective-permute-start.7 = (bf16[2880,128]{1,0:T(8,128)(2,1)}, bf16[2880,128]{1,0:T(8,128)(2,1)S(1)}, u32[]{:S(2)}, u32[]{:S(2)}) collective-permute-start(bf16[2880,128]{1,0:T(8,128)(2,1)} %bitcast.13), channel_id=1, source_target_pairs={{0,4},{4,0},{1,5},{5,1},{2,6},{6,2},{3,7},{7,3},{8,12},{12,8},{9,1... | collective-permute-start | bytes 2211848 | tf_op jit(solution)/shard_map/ppermute | solution.py:397
  22.8 11.3 %collective-permute-start.9 = (bf16[2880,128]{1,0:T(8,128)(2,1)S(1)}, bf16[2880,128]{1,0:T(8,128)(2,1)S(1)}, u32[]{:S(2)}, u32[]{:S(2)}) collective-permute-start(bf16[2880,128]{1,0:T(8,128)(2,1)S(1)} %collective-permute-done.8.refs_10_.refs_6_), channel_id=1, source_target_pairs={{0,4},{4,0},{1,5},{5,1},{2,6},{6,2},{3,7},{7,3},{8,12},{12,8},{9,1... | collective-permute-start | bytes 2211848 | tf_op jit(solution)/shard_map/ppermute | solution.py:397
  22.8 7.5 %collective-permute-start.4 = (bf16[32,2880]{1,0:T(8,128)(2,1)S(1)}, bf16[32,2880]{1,0:T(8,128)(2,1)S(1)}, u32[]{:S(2)}, u32[]{:S(2)}) collective-permute-start(bf16[32,2880]{1,0:T(8,128)(2,1)S(1)} %collective-permute-done.refs_1_), channel_id=1, source_target_pairs={{0,16},{16,0},{1,17},{17,1},{2,18},{18,2},{3,19},{19,3},{4,20},{20... | collective-permute-start | bytes 552968 | tf_op jit(solution)/shard_map/ppermute | solution.py:397
  24.3 9.8 %collective-permute-start.6 = (bf16[32,2880]{1,0:T(8,128)(2,1)S(1)}, bf16[32,2880]{1,0:T(8,128)(2,1)}, u32[]{:S(2)}, u32[]{:S(2)}) collective-permute-start(bf16[32,2880]{1,0:T(8,128)(2,1)S(1)} %collective-permute-done.3.refs_3_), channel_id=1, source_target_pairs={{0,16},{16,0},{1,17},{17,1},{2,18},{18,2},{3,19},{19,3},{4,20},{20... | collective-permute-start | bytes 552968 | tf_op jit(solution)/shard_map/ppermute | solution.py:397
  38.7 5.0 %collective-permute-start.12 = (bf16[128,256]{1,0:T(8,128)(2,1)S(1)}, bf16[128,256]{1,0:T(8,128)(2,1)S(1)}, u32[]{:S(2)}, u32[]{:S(2)}) collective-permute-start(bf16[128,256]{1,0:T(8,128)(2,1)S(1)} %get-tuple-element.42), channel_id=1, source_target_pairs={{0,12},{4,8},{8,4},{12,0},{1,13},{5,9},{9,5},{13,1},{2,14},{6,10},... | collective-permute-start | bytes 196616 | tf_op jit(solution)/shard_map/ppermute | solution.py:401
  44.3 39.7 %collective-permute-start.15 = (bf16[256,2944]{1,0:T(8,128)(2,1)}, bf16[256,2944]{1,0:T(8,128)(2,1)}, u32[]{:S(2)}, u32[]{:S(2)}) collective-permute-start(bf16[256,2944]{1,0:T(8,128)(2,1)} %get-tuple-element.50.refs_0_), channel_id=1, source_target_pairs={{0,4},{4,0},{1,5},{5,1},{2,6},{6,2},{3,7},{7,3},{8,12},{12,8},{9,1... | collective-permute-start | bytes 4521992 | tf_op jit(solution)/shard_map/ppermute | solution.py:397
  44.5 39.4 %collective-permute-start.16 = (bf16[256,2944]{1,0:T(8,128)(2,1)}, bf16[256,2944]{1,0:T(8,128)(2,1)}, u32[]{:S(2)}, u32[]{:S(2)}) collective-permute-start(bf16[256,2944]{1,0:T(8,128)(2,1)} %get-tuple-element.50.refs_0_), channel_id=1, source_target_pairs={{0,8},{8,0},{1,9},{9,1},{2,10},{10,2},{3,11},{11,3},{4,12},{12,4},... | collective-permute-start | bytes 4521992 | tf_op jit(solution)/shard_map/ppermute | solution.py:397
  45.1 8.9 %collective-permute-start.13 = (bf16[4,2,128,128]{3,2,1,0:T(8,128)(2,1)S(1)}, bf16[4,2,128,128]{3,2,1,0:T(8,128)(2,1)S(1)}, u32[]{:S(2)}, u32[]{:S(2)}) collective-permute-start(bf16[4,2,128,128]{3,2,1,0:T(8,128)(2,1)S(1)} %arrange.1.own_ref), channel_id=1, source_target_pairs={{0,1},{1,2},{2,3},{3,4},{4,5},{5,6},{6,7},{7,8},{8,9},{9,10},{10,1... | collective-permute-start | bytes 786440 | tf_op jit(solution)/shard_map/ppermute | solution.py:407
  67.8 10.7 %collective-permute-start.14 = (bf16[4,2,128,128]{3,2,1,0:T(8,128)(2,1)S(1)}, bf16[4,2,128,128]{3,2,1,0:T(8,128)(2,1)S(1)}, u32[]{:S(2)}, u32[]{:S(2)}) collective-permute-start(bf16[4,2,128,128]{3,2,1,0:T(8,128)(2,1)S(1)} %get-tuple-element.45), channel_id=1, source_target_pairs={{1,0},{2,1},{3,2},{4,3},{5,4},{6,5},{7,6},{8,7},{9,8},{10,9},{11,1... | collective-permute-start | bytes 786440 | tf_op jit(solution)/shard_map/ppermute | solution.py:407
  81.2 5.4 %collective-permute-start.19 = (bf16[128,256]{1,0:T(8,128)(2,1)S(1)}, bf16[128,256]{1,0:T(8,128)(2,1)S(1)}, u32[]{:S(2)}, u32[]{:S(2)}) collective-permute-start(bf16[128,256]{1,0:T(8,128)(2,1)S(1)} %get-tuple-element.54), channel_id=1, source_target_pairs={{0,8},{4,12},{8,0},{12,4},{1,9},{5,13},{9,1},{13,5},{2,10},{6,14},... | collective-permute-start | bytes 196616 | tf_op jit(solution)/shard_map/ppermute | solution.py:401
  89.7 7.6 %collective-permute-start.21 = (bf16[32,2880]{1,0:T(8,128)(2,1)S(1)}, bf16[32,2880]{1,0:T(8,128)(2,1)S(1)}, u32[]{:S(2)}, u32[]{:S(2)}) collective-permute-start(bf16[32,2880]{1,0:T(8,128)(2,1)S(1)} %get-tuple-element.57), channel_id=1, source_target_pairs={{0,16},{16,0},{1,17},{17,1},{2,18},{18,2},{3,19},{19,3},{4,20},{20... | collective-permute-start | bytes 552968 | tf_op jit(solution)/shard_map/ppermute | solution.py:397
  91.3 10.9 %collective-permute-start.23 = (bf16[32,2880]{1,0:T(8,128)(2,1)S(1)}, bf16[32,2880]{1,0:T(8,128)(2,1)S(1)}, u32[]{:S(2)}, u32[]{:S(2)}) collective-permute-start(bf16[32,2880]{1,0:T(8,128)(2,1)S(1)} %get-tuple-element.59), channel_id=1, source_target_pairs={{0,16},{16,0},{1,17},{17,1},{2,18},{18,2},{3,19},{19,3},{4,20},{20... | collective-permute-start | bytes 552968 | tf_op jit(solution)/shard_map/ppermute | solution.py:397
  91.8 12.8 %collective-permute-start.25 = (bf16[32,2880]{1,0:T(8,128)(2,1)S(1)}, bf16[32,2880]{1,0:T(8,128)(2,1)S(1)}, u32[]{:S(2)}, u32[]{:S(2)}) collective-permute-start(bf16[32,2880]{1,0:T(8,128)(2,1)S(1)} %get-tuple-element.61), channel_id=1, source_target_pairs={{0,16},{16,0},{1,17},{17,1},{2,18},{18,2},{3,19},{19,3},{4,20},{20... | collective-permute-start | bytes 552968 | tf_op jit(solution)/shard_map/ppermute | solution.py:397
  93.3 14.0 %collective-permute-start.17 = (bf16[256,2944]{1,0:T(8,128)(2,1)}, bf16[256,2944]{1,0:T(8,128)(2,1)S(1)}, u32[]{:S(2)}, u32[]{:S(2)}) collective-permute-start(bf16[256,2944]{1,0:T(8,128)(2,1)} %collective-permute-done.16.refs_2_), channel_id=1, source_target_pairs={{0,4},{4,0},{1,5},{5,1},{2,6},{6,2},{3,7},{7,3},{8,12},{12,8},{9,1... | collective-permute-start | bytes 4521992 | tf_op jit(solution)/shard_map/ppermute | solution.py:397
  97.4 15.9 %collective-permute-start.22 = (bf16[32,2880]{1,0:T(8,128)(2,1)S(1)}, bf16[32,2880]{1,0:T(8,128)(2,1)S(1)}, u32[]{:S(2)}, u32[]{:S(2)}) collective-permute-start(bf16[32,2880]{1,0:T(8,128)(2,1)S(1)} %add_convert_fusion.2), channel_id=1, source_target_pairs={{0,3},{1,2},{2,1},{3,0},{4,7},{5,6},{6,5},{7,4},{8,11},{9,10},{10,... | collective-permute-start | bytes 552968 | tf_op jit(solution)/shard_map/ppermute | solution.py:397
  102.3 12.4 %collective-permute-start.24 = (bf16[32,2880]{1,0:T(8,128)(2,1)S(1)}, bf16[32,2880]{1,0:T(8,128)(2,1)S(1)}, u32[]{:S(2)}, u32[]{:S(2)}) collective-permute-start(bf16[32,2880]{1,0:T(8,128)(2,1)S(1)} %add_convert_fusion.1), channel_id=1, source_target_pairs={{0,2},{1,3},{2,0},{3,1},{4,6},{5,7},{6,4},{7,5},{8,10},{9,11},{10,... | collective-permute-start | bytes 552968 | tf_op jit(solution)/shard_map/ppermute | solution.py:397
  104.7 10.0 %collective-permute-start.26 = (bf16[32,2880]{1,0:T(8,128)(2,1)S(1)}, bf16[32,2880]{1,0:T(8,128)(2,1)S(1)}, u32[]{:S(2)}, u32[]{:S(2)}) collective-permute-start(bf16[32,2880]{1,0:T(8,128)(2,1)S(1)} %add_convert_fusion), channel_id=1, source_target_pairs={{0,1},{1,0},{2,3},{3,2},{4,5},{5,4},{6,7},{7,6},{8,9},{9,8},{10,11... | collective-permute-start | bytes 552968 | tf_op jit(solution)/shard_map/ppermute | solution.py:397
  106.9 7.8 %collective-permute-start.27 = (bf16[32,2880]{1,0:T(8,128)(2,1)S(1)}, bf16[32,2880]{1,0:T(8,128)(2,1)S(1)}, u32[]{:S(2)}, u32[]{:S(2)}) collective-permute-start(bf16[32,2880]{1,0:T(8,128)(2,1)S(1)} %get-tuple-element.65), channel_id=1, source_target_pairs={{0,16},{16,0},{1,17},{17,1},{2,18},{18,2},{3,19},{19,3},{4,20},{20... | collective-permute-start | bytes 552968 | tf_op jit(solution)/shard_map/ppermute | solution.py:397
  (8 other events, 50.0 us)
